TPU v7x, 32 devices: a whole 2x2x4 slice. The times are simulated.
32 devices in a mesh: dp: 16 (over z, y, core), tensor: 2 (over x).
Axes of the slice: x: 2, y: 2, z: 4, core: 2. Of those that a mesh axis runs over, the one named last changes fastest.
Arguments:
- tokens: bfloat16 [3, 2048, 2048], P(None, 'dp'), may hold values from -6 to 6
- doc_position: int32 [3, 2048], P(None, 'dp'), may hold values from 0 to 1023, as said below
- attn_gain: bfloat16 [2048], P('dp'), may hold values from 0.25 to 1.75
- w_query: bfloat16 [2048, 2048], P('dp', 'tensor'), may hold values from -0.125 to 0.125
- w_key: bfloat16 [2048, 256], P('dp', 'tensor'), may hold values from -0.125 to 0.125
- w_value: bfloat16 [2048, 256], P('dp', 'tensor'), may hold values from -0.125 to 0.125
- w_out: bfloat16 [2048, 2048], P('tensor', 'dp'), may hold values from -0.75 to 0.75
- ffn_gain: bfloat16 [2048], P('dp'), may hold values from 0.25 to 1.75
- w_gate: bfloat16 [2048, 5632], P('dp', 'tensor'), may hold values from -0.125 to 0.125
- w_up: bfloat16 [2048, 5632], P('dp', 'tensor'), may hold values from -0.125 to 0.125
- w_down: bfloat16 [5632, 2048], P('tensor', 'dp'), may hold values from -0.078125 to 0.078125
- cotangent: bfloat16 [3, 2048, 2048], P(None, 'dp'), may hold values from -6 to 6
Outputs:
- output: bfloat16 [3, 2048, 2048], P(None, 'dp')
- grad_tokens: float32 [3, 2048, 2048], P(None, 'dp')
- grad_attn_gain: float32 [2048], P('dp')
- grad_w_query: float32 [2048, 2048], P('dp', 'tensor')
- grad_w_key: float32 [2048, 256], P('dp', 'tensor')
- grad_w_value: float32 [2048, 256], P('dp', 'tensor')
- grad_w_out: float32 [2048, 2048], P('tensor', 'dp')
- grad_ffn_gain: float32 [2048], P('dp')
- grad_w_gate: float32 [2048, 5632], P('dp', 'tensor')
- grad_w_up: float32 [2048, 5632], P('dp', 'tensor')
- grad_w_down: float32 [5632, 2048], P('tensor', 'dp')
Inputs may be any that keep to these rules, and one draw needn't show every extreme that they name: `doc_position`: each micro-batch is one packed sequence of documents. Documents start at every multiple of 1024 tokens and never cross one; positions count up by one within a document and restart at 0 where a new one begins; in each micro-batch one aligned span of 1024 tokens is a single document.
All inputs are finite; a program needn't handle non-finite values.
Results may differ from a plain program's by a relative error of at most 0.015.
Values may be sent and summed in bfloat16 or wider, within the bound.
A program may use at most 256 MiB of HBM per device.

v0:
```python
import jax
import jax.numpy as jnp
from jax import lax
from jax.sharding import PartitionSpec as P

HEAD_DIM = 64
SEQ_LEN = 1024


epsilon = 1e-05


def passed_along(block, axis, distance):
    devices = range(lax.axis_size(axis))
    route = [(i - distance, i) for i in devices if i - distance in devices]
    return lax.ppermute(block, axis, route)


def dot_first(left, right):
    return lax.dot_general(
        left, right, (((0,), (0,)), ((), ())), preferred_element_type=jnp.float32
    )


def dot_last(left, right):
    return lax.dot_general(
        left, right, (((1,), (1,)), ((), ())), preferred_element_type=jnp.float32
    )


def normalize(value, gain):
    ratio = lax.rsqrt(jnp.mean(value * value, axis=-1, keepdims=True) + epsilon)
    return (value * ratio * gain, ratio)


def norm_back(grad, value, ratio, gain):
    scaled = grad * gain
    inner = jnp.mean(scaled * value, axis=-1, keepdims=True)
    return (ratio * scaled - value * ratio**3 * inner, jnp.sum(grad * value * ratio, axis=0))


def angles(position):
    power = jnp.arange(HEAD_DIM // 2, dtype=jnp.float32) * (2.0 / HEAD_DIM)
    inverse = 10000.0 ** (-power)
    turned = position.astype(jnp.float32)[:, None] * inverse[None, :]
    return (jnp.cos(turned)[:, None, :], jnp.sin(turned)[:, None, :])


def rotate(value, cosine, sine):
    half_dim = value.shape[-1] // 2
    first_half = value[..., :half_dim]
    second_half = value[..., half_dim:]
    return jnp.concatenate(
        [first_half * cosine - second_half * sine, second_half * cosine + first_half * sine],
        axis=-1,
    )


def unrotate(grad, cosine, sine):
    half_dim = grad.shape[-1] // 2
    first_half = grad[..., :half_dim]
    second_half = grad[..., half_dim:]
    return jnp.concatenate(
        [first_half * cosine + second_half * sine, second_half * cosine - first_half * sine],
        axis=-1,
    )


def masked_scores(grouped, window_keys, position, span_blocks):
    rows = grouped.shape[0]
    scores = jnp.einsum(
        "tkgd,jkd->kgtj", grouped, window_keys, preferred_element_type=jnp.float32
    ) * HEAD_DIM ** (-0.5)
    places = jnp.arange(rows)
    key_places = jnp.arange(span_blocks * rows) - (span_blocks - 1) * rows
    distance = places[:, None] - key_places[None, :]
    allowed = (distance >= 0) & (distance <= position[:, None])
    return jnp.where(allowed, scores, -1e30)


def forward_block(hidden_in, position, weights, span_blocks):
    gain_one, query_w, key_w, value_w, out_w, gain_two, gate_w, up_w, down_w = weights
    rows = hidden_in.shape[0]
    local_heads = query_w.shape[1] // HEAD_DIM
    local_groups = key_w.shape[1] // HEAD_DIM
    hidden_f = hidden_in.astype(jnp.float32)
    normed, ratio_one = normalize(hidden_f, gain_one.astype(jnp.float32))
    normed_low = normed.astype(jnp.bfloat16)
    cosine, sine = angles(position)
    query_raw = jnp.dot(normed_low, query_w, preferred_element_type=jnp.float32).reshape(
        rows, local_heads, HEAD_DIM
    )
    queries = rotate(query_raw, cosine, sine).astype(jnp.bfloat16)
    key_raw = jnp.dot(normed_low, key_w, preferred_element_type=jnp.float32).reshape(
        rows, local_groups, HEAD_DIM
    )
    keys = rotate(key_raw, cosine, sine).astype(jnp.bfloat16).reshape(rows, local_groups * HEAD_DIM)
    values = jnp.dot(normed_low, value_w, preferred_element_type=jnp.float32).astype(jnp.bfloat16)
    key_blocks = [keys]
    value_blocks = [values]
    for back_step in range(1, span_blocks):
        earlier_key, earlier_value = passed_along((keys, values), "dp", back_step)
        key_blocks.insert(0, earlier_key)
        value_blocks.insert(0, earlier_value)
    window_keys = jnp.concatenate(key_blocks, axis=0).reshape(
        span_blocks * rows, local_groups, HEAD_DIM
    )
    window_values = jnp.concatenate(value_blocks, axis=0).reshape(
        span_blocks * rows, local_groups, HEAD_DIM
    )
    grouped = queries.reshape(rows, local_groups, local_heads // local_groups, HEAD_DIM)
    scores = masked_scores(grouped, window_keys, position, span_blocks)
    peak = jnp.max(scores, axis=-1, keepdims=True)
    expon = jnp.exp(scores - peak)
    total = jnp.sum(expon, axis=-1, keepdims=True)
    logsum = peak + jnp.log(total)
    probs_low = (expon / total).astype(jnp.bfloat16)
    mixed = jnp.einsum(
        "kgtj,jkd->tkgd", probs_low, window_values, preferred_element_type=jnp.float32
    )
    mixed = mixed.reshape(rows, local_heads * HEAD_DIM).astype(jnp.bfloat16)
    attended = lax.psum(jnp.dot(mixed, out_w, preferred_element_type=jnp.float32), "tensor")
    middle = hidden_f + attended
    normed_two, ratio_two = normalize(middle, gain_two.astype(jnp.float32))
    normed_two_low = normed_two.astype(jnp.bfloat16)
    gate = jnp.dot(normed_two_low, gate_w, preferred_element_type=jnp.float32)
    upward = jnp.dot(normed_two_low, up_w, preferred_element_type=jnp.float32)
    activated = (jax.nn.silu(gate) * upward).astype(jnp.bfloat16)
    feed = lax.psum(
        jnp.dot(activated, down_w, preferred_element_type=jnp.float32).astype(jnp.bfloat16),
        "tensor",
    ).astype(jnp.float32)
    final = middle + feed
    kept = (
        hidden_f,
        ratio_one,
        normed_low,
        cosine,
        sine,
        grouped,
        window_keys,
        window_values,
        position,
        logsum,
        mixed,
        middle,
        ratio_two,
        normed_two_low,
        gate,
        upward,
        activated,
    )
    return (final.astype(jnp.bfloat16), kept)


def backward_block(grad_final, kept, weights, span_blocks):
    gain_one, query_w, key_w, value_w, out_w, gain_two, gate_w, up_w, down_w = weights
    (
        hidden_f,
        ratio_one,
        normed_low,
        cosine,
        sine,
        grouped,
        window_keys,
        window_values,
        position,
        logsum,
        mixed,
        middle,
        ratio_two,
        normed_two_low,
        gate,
        upward,
        activated,
    ) = kept
    rows = hidden_f.shape[0]
    local_groups = window_keys.shape[1]
    local_heads = grouped.shape[1] * grouped.shape[2]
    grad_down_w = dot_first(activated, grad_final)
    grad_act = jnp.dot(grad_final, down_w.T, preferred_element_type=jnp.float32)
    sigmoid = jax.nn.sigmoid(gate)
    grad_gate_low = (grad_act * upward * sigmoid * (1.0 + gate * (1.0 - sigmoid))).astype(
        jnp.bfloat16
    )
    grad_up_low = (grad_act * (gate * sigmoid)).astype(jnp.bfloat16)
    grad_gate_w = dot_first(normed_two_low, grad_gate_low)
    grad_up_w = dot_first(normed_two_low, grad_up_low)
    grad_normed_two = lax.psum(
        dot_last(grad_gate_low, gate_w) + dot_last(grad_up_low, up_w), "tensor"
    )
    grad_mid_norm, grad_gain_two = norm_back(
        grad_normed_two, middle, ratio_two, gain_two.astype(jnp.float32)
    )
    grad_middle = grad_final.astype(jnp.float32) + grad_mid_norm
    grad_middle_low = grad_middle.astype(jnp.bfloat16)
    grad_out_w = dot_first(mixed, grad_middle_low)
    grad_mixed = dot_last(grad_middle_low, out_w).astype(jnp.bfloat16)
    grad_grouped = grad_mixed.reshape(grouped.shape)
    scores = masked_scores(grouped, window_keys, position, span_blocks)
    probs = jnp.exp(scores - logsum)
    grad_window_values = jnp.einsum(
        "kgtj,tkgd->jkd",
        probs.astype(jnp.bfloat16),
        grad_grouped,
        preferred_element_type=jnp.float32,
    )
    grad_probs = jnp.einsum(
        "tkgd,jkd->kgtj", grad_grouped, window_values, preferred_element_type=jnp.float32
    )
    inner = jnp.sum(probs * grad_probs, axis=-1, keepdims=True)
    grad_scores = (probs * (grad_probs - inner)).astype(jnp.bfloat16)
    grad_queries = jnp.einsum(
        "kgtj,jkd->tkgd", grad_scores, window_keys, preferred_element_type=jnp.float32
    ) * HEAD_DIM ** (-0.5)
    grad_window_keys = jnp.einsum(
        "kgtj,tkgd->jkd", grad_scores, grouped, preferred_element_type=jnp.float32
    ) * HEAD_DIM ** (-0.5)
    last_start = (span_blocks - 1) * rows
    key_total = grad_window_keys[last_start:]
    value_total = grad_window_values[last_start:]
    for back_step in range(1, span_blocks):
        block_start = (span_blocks - 1 - back_step) * rows
        sent_keys = grad_window_keys[block_start : block_start + rows]
        sent_values = grad_window_values[block_start : block_start + rows]
        came_keys, came_values = (
            passed_along(sent_keys.astype(jnp.bfloat16), "dp", -back_step).astype(sent_keys.dtype),
            passed_along(sent_values.astype(jnp.bfloat16), "dp", -back_step).astype(
                sent_values.dtype
            ),
        )
        key_total = key_total + came_keys
        value_total = value_total + came_values
    grad_key_raw = (
        unrotate(key_total, cosine, sine)
        .astype(jnp.bfloat16)
        .reshape(rows, local_groups * HEAD_DIM)
    )
    grad_values_low = value_total.astype(jnp.bfloat16).reshape(rows, local_groups * HEAD_DIM)
    grad_query_raw = (
        unrotate(grad_queries.reshape(rows, local_heads, HEAD_DIM), cosine, sine)
        .astype(jnp.bfloat16)
        .reshape(rows, local_heads * HEAD_DIM)
    )
    grad_query_w = dot_first(normed_low, grad_query_raw)
    grad_key_w = dot_first(normed_low, grad_key_raw)
    grad_value_w = dot_first(normed_low, grad_values_low)
    partial_normed = (
        dot_last(grad_query_raw, query_w)
        + dot_last(grad_key_raw, key_w)
        + dot_last(grad_values_low, value_w)
    )
    grad_normed = lax.psum(partial_normed.astype(jnp.bfloat16), "tensor").astype(jnp.float32)
    grad_in_norm, grad_gain_one = norm_back(
        grad_normed, hidden_f, ratio_one, gain_one.astype(jnp.float32)
    )
    grad_input = grad_middle + grad_in_norm
    return (
        grad_input,
        (
            grad_gain_one,
            grad_query_w,
            grad_key_w,
            grad_value_w,
            grad_out_w,
            grad_gain_two,
            grad_gate_w,
            grad_up_w,
            grad_down_w,
        ),
    )


def body(
    tokens,
    doc_position,
    attn_gain,
    w_query,
    w_key,
    w_value,
    w_out,
    ffn_gain,
    w_gate,
    w_up,
    w_down,
    cotangent,
):
    weights = (
        lax.all_gather(attn_gain, "dp", axis=0, tiled=True),
        lax.all_gather(w_query, "dp", axis=0, tiled=True),
        lax.all_gather(w_key, "dp", axis=0, tiled=True),
        lax.all_gather(w_value, "dp", axis=0, tiled=True),
        lax.all_gather(w_out, "dp", axis=1, tiled=True),
        lax.all_gather(ffn_gain, "dp", axis=0, tiled=True),
        lax.all_gather(w_gate, "dp", axis=0, tiled=True),
        lax.all_gather(w_up, "dp", axis=0, tiled=True),
        lax.all_gather(w_down, "dp", axis=1, tiled=True),
    )
    micro_count = tokens.shape[0]
    stretch_rows = tokens.shape[1]
    span_blocks = SEQ_LEN // stretch_rows
    outputs = []
    memory = []
    for micro_index in range(micro_count):
        result, kept = forward_block(
            tokens[micro_index], doc_position[micro_index], weights, span_blocks
        )
        outputs.append(result)
        memory.append(kept)
    weights = (
        lax.all_gather(attn_gain, "dp", axis=0, tiled=True),
        lax.all_gather(w_query, "dp", axis=0, tiled=True),
        lax.all_gather(w_key, "dp", axis=0, tiled=True),
        lax.all_gather(w_value, "dp", axis=0, tiled=True),
        lax.all_gather(w_out, "dp", axis=1, tiled=True),
        lax.all_gather(ffn_gain, "dp", axis=0, tiled=True),
        lax.all_gather(w_gate, "dp", axis=0, tiled=True),
        lax.all_gather(w_up, "dp", axis=0, tiled=True),
        lax.all_gather(w_down, "dp", axis=1, tiled=True),
    )
    input_grads = []
    totals = None
    for micro_index in range(micro_count):
        grad_input, terms = backward_block(
            cotangent[micro_index], memory[micro_index], weights, span_blocks
        )
        input_grads.append(grad_input)
        if totals is None:
            totals = terms
        else:
            totals = tuple((earlier + later for earlier, later in zip(totals, terms)))
    (
        gain_one_sum,
        query_sum,
        key_sum,
        value_sum,
        out_sum,
        gain_two_sum,
        gate_sum,
        up_sum,
        down_sum,
    ) = totals
    summed = (
        lax.psum_scatter(gain_one_sum, "dp", scatter_dimension=0, tiled=True),
        lax.psum_scatter(query_sum, "dp", scatter_dimension=0, tiled=True),
        lax.psum_scatter(key_sum, "dp", scatter_dimension=0, tiled=True),
        lax.psum_scatter(value_sum, "dp", scatter_dimension=0, tiled=True),
        lax.psum_scatter(out_sum, "dp", scatter_dimension=1, tiled=True),
        lax.psum_scatter(gain_two_sum, "dp", scatter_dimension=0, tiled=True),
        lax.psum_scatter(gate_sum, "dp", scatter_dimension=0, tiled=True),
        lax.psum_scatter(up_sum, "dp", scatter_dimension=0, tiled=True),
        lax.psum_scatter(down_sum, "dp", scatter_dimension=1, tiled=True),
    )
    return (jnp.stack(outputs), jnp.stack(input_grads)) + tuple(summed)


def solution(mesh):
    return jax.shard_map(
        body,
        mesh=mesh,
        in_specs=(
            P(None, "dp", None),
            P(None, "dp"),
            P("dp"),
            P("dp", "tensor"),
            P("dp", "tensor"),
            P("dp", "tensor"),
            P("tensor", "dp"),
            P("dp"),
            P("dp", "tensor"),
            P("dp", "tensor"),
            P("tensor", "dp"),
            P(None, "dp", None),
        ),
        out_specs=(
            P(None, "dp", None),
            P(None, "dp", None),
            P("dp"),
            P("dp", "tensor"),
            P("dp", "tensor"),
            P("dp", "tensor"),
            P("tensor", "dp"),
            P("dp"),
            P("dp", "tensor"),
            P("dp", "tensor"),
            P("tensor", "dp"),
        ),
        check_vma=False,
    )
```

profile of v0, /device:TPU:0, one launch (start us, length us, event | category | flops | bytes accessed | tf_op | source)
XLA Modules:
  0.0 2057.6 jit_solution(8389004625431570120)
XLA Ops:
  8.0 23.2 %all-gather = bf16[16,1,128]{2,1,0:T(2,128)(2,1)S(1)} all-gather(bf16[1,1,128]{2,1,0:T(2,128)(2,1)} %bitcast.610), channel_id=1, replica_groups=mesh['dp'=16,'tensor'=2] {'dp'}, dimensions={0}, use_global_device_ids=true | all-gather | bytes 4352 | tf_op jit(solution)/shard_map/all_gather | solution.py:289
  33.6 20.6 all_gather.37
  69.7 19.7 all_gather.38
  207.3 13.6 fusion.69
  235.6 18.8 all-gather.1
  254.4 64.9 %all-reduce.12.cloned.1.call-done = (f32[128,2048]{1,0:T(8,128)}, f32[128,2048]{1,0:T(8,128)}, f32[128,2048]{1,0:T(8,128)}) async-done(((f32[128,2048]{1,0:T(8,128)}, f32[128,2048]{1,0:T(8,128)}, f32[128,2048]{1,0:T(8,128)}), (f32[128,2048]{1,0:T(8,128)}, f32[128,2048]{1,0:T(8,128)}, f32[128,2048]{1,0:T(8,128)})) %all-reduce.12.cloned.1.call-update) | async-done | bytes 3145744 | tf_op jit(solution)/shard_map/psum | solution.py:122
  324.1 91.9 %all-gather.12.cloned.1.call-done = bf16[2048,2816]{1,0:T(8,128)(2,1)} async-done(((bf16[128,2816]{1,0:T(8,128)(2,1)}), bf16[2048,2816]{1,0:T(8,128)(2,1)}) %all-gather.12.cloned.1.call-update) | async-done | bytes 11534352 | tf_op jit(solution)/shard_map/all_gather | solution.py:295
  423.1 87.9 %all-gather.14.cloned.1.call-done = bf16[2048,2816]{1,0:T(8,128)(2,1)} async-done(((bf16[128,2816]{1,0:T(8,128)(2,1)}), bf16[2048,2816]{1,0:T(8,128)(2,1)}) %all-gather.14.cloned.1.call-update) | async-done | bytes 11534352 | tf_op jit(solution)/shard_map/all_gather | solution.py:296
  531.9 76.9 %all-gather.16.cloned.1.call-done = bf16[2816,2048]{1,0:T(8,128)(2,1)} async-done(((bf16[2816,128]{1,0:T(8,128)(2,1)}), bf16[2816,2048]{1,0:T(8,128)(2,1)}) %all-gather.16.cloned.1.call-update) | async-done | bytes 11534352 | tf_op jit(solution)/shard_map/all_gather | solution.py:297
  608.8 10.7 multiply_convert_fusion
  620.5 8.2 fusion.280
  628.7 10.7 multiply_convert_fusion.2
  645.3 10.6 multiply_convert_fusion.4
  661.1 9.2 convolution_add_fusion.10
  670.3 9.2 convolution_add_fusion.11
  684.4 8.1 convolution_convert_fusion
  698.4 70.3 %all-reduce.10.cloned.1.call-done = (f32[128,2048]{1,0:T(8,128)}, f32[128,2048]{1,0:T(8,128)}, f32[128,2048]{1,0:T(8,128)}) async-done(((f32[128,2048]{1,0:T(8,128)}, f32[128,2048]{1,0:T(8,128)}, f32[128,2048]{1,0:T(8,128)}), (f32[128,2048]{1,0:T(8,128)}, f32[128,2048]{1,0:T(8,128)}, f32[128,2048]{1,0:T(8,128)})) %all-reduce.10.cloned.1.call-update) | async-done | bytes 3145744 | tf_op jit(solution)/shard_map/psum | solution.py:189
  946.5 9.6 fusion.282
  956.0 9.4 fusion.283
  965.5 25.1 %add_add_fusion.2 = f32[2048,2816]{1,0:T(8,128)} fusion(f32[2048,2816]{1,0:T(8,128)} %fusion.282, f32[2048,2816]{1,0:T(8,128)} %fusion.283, bf16[128,2048]{1,0:T(8,128)(2,1)S(1)} %copy-done.14, bf16[128,2816]{1,0:T(8,128)(2,1)S(1)} %copy-done.49), kind=kOutput, calls=%fused_computation.2 | convolution fusion | flops 1487929344 | bytes 70451200 | tf_op jit(solution)/shard_map/dot_general | solution.py:20
  991.7 9.3 fusion.284
  1001.0 9.4 fusion.285
  1010.4 24.1 %add_add_fusion.1 = f32[2048,2816]{1,0:T(8,128)} fusion(f32[2048,2816]{1,0:T(8,128)} %fusion.284, f32[2048,2816]{1,0:T(8,128)} %fusion.285, bf16[128,2048]{1,0:T(8,128)(2,1)S(1)} %copy-done.14, bf16[128,2816]{1,0:T(8,128)(2,1)S(1)} %copy-done.47), kind=kOutput, calls=%fused_computation.1 | convolution fusion | flops 1487929344 | bytes 70451200 | tf_op jit(solution)/shard_map/dot_general | solution.py:20
  1036.1 9.3 fusion.121
  1045.4 9.4 fusion.117
  1054.8 24.4 %add_add_fusion = f32[2816,2048]{1,0:T(8,128)} fusion(f32[2816,2048]{1,0:T(8,128)} %fusion.121, f32[2816,2048]{1,0:T(8,128)} %fusion.117, bf16[128,2816]{1,0:T(8,128)(2,1)S(1)} %copy-done.35, bf16[3,128,2048]{2,1,0:T(8,128)(2,1)S(1)} %copy-done.37), kind=kOutput, calls=%fused_computation | convolution fusion | flops 1487929344 | bytes 70451200 | tf_op jit(solution)/shard_map/dot_general | solution.py:20
  1083.7 67.3 %all-reduce.2 = (f32[2048]{0:T(1024)S(1)}, f32[2048]{0:T(1024)S(1)}) all-reduce(f32[2048]{0:T(1024)S(1)} %add_add_fusion.6, f32[2048]{0:T(1024)S(1)} %add_add_fusion.5), channel_id=2, replica_groups=mesh['dp'=16,'tensor'=2] {'dp'}, use_global_device_ids=true, to_apply=%region_36.37.clone | all-reduce | flops 4096 | bytes 32768
  1161.3 85.7 %reduce-scatter.8.cloned.1.call-done = f32[128,1024]{1,0:T(8,128)} async-done(((f32[2048,1024]{1,0:T(8,128)}), f32[128,1024]{1,0:T(8,128)}) %reduce-scatter.8.cloned.1.call-update) | async-done | bytes 524304 | tf_op jit(solution)/shard_map/reduce_scatter | solution.py:345
  1246.9 109.7 %reduce-scatter.14.cloned.1.call-done = f32[1024,128]{1,0:T(8,128)} async-done(((f32[1024,2048]{1,0:T(8,128)}), f32[1024,128]{1,0:T(8,128)}) %reduce-scatter.14.cloned.1.call-update) | async-done | bytes 524304 | tf_op jit(solution)/shard_map/reduce_scatter | solution.py:348
  1356.6 231.9 %reduce-scatter.16.cloned.1.call-done = f32[128,2816]{1,0:T(8,128)} async-done(((f32[2048,2816]{1,0:T(8,128)}), f32[128,2816]{1,0:T(8,128)}) %reduce-scatter.16.cloned.1.call-update) | async-done | bytes 1441808 | tf_op jit(solution)/shard_map/reduce_scatter | solution.py:350
  1588.5 231.1 %reduce-scatter.18.cloned.1.call-done = f32[128,2816]{1,0:T(8,128)} async-done(((f32[2048,2816]{1,0:T(8,128)}), f32[128,2816]{1,0:T(8,128)}) %reduce-scatter.18.cloned.1.call-update) | async-done | bytes 1441808 | tf_op jit(solution)/shard_map/reduce_scatter | solution.py:351
  1819.6 231.1 %reduce-scatter.20.cloned.1.call-done = f32[2816,128]{1,0:T(8,128)} async-done(((f32[2816,2048]{1,0:T(8,128)}), f32[2816,128]{1,0:T(8,128)}) %reduce-scatter.20.cloned.1.call-update) | async-done | bytes 1441808 | tf_op jit(solution)/shard_map/reduce_scatter | solution.py:352
  (749 shorter events, 397.7 us)
Async XLA Ops:
  7.2 176.6 %all-gather.8.cloned.1.call-start = ((), (), s32[]{:S(2)}) async-start(), calls=%async_computation.7 | async-start | bytes 4456448 | tf_op jit(solution)/shard_map/all_gather | solution.py:290
  7.9 216.1 %all-gather.10.cloned.1.call-start = ((), (), s32[]{:S(2)}) async-start(), calls=%async_computation.8 | async-start | bytes 4456448 | tf_op jit(solution)/shard_map/all_gather | solution.py:293
  55.7 41.1 %collective-permute-start.28 = (bf16[128,128]{1,0:T(8,128)(2,1)S(1)}, bf16[128,128]{1,0:T(8,128)(2,1)}, u32[]{:S(2)}, u32[]{:S(2)}) collective-permute-start(bf16[128,128]{1,0:T(8,128)(2,1)S(1)} %convolution_convert_fusion.6), channel_id=1, source_target_pairs={{0,14},{2,16},{4,18},{6,20},{8,22},{10,24},{12,26},{14,28},{16,30}... | collective-permute-start | bytes 98312 | tf_op jit(solution)/shard_map/ppermute | solution.py:16
  59.1 42.2 %collective-permute-start.29 = (bf16[128,128]{1,0:T(8,128)(2,1)S(1)}, bf16[128,128]{1,0:T(8,128)(2,1)S(1)}, u32[]{:S(2)}, u32[]{:S(2)}) collective-permute-start(bf16[128,128]{1,0:T(8,128)(2,1)S(1)} %convolution_convert_fusion.6), channel_id=1, source_target_pairs={{0,12},{2,14},{4,16},{6,18},{8,20},{10,22},{12,24},{14,26},{16,28}... | collective-permute-start | bytes 98312 | tf_op jit(solution)/shard_map/ppermute | solution.py:16
  61.6 41.7 %collective-permute-start.30 = (bf16[128,128]{1,0:T(8,128)(2,1)S(1)}, bf16[128,128]{1,0:T(8,128)(2,1)S(1)}, u32[]{:S(2)}, u32[]{:S(2)}) collective-permute-start(bf16[128,128]{1,0:T(8,128)(2,1)S(1)} %convolution_convert_fusion.6), channel_id=1, source_target_pairs={{0,10},{2,12},{4,14},{6,16},{8,18},{10,20},{12,22},{14,24},{16,26}... | collective-permute-start | bytes 98312 | tf_op jit(solution)/shard_map/ppermute | solution.py:16
  62.9 41.8 %collective-permute-start.31 = (bf16[128,128]{1,0:T(8,128)(2,1)S(1)}, bf16[128,128]{1,0:T(8,128)(2,1)S(1)}, u32[]{:S(2)}, u32[]{:S(2)}) collective-permute-start(bf16[128,128]{1,0:T(8,128)(2,1)S(1)} %convolution_convert_fusion.6), channel_id=1, source_target_pairs={{0,8},{2,10},{4,12},{6,14},{8,16},{10,18},{12,20},{14,22},{16,24},... | collective-permute-start | bytes 98312 | tf_op jit(solution)/shard_map/ppermute | solution.py:16
  66.2 42.6 %collective-permute-start.32 = (bf16[128,128]{1,0:T(8,128)(2,1)S(1)}, bf16[128,128]{1,0:T(8,128)(2,1)S(1)}, u32[]{:S(2)}, u32[]{:S(2)}) collective-permute-start(bf16[128,128]{1,0:T(8,128)(2,1)S(1)} %convolution_convert_fusion.6), channel_id=1, source_target_pairs={{0,6},{2,8},{4,10},{6,12},{8,14},{10,16},{12,18},{14,20},{16,22},{... | collective-permute-start | bytes 98312 | tf_op jit(solution)/shard_map/ppermute | solution.py:16
  69.0 250.2 %all-reduce.12.cloned.1.call-start = ((), (), s32[]{:S(2)}) async-start(), calls=%async_computation.20 | async-start | bytes 6291456 | tf_op jit(solution)/shard_map/psum | solution.py:122
  96.8 13.6 collective-permute-start.33
  104.7 13.1 collective-permute-start.36
  120.4 12.5 collective-permute-start.15
  233.8 182.2 %all-gather.12.cloned.1.call-start = ((), (), s32[]{:S(2)}) async-start(), calls=%async_computation.9 | async-start | bytes 12255232 | tf_op jit(solution)/shard_map/all_gather | solution.py:295
  234.4 276.6 %all-gather.14.cloned.1.call-start = ((), (), s32[]{:S(2)}) async-start(), calls=%async_computation.10 | async-start | bytes 12255232 | tf_op jit(solution)/shard_map/all_gather | solution.py:296
  235.0 373.9 %all-gather.16.cloned.1.call-start = ((), (), s32[]{:S(2)}) async-start(), calls=%async_computation.11 | async-start | bytes 12255232 | tf_op jit(solution)/shard_map/all_gather | solution.py:297
  235.5 533.2 %all-reduce.10.cloned.1.call-start = ((), (), s32[]{:S(2)}) async-start(), calls=%async_computation.19 | async-start | bytes 6291456 | tf_op jit(solution)/shard_map/psum | solution.py:189
  684.2 396.9 %all-reduce.14.cloned.1.call-start = ((), (), s32[]{:S(2)}) async-start(), calls=%async_computation.21 | async-start | bytes 6291456 | tf_op jit(solution)/shard_map/psum | solution.py:129
  871.3 12.2 collective-permute-start.83
  872.6 12.2 collective-permute-start.82
  873.9 12.5 collective-permute-start.81
  875.2 12.5 collective-permute-start.80
  876.5 12.5 collective-permute-start.79
  889.1 13.0 collective-permute-start.67
  890.4 12.9 collective-permute-start.66
  891.7 12.9 collective-permute-start.65
  904.7 13.1 collective-permute-start.53
  921.1 240.2 %reduce-scatter.10.cloned.1.call-start = ((), (), s32[]{:S(2)}) async-start(), calls=%async_computation.13 | async-start | bytes 1114112 | tf_op jit(solution)/shard_map/reduce_scatter | solution.py:346
  925.5 235.7 %reduce-scatter.12.cloned.1.call-start = ((), (), s32[]{:S(2)}) async-start(), calls=%async_computation.14 | async-start | bytes 1114112 | tf_op jit(solution)/shard_map/reduce_scatter | solution.py:347
  928.5 318.4 %reduce-scatter.8.cloned.1.call-start = ((), (), s32[]{:S(2)}) async-start(), calls=%async_computation.12 | async-start | bytes 8912896 | tf_op jit(solution)/shard_map/reduce_scatter | solution.py:345
  936.9 419.7 %reduce-scatter.14.cloned.1.call-start = ((), (), s32[]{:S(2)}) async-start(), calls=%async_computation.15 | async-start | bytes 8912896 | tf_op jit(solution)/shard_map/reduce_scatter | solution.py:348
  945.2 643.2 %reduce-scatter.16.cloned.1.call-start = ((), (), s32[]{:S(2)}) async-start(), calls=%async_computation.16 | async-start | bytes 24510464 | tf_op jit(solution)/shard_map/reduce_scatter | solution.py:350
  990.6 828.9 %reduce-scatter.18.cloned.1.call-start = ((), (), s32[]{:S(2)}) async-start(), calls=%async_computation.17 | async-start | bytes 24510464 | tf_op jit(solution)/shard_map/reduce_scatter | solution.py:351
  1034.5 1016.1 %reduce-scatter.20.cloned.1.call-start = ((), (), s32[]{:S(2)}) async-start(), calls=%async_computation.18 | async-start | bytes 24510464 | tf_op jit(solution)/shard_map/reduce_scatter | solution.py:352
  (238 other events, 4873.8 us)
Sparse Core Ops, SparseCore 0:
  10.2 54.9 all-gather.7
  69.2 56.3 all-gather.9
  233.9 85.3 all-reduce.11
  321.7 94.3 all-gather.11
  418.4 92.4 all-gather.13
  513.2 95.6 all-gather.15
  684.4 84.2 all-reduce.9
  921.2 94.3 all-reduce.13
  1020.2 57.3 reduce-scatter.9
  1081.7 56.4 reduce-scatter.11
  1143.3 103.5 reduce-scatter.7
  1252.0 104.5 reduce-scatter.13
  1361.8 226.5 reduce-scatter.15
  1593.6 225.9 reduce-scatter.17
  1824.7 225.9 reduce-scatter.19
where the time goes:
time: 2070 us; the launch traced here: 2060 us
  waiting for transfers between devices  1310 us (63%)
  matrix products  354 us (17%)
  blocking collectives  150 us (7%)
  starting transfers between devices  146 us (7%)
  other arithmetic  53.6 us (3%)
  local copies, waits for them, and re-layouts  27.8 us (1%)
    reduce_scatter x1, waiting for transfers between devices, body(): lax.psum_scatter(gate_sum, 'dp', scatter_dimension=0, tiled=True)  232 us
    reduce_scatter x1, waiting for transfers between devices, body(): lax.psum_scatter(up_sum, 'dp', scatter_dimension=0, tiled=True)  231 us
    reduce_scatter x1, waiting for transfers between devices, body(): lax.psum_scatter(down_sum, 'dp', scatter_dimension=1, tiled=True)  231 us
    dot_general x21, matrix products, dot_first(): lax.dot_general(left, right, (((0,), (0,)), ((), ())), preferred_element_...  152 us
    ppermute x84, starting transfers between devices, passed_along(): return lax.ppermute(block, axis, route)  145 us
    reduce_scatter x1, waiting for transfers between devices, body(): lax.psum_scatter(out_sum, 'dp', scatter_dimension=1, tiled=True)  110 us
    all_gather x1, waiting for transfers between devices, body(): lax.all_gather(w_gate, 'dp', axis=0, tiled=True)  91.9 us
    all_gather x1, waiting for transfers between devices, body(): lax.all_gather(w_up, 'dp', axis=0, tiled=True)  87.9 us
  transfers between devices with their start and end apart: 99, of which 16 were waited for; matrix products, arithmetic and copies ran while one was open for 14% of the time, Pallas kernels for 0%

commit v1 on v0

v1 whole, which is shorter than its diff:
```python
import functools

import jax
import jax.numpy as jnp
from jax import lax
from jax.experimental import pallas as pl
from jax.experimental.pallas import tpu as pltpu
from jax.sharding import PartitionSpec as P

HEAD_DIM = 64
SEQ_LEN = 1024
BF = jnp.bfloat16
F32 = jnp.float32
epsilon = 1e-05
VMEM_LIMIT = 48 * 1024 * 1024


def swap_core(block):
    size = lax.axis_size("dp")
    return lax.ppermute(block, "dp", [(i, i ^ 1) for i in range(size)])


def swap_chip(block, distance):
    size = lax.axis_size("dp")
    return lax.ppermute(block, "dp", [(i, i ^ (2 * distance)) for i in range(size)])


def swap_tensor(block):
    return lax.ppermute(block, "tensor", [(0, 1), (1, 0)])


def gather_blocks(own, order):
    held = {0: own}
    for bit in order:
        came = {key | bit: swap_chip(block, bit) for key, block in held.items()}
        held.update(came)
    return held


def scatter_blocks(blocks, order):
    held = dict(blocks)
    for bit in reversed(order):
        kept = {}
        for key in sorted(held):
            if key & bit:
                came = swap_chip(held[key].astype(BF), bit)
                kept[key ^ bit] = came
        held = {key: held[key].astype(F32) + came.astype(F32) for key, came in kept.items()}
    return held[0]


def dot_plain(left, right):
    return jnp.dot(left, right, preferred_element_type=F32)


def dot_first(left, right):
    return lax.dot_general(left, right, (((0,), (0,)), ((), ())), preferred_element_type=F32)


def dot_last(left, right):
    return lax.dot_general(left, right, (((1,), (1,)), ((), ())), preferred_element_type=F32)


def norm_back(grad, value, ratio, gain):
    scaled = grad * gain
    inner = jnp.mean(scaled * value, axis=-1, keepdims=True)
    return (ratio * scaled - value * ratio**3 * inner, jnp.sum(grad * value * ratio, axis=0))


def turn(value, cosine, sine, back):
    tiles = []
    lane = lax.broadcasted_iota(jnp.int32, (value.shape[0], 128), 1)
    first = (lane % 64) < 32
    for start in range(0, value.shape[1], 128):
        tile = value[:, start : start + 128]
        up = pltpu.roll(tile, 96, 1)
        down = pltpu.roll(tile, 32, 1)
        if back:
            other = jnp.where(first, up, -down)
        else:
            other = jnp.where(first, -up, down)
        tiles.append(tile * cosine + other * sine)
    return tiles[0] if len(tiles) == 1 else jnp.concatenate(tiles, axis=1)


def project_kernel(n_ref, w_ref, cos_ref, sin_ref, q_ref, kv_ref):
    raw = jnp.dot(n_ref[...], w_ref[...], preferred_element_type=F32)
    heads = raw.shape[1] - 128
    cosine, sine = cos_ref[...], sin_ref[...]
    q_ref[...] = (turn(raw[:, :heads], cosine, sine, False) * HEAD_DIM ** (-0.5)).astype(BF)
    both = raw[:, heads:]
    turned = turn(both, cosine, sine, False)
    lane = lax.broadcasted_iota(jnp.int32, both.shape, 1)
    kv_ref[...] = jnp.where(lane < HEAD_DIM, turned, both).astype(BF)


def project(normed, weight, cosine, sine):
    rows, depth = normed.shape
    cols = weight.shape[1]
    step = 256
    return pl.pallas_call(
        project_kernel,
        grid=(rows // step,),
        in_specs=[
            pl.BlockSpec((step, depth), lambda i: (i, 0)),
            pl.BlockSpec((depth, cols), lambda i: (0, 0)),
            pl.BlockSpec((step, 128), lambda i: (i, 0)),
            pl.BlockSpec((step, 128), lambda i: (i, 0)),
        ],
        out_specs=[
            pl.BlockSpec((step, cols - 128), lambda i: (i, 0)),
            pl.BlockSpec((step, 128), lambda i: (i, 0)),
        ],
        out_shape=[
            jax.ShapeDtypeStruct((rows, cols - 128), BF),
            jax.ShapeDtypeStruct((rows, 128), BF),
        ],
        compiler_params=pltpu.CompilerParams(vmem_limit_bytes=VMEM_LIMIT),
        cost_estimate=pl.CostEstimate(
            flops=2 * rows * depth * cols,
            bytes_accessed=2 * (rows * depth + depth * cols + rows * cols) + 8 * rows * 128,
            transcendentals=0,
        ),
        name="project",
    )(normed, weight, cosine, sine)


def mask_bias(kpos_ref, row_ref):
    row = row_ref[0]
    place, floor = row[0:1, :], row[1:2, :]
    kpos = kpos_ref[...]
    allowed = (kpos <= place) & (kpos >= floor)
    return jnp.where(allowed, 0.0, -1e30).astype(F32)


def attend_kernel(count, kpos_ref, row_ref, q_ref, *refs):
    kv_refs, (mixed_ref, lse_ref, bias_ref) = refs[:count], refs[count:]
    rows = 256
    kv = jnp.concatenate([ref[...].reshape(rows, 128) for ref in kv_refs], axis=0)
    keys = kv[:, :HEAD_DIM]
    values_t = kv.T[HEAD_DIM:, :]
    bias_ref[...] = mask_bias(kpos_ref, row_ref)
    queries = q_ref[...].reshape(rows, q_ref.shape[-1])
    parts = []
    sums = []
    for head in range(queries.shape[1] // HEAD_DIM):
        q_head = queries[:, head * HEAD_DIM : (head + 1) * HEAD_DIM]
        scores = dot_last(keys, q_head) + bias_ref[...]
        peak = jnp.max(scores, axis=0, keepdims=True)
        expon = jnp.exp(scores - peak)
        total = jnp.sum(expon, axis=0, keepdims=True)
        mixed = dot_plain(values_t, expon.astype(BF)) * (1.0 / total)
        parts.append(mixed)
        sums.append(peak + jnp.log(total))
    mixed_t = jnp.concatenate(parts, axis=0)
    mixed_ref[...] = mixed_t.T.astype(BF).reshape(mixed_ref.shape)
    lse_ref[0] = jnp.concatenate(sums, axis=0)


def attend(kpos, rowinfo, queries, kvs):
    half, micro, rows, cols = queries.shape
    heads = cols // HEAD_DIM
    span = kpos.shape[0]
    tokens = half * rows
    kv_spec = pl.BlockSpec((half, 1, rows, 128), lambda i: (0, i, 0, 0))
    q_spec = pl.BlockSpec((half, 1, rows, cols), lambda i: (0, i, 0, 0))
    return pl.pallas_call(
        functools.partial(attend_kernel, len(kvs)),
        grid=(micro,),
        in_specs=[
            pl.BlockSpec((span, 1), lambda i: (0, 0)),
            pl.BlockSpec((1, 2, tokens), lambda i: (i, 0, 0)),
            q_spec,
        ]
        + [kv_spec] * len(kvs),
        out_specs=[q_spec, pl.BlockSpec((1, heads, tokens), lambda i: (i, 0, 0))],
        out_shape=[
            jax.ShapeDtypeStruct(queries.shape, BF),
            jax.ShapeDtypeStruct((micro, heads, tokens), F32),
        ],
        scratch_shapes=[pltpu.VMEM((span, tokens), F32)],
        compiler_params=pltpu.CompilerParams(vmem_limit_bytes=VMEM_LIMIT),
        cost_estimate=pl.CostEstimate(
            flops=16 * micro * heads * tokens * span * HEAD_DIM,
            bytes_accessed=4 * micro * tokens * cols,
            transcendentals=micro * heads * tokens * span,
        ),
        name="attend",
    )(kpos, rowinfo, queries, *kvs)


def attend_back_kernel(
    count, kpos_ref, row_ref, cos_ref, sin_ref, q_ref, go_ref, lse_ref, *refs
):
    kv_refs = refs[:count]
    dq_ref = refs[count]
    dkv_refs = refs[count + 1 : 2 * count + 1]
    bias_ref, dk_ref, dv_ref = refs[2 * count + 1 :]
    rows = 256
    kv = jnp.concatenate([ref[...].reshape(rows, 128) for ref in kv_refs], axis=0)
    keys = kv[:, :HEAD_DIM]
    values = kv[:, HEAD_DIM:]
    keys_t = kv.T[:HEAD_DIM, :]
    bias_ref[...] = mask_bias(kpos_ref, row_ref)
    queries = q_ref[...].reshape(rows, q_ref.shape[-1])
    grads = go_ref[...].reshape(rows, q_ref.shape[-1])
    parts = []
    for head in range(queries.shape[1] // HEAD_DIM):
        q_head = queries[:, head * HEAD_DIM : (head + 1) * HEAD_DIM]
        g_head = grads[:, head * HEAD_DIM : (head + 1) * HEAD_DIM]
        scores = dot_last(keys, q_head) + bias_ref[...]
        probs = jnp.exp(scores - lse_ref[0, head : head + 1, :])
        grad_probs = dot_last(values, g_head)
        inner = jnp.sum(probs * grad_probs, axis=0, keepdims=True)
        grad_scores = (probs * (grad_probs - inner)).astype(BF)
        grad_values = dot_plain(probs.astype(BF), g_head)
        grad_keys = dot_plain(grad_scores, q_head)
        if head == 0:
            dv_ref[...] = grad_values
            dk_ref[...] = grad_keys
        else:
            dv_ref[...] += grad_values
            dk_ref[...] += grad_keys
        parts.append(dot_plain(keys_t, grad_scores))
    grad_queries = jnp.concatenate(parts, axis=0).T * HEAD_DIM ** (-0.5)
    cosine = cos_ref[...].reshape(rows, 128)
    sine = sin_ref[...].reshape(rows, 128)
    dq_ref[...] = turn(grad_queries, cosine, sine, True).astype(BF).reshape(dq_ref.shape)
    both = jnp.concatenate([dk_ref[...], dv_ref[...]], axis=1)
    for place, ref in enumerate(dkv_refs):
        ref[...] = both[place * rows : (place + 1) * rows].astype(ref.dtype).reshape(ref.shape)


def attend_back(kpos, rowinfo, cosine, sine, queries, grads, lse, kvs):
    half, micro, rows, cols = queries.shape
    heads = cols // HEAD_DIM
    span = kpos.shape[0]
    tokens = half * rows
    kv_spec = pl.BlockSpec((half, 1, rows, 128), lambda i: (0, i, 0, 0))
    q_spec = pl.BlockSpec((half, 1, rows, cols), lambda i: (0, i, 0, 0))
    return pl.pallas_call(
        functools.partial(attend_back_kernel, len(kvs)),
        grid=(micro,),
        in_specs=[
            pl.BlockSpec((span, 1), lambda i: (0, 0)),
            pl.BlockSpec((1, 2, tokens), lambda i: (i, 0, 0)),
            kv_spec,
            kv_spec,
            q_spec,
            q_spec,
            pl.BlockSpec((1, heads, tokens), lambda i: (i, 0, 0)),
        ]
        + [kv_spec] * len(kvs),
        out_specs=[q_spec] + [kv_spec] * len(kvs),
        out_shape=[jax.ShapeDtypeStruct(queries.shape, BF)]
        + [
            jax.ShapeDtypeStruct((half, micro, rows, 128), F32 if place == 0 else BF)
            for place in range(len(kvs))
        ],
        scratch_shapes=[
            pltpu.VMEM((span, tokens), F32),
            pltpu.VMEM((span, HEAD_DIM), F32),
            pltpu.VMEM((span, HEAD_DIM), F32),
        ],
        compiler_params=pltpu.CompilerParams(vmem_limit_bytes=VMEM_LIMIT),
        cost_estimate=pl.CostEstimate(
            flops=40 * micro * heads * tokens * span * HEAD_DIM,
            bytes_accessed=8 * micro * tokens * cols,
            transcendentals=micro * heads * tokens * span,
        ),
        name="attend_back",
    )(kpos, rowinfo, cosine, sine, queries, grads, lse, *kvs)


def body(
    tokens,
    doc_position,
    attn_gain,
    w_query,
    w_key,
    w_value,
    w_out,
    ffn_gain,
    w_gate,
    w_up,
    w_down,
    cotangent,
):
    size = lax.axis_size("dp")
    chips = size // 2
    bits = [1 << place for place in range(chips.bit_length() - 1)]
    me = lax.axis_index("dp")
    core = me % 2
    chip = me // 2
    micro, stretch, width = tokens.shape
    count = micro * stretch
    block = width // chips

    late_first = bits[::-1]
    span_chips = SEQ_LEN // (2 * stretch)
    in_span = chip % span_chips

    keys_order = [0]
    for bit in late_first:
        keys_order = keys_order + [key | bit for key in keys_order]

    def rearranged(array):
        return jnp.concatenate(
            [
                lax.dynamic_slice_in_dim(array, (chip ^ key) * block, block, array.ndim - 1)
                for key in keys_order
            ],
            axis=-1,
        )

    def restored(array):
        where = [keys_order.index(key) for key in range(chips)]
        places = jnp.array(where, jnp.int32)
        return jnp.concatenate(
            [
                lax.dynamic_slice_in_dim(
                    array, places[chip ^ natural] * block, block, array.ndim - 1
                )
                for natural in range(chips)
            ],
            axis=-1,
        )

    def split_core(weight):
        half = weight.shape[1] // 2
        first, second = weight[:, :half], weight[:, half:]
        mine = jnp.where(core == 0, first, second)
        other = jnp.where(core == 0, second, first)
        return mine, other

    def joined_core(mine, came):
        return jnp.where(
            core == 0,
            jnp.concatenate([mine, came], axis=0),
            jnp.concatenate([came, mine], axis=0),
        )

    attn_parts = [split_core(w) for w in (w_query, w_key, w_value, w_out.T)]
    attn_mine = jnp.concatenate([p[0] for p in attn_parts], axis=1)
    attn_other = jnp.concatenate([p[1] for p in attn_parts], axis=1)
    attn_own = joined_core(attn_mine, swap_core(attn_other))
    gate_parts = split_core(w_gate)
    gate_own = joined_core(gate_parts[0], swap_core(gate_parts[1]))
    up_parts = split_core(w_up)
    up_own = joined_core(up_parts[0], swap_core(up_parts[1]))
    down_parts = split_core(w_down.T)
    down_own = joined_core(down_parts[0], swap_core(down_parts[1]))

    def whole(own, order):
        held = gather_blocks(own, order)
        return jnp.concatenate([held[key] for key in keys_order], axis=0)

    gains = jnp.stack([attn_gain, ffn_gain])
    gains = lax.all_gather(gains, "dp", axis=1, tiled=True).astype(F32)
    gains = rearranged(gains)
    gain_one, gain_two = gains[0:1], gains[1:2]

    hidden = rearranged(tokens.reshape(count, width))
    grad_final = rearranged(cotangent.reshape(count, width))
    hidden_f = hidden.astype(F32)
    ratio_one = lax.rsqrt(jnp.mean(hidden_f * hidden_f, axis=-1, keepdims=True) + epsilon)
    normed_own = (hidden_f * ratio_one * gain_one).astype(BF)
    normed = jnp.concatenate([normed_own, swap_core(normed_own)], axis=0)
    grad_final_both = jnp.concatenate([grad_final, swap_core(grad_final)], axis=0)
    position_both = jnp.stack([doc_position, swap_core(doc_position)])

    power = jnp.arange(HEAD_DIM // 2, dtype=F32) * (2.0 / HEAD_DIM)
    inverse = 10000.0 ** (-power)
    turned = position_both.reshape(2 * count).astype(F32)[:, None] * jnp.tile(inverse, 4)[None, :]
    cosine, sine = jnp.cos(turned), jnp.sin(turned)

    inner = jnp.arange(2 * stretch, dtype=jnp.int32) ^ (core * stretch)
    row_place = in_span * (2 * stretch) + inner
    kpos = jnp.concatenate(
        [(in_span ^ key) * (2 * stretch) + inner for key in range(span_chips)]
    ).reshape(-1, 1)
    row_position = position_both.transpose(1, 0, 2).reshape(micro, 2 * stretch)
    row_places = jnp.broadcast_to(row_place[None, :], row_position.shape)
    rowinfo = jnp.stack([row_places, row_places - row_position], axis=1)

    attn_w = whole(attn_own, late_first)
    n_q = w_query.shape[1] // 2
    n_kv = w_key.shape[1] // 2
    qkv_w = attn_w[:, : n_q + 2 * n_kv]
    out_wt = attn_w[:, n_q + 2 * n_kv :]
    queries, kv_own = project(normed, qkv_w, cosine, sine)
    kv_shape = (2, micro, stretch, 2 * n_kv)
    kvs = [kv_own.reshape(kv_shape)] + [
        swap_chip(kv_own, key).reshape(kv_shape) for key in range(1, span_chips)
    ]
    queries = queries.reshape(2, micro, stretch, n_q)
    mixed, lse = attend(kpos, rowinfo, queries, kvs)
    mixed = mixed.reshape(2 * count, n_q)

    def summed(partial):
        partial = partial.astype(BF)
        mine = (partial[:count].astype(F32) + swap_core(partial[count:]).astype(F32)).astype(BF)
        return mine.astype(F32) + swap_tensor(mine).astype(F32)

    attended = summed(dot_last(mixed, out_wt))
    middle = hidden_f + attended
    ratio_two = lax.rsqrt(jnp.mean(middle * middle, axis=-1, keepdims=True) + epsilon)
    normed_two_own = (middle * ratio_two * gain_two).astype(BF)
    normed_two = jnp.concatenate([normed_two_own, swap_core(normed_two_own)], axis=0)

    gate_w = whole(gate_own, late_first)
    up_w = whole(up_own, late_first)
    down_wt = whole(down_own, late_first)
    gate = dot_plain(normed_two, gate_w)
    upward = dot_plain(normed_two, up_w)
    sigmoid = jax.nn.sigmoid(gate)
    silu = gate * sigmoid
    activated = (silu * upward).astype(BF)

    def weight_grad(left, right, order):
        first = order[-1]
        top = [place for place, key in enumerate(keys_order) if key & first]
        half = chips // 2
        assert top == list(range(half, chips))
        sent = dot_first(left[:, half * block :], right).astype(BF)
        kept = dot_first(left[:, : half * block], right)
        blocks = {}
        for place in range(half):
            blocks[keys_order[place]] = kept[place * block : (place + 1) * block]
            blocks[keys_order[place + half]] = sent[place * block : (place + 1) * block]
        return scatter_blocks(blocks, order)

    def unsplit_core(total):
        half = block // 2
        mine = jnp.where(core == 0, total[:half], total[half:])
        other = jnp.where(core == 0, total[half:], total[:half])
        came = swap_core(other)
        return mine, came

    def columns(mine, came):
        return jnp.where(
            core == 0,
            jnp.concatenate([mine, came], axis=1),
            jnp.concatenate([came, mine], axis=1),
        )

    grad_down = weight_grad(grad_final_both, activated, late_first)
    feed = summed(dot_last(activated, down_wt))
    output = restored((middle + feed).astype(BF))

    grad_act = dot_plain(grad_final_both, down_wt)
    grad_gate_low = (grad_act * upward * sigmoid * (1.0 + gate * (1.0 - sigmoid))).astype(BF)
    grad_up_low = (grad_act * silu).astype(BF)
    grad_normed_two = summed(dot_last(grad_gate_low, gate_w) + dot_last(grad_up_low, up_w))
    grad_gate = weight_grad(normed_two, grad_gate_low, late_first)
    grad_up = weight_grad(normed_two, grad_up_low, late_first)
    grad_mid_norm, grad_gain_two = norm_back(grad_normed_two, middle, ratio_two, gain_two)
    grad_middle = grad_final.astype(F32) + grad_mid_norm
    grad_middle_low = grad_middle.astype(BF)
    grad_middle_both = jnp.concatenate([grad_middle_low, swap_core(grad_middle_low)], axis=0)

    grad_mixed = dot_plain(grad_middle_both, out_wt).astype(BF)
    results = attend_back(
        kpos,
        rowinfo,
        cosine.reshape(2, micro, stretch, 128),
        sine.reshape(2, micro, stretch, 128),
        queries,
        grad_mixed.reshape(queries.shape),
        lse,
        kvs,
    )
    grad_query_raw = results[0].reshape(2 * count, n_q)
    grad_kv = results[1].reshape(2 * count, 2 * n_kv)
    for key in range(1, span_chips):
        grad_kv = grad_kv + swap_chip(results[1 + key].reshape(2 * count, 2 * n_kv), key).astype(
            F32
        )
    grad_k, grad_v = grad_kv[:, :n_kv], grad_kv[:, n_kv:]
    half_dim = HEAD_DIM // 2
    cos_h, sin_h = cosine[:, :half_dim], sine[:, :half_dim]
    first_half, second_half = grad_k[:, :half_dim], grad_k[:, half_dim:]
    grad_raw = jnp.concatenate(
        [
            grad_query_raw,
            (first_half * cos_h + second_half * sin_h).astype(BF),
            (second_half * cos_h - first_half * sin_h).astype(BF),
            grad_v.astype(BF),
        ],
        axis=1,
    )
    grad_out_t = weight_grad(grad_middle_both, mixed, late_first)
    grad_qkv = weight_grad(normed, grad_raw, late_first)
    grad_normed = summed(dot_last(grad_raw, qkv_w))
    grad_in_norm, grad_gain_one = norm_back(grad_normed, hidden_f, ratio_one, gain_one)
    grad_tokens = restored(grad_middle + grad_in_norm)

    grad_gains = restored(jnp.stack([grad_gain_one, grad_gain_two]))
    grad_gains = lax.psum_scatter(grad_gains, "dp", scatter_dimension=1, tiled=True)

    def split_cols(pair, start, stop):
        return columns(pair[0][:, start:stop], pair[1][:, start:stop])

    pair = unsplit_core(grad_qkv)
    grad_w_query = split_cols(pair, 0, n_q)
    grad_w_key = split_cols(pair, n_q, n_q + n_kv)
    grad_w_value = split_cols(pair, n_q + n_kv, n_q + 2 * n_kv)
    grad_w_out = columns(*unsplit_core(grad_out_t)).T
    grad_w_gate = columns(*unsplit_core(grad_gate))
    grad_w_up = columns(*unsplit_core(grad_up))
    grad_w_down = columns(*unsplit_core(grad_down)).T
    return (
        output.reshape(tokens.shape),
        grad_tokens.reshape(tokens.shape),
        grad_gains[0],
        grad_w_query,
        grad_w_key,
        grad_w_value,
        grad_w_out,
        grad_gains[1],
        grad_w_gate,
        grad_w_up,
        grad_w_down,
    )


def solution(mesh):
    return jax.shard_map(
        body,
        mesh=mesh,
        in_specs=(
            P(None, "dp", None),
            P(None, "dp"),
            P("dp"),
            P("dp", "tensor"),
            P("dp", "tensor"),
            P("dp", "tensor"),
            P("tensor", "dp"),
            P("dp"),
            P("dp", "tensor"),
            P("dp", "tensor"),
            P("tensor", "dp"),
            P(None, "dp", None),
        ),
        out_specs=(
            P(None, "dp", None),
            P(None, "dp", None),
            P("dp"),
            P("dp", "tensor"),
            P("dp", "tensor"),
            P("dp", "tensor"),
            P("tensor", "dp"),
            P("dp"),
            P("dp", "tensor"),
            P("dp", "tensor"),
            P("tensor", "dp"),
        ),
        check_vma=False,
    )
```

time: 2070 us -> 999 us (0.48)
  waiting for transfers between devices: 1310 us -> 611 us
  matrix products: 354 us -> 95.3 us
  blocking collectives: 150 us -> 22.6 us
  starting transfers between devices: 146 us -> 79.1 us
  Pallas kernels: 0 us -> 44.9 us
  local copies, waits for them, and re-layouts: 27.8 us -> 50.8 us
    reduce_scatter x7 -> x0, waiting for transfers between devices: 889 us -> none  [the longest x1 232 us: body(): lax.psum_scatter(gate_sum, 'dp', scatter_dimension=0, tiled=True)]
    ppermute x84 -> x91, waiting for transfers between devices: 23.6 us -> 556 us  [the longest x69 511 us: swap_chip(): lax.ppermute(block, 'dp', [(i, i ^ 2 * distance) for i in range(size)])]
    all_gather x5 -> x0, waiting for transfers between devices: 257 us -> none  [the longest x1 91.9 us: body(): lax.all_gather(w_gate, 'dp', axis=0, tiled=True)]
    psum x3 -> x0, waiting for transfers between devices: 135 us -> none  [the longest x1 70.3 us: backward_block(): lax.psum(dot_last(grad_gate_low, gate_w) + dot_last(grad_up_low, up_w), '...]
    dot_general x21 -> x10, matrix products: 152 us -> 34.5 us  [dot_first(): lax.dot_general(left, right, (((0,), (0,)), ((), ())), preferred_element_...]
    dot_general x42 -> x4, matrix products: 146 us -> 33.8 us  [dot_plain(): return jnp.dot(left, right, preferred_element_type=F32)]
    unnamed x1 -> x0, blocking collectives: 67.3 us -> none
    ppermute x84 -> x91, starting transfers between devices: 145 us -> 79 us  [the longest x69 71.4 us: swap_chip(): lax.ppermute(block, 'dp', [(i, i ^ 2 * distance) for i in range(size)])]
  transfers between devices with their start and end apart: 99 -> 92, of which waited for: 16 -> 46; matrix products, arithmetic and copies ran while one was open for 14% -> 17% of each run, Pallas kernels for 0% -> 2%
where the time goes in v1:
time: 999 us; the launch traced here: 990 us
  waiting for transfers between devices  611 us (61%)
  matrix products  95.3 us (10%)
  starting transfers between devices  79.1 us (8%)
  other arithmetic  66.3 us (7%)
  local copies, waits for them, and re-layouts  50.8 us (5%)
  Pallas kernels  44.9 us (4%)
  blocking collectives  22.6 us (2%)
  between operations  20.8 us (2%)
    ppermute x69, waiting for transfers between devices, swap_chip(): lax.ppermute(block, 'dp', [(i, i ^ 2 * distance) for i in range(size)])  511 us
    ppermute x69, starting transfers between devices, swap_chip(): lax.ppermute(block, 'dp', [(i, i ^ 2 * distance) for i in range(size)])  71.4 us
    unnamed x2, waiting for transfers between devices  54.3 us
    ppermute x4, waiting for transfers between devices, swap_tensor(): return lax.ppermute(block, 'tensor', [(0, 1), (1, 0)])  45 us
    unnamed x173, local copies, waits for them, and re-layouts  36.5 us
    dot_general x10, matrix products, dot_first(): lax.dot_general(left, right, (((0,), (0,)), ((), ())), preferred_element_...  34.5 us
    dot_general x4, matrix products, dot_plain(): return jnp.dot(left, right, preferred_element_type=F32)  33.8 us
    dot_general x5, matrix products, dot_last(): lax.dot_general(left, right, (((1,), (1,)), ((), ())), preferred_element_...  27 us
  transfers between devices with their start and end apart: 92, of which 46 were waited for; matrix products, arithmetic and copies ran while one was open for 17% of the time, Pallas kernels for 2%

profile of v1, /device:TPU:0, one launch (start us, length us, event | category | flops | bytes accessed | tf_op | source)
XLA Modules:
  0.0 990.3 jit_solution(1479824892084261927)
XLA Ops:
  22.9 22.6 %all_gather.3 = bf16[2,2048]{1,0:T(2,128)(2,1)S(1)} all-gather(bf16[2,128]{1,0:T(2,128)(2,1)S(1)} %pad_maximum_fusion.11), channel_id=1, replica_groups=mesh['dp'=16,'tensor'=2] {'dp'}, dimensions={1}, use_global_device_ids=true | all-gather | bytes 8704 | tf_op jit(solution)/shard_map/all_gather | solution.py:359
  81.3 19.0 %collective-permute-done.3 = bf16[256,1152]{1,0:T(8,128)(2,1)S(1)} collective-permute-done((bf16[256,1152]{1,0:T(8,128)(2,1)S(1)}, bf16[256,1152]{1,0:T(8,128)(2,1)S(1)}, u32[]{:S(2)}, u32[]{:S(2)}) %collective-permute-start.3) | collective-permute-done | bytes 589856 | tf_op jit(solution)/shard_map/ppermute | solution.py:25
  103.3 28.0 %collective-permute-done.25 = bf16[256,1408]{1,0:T(8,128)(2,1)S(1)} collective-permute-done((bf16[256,1408]{1,0:T(8,128)(2,1)S(1)}, bf16[256,1408]{1,0:T(8,128)(2,1)S(1)}, u32[]{:S(2)}, u32[]{:S(2)}) %collective-permute-start.25) | collective-permute-done | bytes 720928 | tf_op jit(solution)/shard_map/ppermute | solution.py:25
  133.9 27.8 %collective-permute-done.17 = bf16[256,1408]{1,0:T(8,128)(2,1)S(1)} collective-permute-done((bf16[256,1408]{1,0:T(8,128)(2,1)S(1)}, bf16[256,1408]{1,0:T(8,128)(2,1)S(1)}, u32[]{:S(2)}, u32[]{:S(2)}) %collective-permute-start.17) | collective-permute-done | bytes 720928 | tf_op jit(solution)/shard_map/ppermute | solution.py:25
  164.8 13.0 %collective-permute-done.7 = bf16[256,1152]{1,0:T(8,128)(2,1)S(1)} collective-permute-done((bf16[256,1152]{1,0:T(8,128)(2,1)S(1)}, bf16[256,1152]{1,0:T(8,128)(2,1)S(1)}, u32[]{:S(2)}, u32[]{:S(2)}) %collective-permute-start.7) | collective-permute-done | bytes 589856 | tf_op jit(solution)/shard_map/ppermute | solution.py:25
  177.9 12.6 %collective-permute-done.8 = bf16[256,1152]{1,0:T(8,128)(2,1)S(1)} collective-permute-done((bf16[256,1152]{1,0:T(8,128)(2,1)S(1)}, bf16[256,1152]{1,0:T(8,128)(2,1)S(1)}, u32[]{:S(2)}, u32[]{:S(2)}) %collective-permute-start.8) | collective-permute-done | bytes 589856 | tf_op jit(solution)/shard_map/ppermute | solution.py:25
  194.0 23.6 %collective-permute-done.9 = bf16[256,1152]{1,0:T(8,128)(2,1)S(1)} collective-permute-done((bf16[256,1152]{1,0:T(8,128)(2,1)S(1)}, bf16[256,1152]{1,0:T(8,128)(2,1)S(1)}, u32[]{:S(2)}, u32[]{:S(2)}) %collective-permute-start.9) | collective-permute-done | bytes 589856 | tf_op jit(solution)/shard_map/ppermute | solution.py:25
  236.4 17.4 %attend.1 = (bf16[2,3,128,512]{3,2,1,0:T(8,128)(2,1)S(1)}, f32[3,8,256]{2,1,0:T(8,128)S(1)}) custom-call(s32[1024,1]{1,0:T(8,128)S(1)} %copy.56.kpos_ref, s32[3,2,256]{2,1,0:T(2,128)S(1)} %pad_add_fusion.row_ref, bf16[2,3,128,512]{3,2,1,0:T(8,128)(2,1)S(1)} %bitcast.80, bf16[2,3,128,128]{3,2,1,0:T(8,128)(2,1)S(1)} %bitcast.69, ...), custom_call_target="tpu_custom_call" | custom-call | flops 6442450944 | bytes 1572864 | tf_op jit(solution)/shard_map/attend/pallas_call | solution.py:167
  291.8 13.4 %collective-permute-done.30 = bf16[256,1408]{1,0:T(8,128)(2,1)S(1)} collective-permute-done((bf16[256,1408]{1,0:T(8,128)(2,1)S(1)}, bf16[256,1408]{1,0:T(8,128)(2,1)S(1)}, u32[]{:S(2)}, u32[]{:S(2)}) %collective-permute-start.30) | collective-permute-done | bytes 720928 | tf_op jit(solution)/shard_map/ppermute | solution.py:25
  309.0 11.7 %collective-permute-done.20 = bf16[256,1408]{1,0:T(8,128)(2,1)S(1)} collective-permute-done((bf16[256,1408]{1,0:T(8,128)(2,1)S(1)}, bf16[256,1408]{1,0:T(8,128)(2,1)S(1)}, u32[]{:S(2)}, u32[]{:S(2)}) %collective-permute-start.20) | collective-permute-done | bytes 720928 | tf_op jit(solution)/shard_map/ppermute | solution.py:25
  323.1 28.3 %collective-permute-done.21 = bf16[256,1408]{1,0:T(8,128)(2,1)S(1)} collective-permute-done((bf16[256,1408]{1,0:T(8,128)(2,1)S(1)}, bf16[256,1408]{1,0:T(8,128)(2,1)S(1)}, u32[]{:S(2)}, u32[]{:S(2)}) %collective-permute-start.21) | collective-permute-done | bytes 720928 | tf_op jit(solution)/shard_map/ppermute | solution.py:25
  357.2 13.2 %collective-permute-done.36 = bf16[256,1408]{1,0:T(8,128)(2,1)S(1)} collective-permute-done((bf16[256,1408]{1,0:T(8,128)(2,1)S(1)}, bf16[256,1408]{1,0:T(8,128)(2,1)S(1)}, u32[]{:S(2)}, u32[]{:S(2)}) %collective-permute-start.36) | collective-permute-done | bytes 720928 | tf_op jit(solution)/shard_map/ppermute | solution.py:25
  372.3 13.6 %collective-permute-done.37 = bf16[256,1408]{1,0:T(8,128)(2,1)S(1)} collective-permute-done((bf16[256,1408]{1,0:T(8,128)(2,1)S(1)}, bf16[256,1408]{1,0:T(8,128)(2,1)S(1)}, u32[]{:S(2)}, u32[]{:S(2)}) %collective-permute-start.37) | collective-permute-done | bytes 720928 | tf_op jit(solution)/shard_map/ppermute | solution.py:25
  387.7 13.6 %collective-permute-done.38 = bf16[256,1408]{1,0:T(8,128)(2,1)S(1)} collective-permute-done((bf16[256,1408]{1,0:T(8,128)(2,1)S(1)}, bf16[256,1408]{1,0:T(8,128)(2,1)S(1)}, u32[]{:S(2)}, u32[]{:S(2)}) %collective-permute-start.38) | collective-permute-done | bytes 720928 | tf_op jit(solution)/shard_map/ppermute | solution.py:25
  404.7 12.1 %collective-permute-done.31 = bf16[256,1408]{1,0:T(8,128)(2,1)S(1)} collective-permute-done((bf16[256,1408]{1,0:T(8,128)(2,1)S(1)}, bf16[256,1408]{1,0:T(8,128)(2,1)S(1)}, u32[]{:S(2)}, u32[]{:S(2)}) %collective-permute-start.31) | collective-permute-done | bytes 720928 | tf_op jit(solution)/shard_map/ppermute | solution.py:25
  416.9 15.3 %collective-permute-done.23 = bf16[256,1408]{1,0:T(8,128)(2,1)S(1)} collective-permute-done((bf16[256,1408]{1,0:T(8,128)(2,1)S(1)}, bf16[256,1408]{1,0:T(8,128)(2,1)S(1)}, u32[]{:S(2)}, u32[]{:S(2)}) %collective-permute-start.23) | collective-permute-done | bytes 720928 | tf_op jit(solution)/shard_map/ppermute | solution.py:25
  433.1 13.5 %collective-permute-done.39 = bf16[256,1408]{1,0:T(8,128)(2,1)S(1)} collective-permute-done((bf16[256,1408]{1,0:T(8,128)(2,1)S(1)}, bf16[256,1408]{1,0:T(8,128)(2,1)S(1)}, u32[]{:S(2)}, u32[]{:S(2)}) %collective-permute-start.39) | collective-permute-done | bytes 720928 | tf_op jit(solution)/shard_map/ppermute | solution.py:25
  464.7 11.5 %multiply_convert_fusion.1 = (bf16[768,1408]{1,0:T(8,128)(2,1)}, bf16[768,1408]{1,0:T(8,128)(2,1)S(1)}, bf16[768,1408]{1,0:T(8,128)(2,1)}) fusion(f32[768,1408]{1,0:T(8,128)} %fusion.2, f32[768,1408]{1,0:T(8,128)} %fusion.14, bf16[2048,1408]{1,0:T(8,128)(2,1)S(1)} %bitcast.138, bf16[384,2048]{1,0:T(8,128)(2,1)} %collective-permute-done.15, ...), kind=kOutput, calls=%fused_computation.8 | convolution fusion | flops 4451696640 | bytes 24051712 | tf_op jit(solution)/shard_map/dot_general | solution.py:53
  532.9 22.0 %collective-permute-done.87 = bf16[256,1408]{1,0:T(8,128)(2,1)S(1)} collective-permute-done((bf16[256,1408]{1,0:T(8,128)(2,1)}, bf16[256,1408]{1,0:T(8,128)(2,1)S(1)}, u32[]{:S(2)}, u32[]{:S(2)}) %collective-permute-start.87) | collective-permute-done | bytes 720928 | tf_op jit(solution)/shard_map/ppermute | solution.py:25
  556.4 13.9 %collective-permute-done.84 = bf16[256,1408]{1,0:T(8,128)(2,1)S(1)} collective-permute-done((bf16[256,1408]{1,0:T(8,128)(2,1)}, bf16[256,1408]{1,0:T(8,128)(2,1)S(1)}, u32[]{:S(2)}, u32[]{:S(2)}) %collective-permute-start.84) | collective-permute-done | bytes 720928 | tf_op jit(solution)/shard_map/ppermute | solution.py:25
  587.4 13.9 %collective-permute-done.76 = bf16[256,1408]{1,0:T(8,128)(2,1)} collective-permute-done((bf16[256,1408]{1,0:T(8,128)(2,1)S(1)}, bf16[256,1408]{1,0:T(8,128)(2,1)}, u32[]{:S(2)}, u32[]{:S(2)}) %collective-permute-start.76) | collective-permute-done | bytes 720928 | tf_op jit(solution)/shard_map/ppermute | solution.py:25
  604.1 12.6 %collective-permute-done.86 = bf16[256,1408]{1,0:T(8,128)(2,1)S(1)} collective-permute-done((bf16[256,1408]{1,0:T(8,128)(2,1)S(1)}, bf16[256,1408]{1,0:T(8,128)(2,1)S(1)}, u32[]{:S(2)}, u32[]{:S(2)}) %collective-permute-start.86) | collective-permute-done | bytes 720928 | tf_op jit(solution)/shard_map/ppermute | solution.py:25
  618.5 13.6 %collective-permute-done.70 = bf16[256,1408]{1,0:T(8,128)(2,1)S(1)} collective-permute-done((bf16[256,1408]{1,0:T(8,128)(2,1)S(1)}, bf16[256,1408]{1,0:T(8,128)(2,1)S(1)}, u32[]{:S(2)}, u32[]{:S(2)}) %collective-permute-start.70) | collective-permute-done | bytes 720928 | tf_op jit(solution)/shard_map/ppermute | solution.py:25
  634.0 13.6 %collective-permute-done.78 = bf16[256,1408]{1,0:T(8,128)(2,1)S(1)} collective-permute-done((bf16[256,1408]{1,0:T(8,128)(2,1)S(1)}, bf16[256,1408]{1,0:T(8,128)(2,1)S(1)}, u32[]{:S(2)}, u32[]{:S(2)}) %collective-permute-start.78) | collective-permute-done | bytes 720928 | tf_op jit(solution)/shard_map/ppermute | solution.py:25
  651.3 25.3 %collective-permute-done.83 = bf16[256,1408]{1,0:T(8,128)(2,1)S(1)} collective-permute-done((bf16[256,1408]{1,0:T(8,128)(2,1)}, bf16[256,1408]{1,0:T(8,128)(2,1)S(1)}, u32[]{:S(2)}, u32[]{:S(2)}) %collective-permute-start.83) | collective-permute-done | bytes 720928 | tf_op jit(solution)/shard_map/ppermute | solution.py:25
  684.2 38.7 %collective-permute-done.69 = bf16[256,1408]{1,0:T(8,128)(2,1)S(1)} collective-permute-done((bf16[256,1408]{1,0:T(8,128)(2,1)}, bf16[256,1408]{1,0:T(8,128)(2,1)S(1)}, u32[]{:S(2)}, u32[]{:S(2)}) %collective-permute-start.69) | collective-permute-done | bytes 720928 | tf_op jit(solution)/shard_map/ppermute | solution.py:25
  726.5 12.4 %collective-permute-done.77 = bf16[256,1408]{1,0:T(8,128)(2,1)S(1)} collective-permute-done((bf16[256,1408]{1,0:T(8,128)(2,1)S(1)}, bf16[256,1408]{1,0:T(8,128)(2,1)S(1)}, u32[]{:S(2)}, u32[]{:S(2)}) %collective-permute-start.77) | collective-permute-done | bytes 720928 | tf_op jit(solution)/shard_map/ppermute | solution.py:25
  743.4 33.8 %collective-permute-done.44 = bf16[384,2048]{1,0:T(8,128)(2,1)S(1)} collective-permute-done((bf16[384,2048]{1,0:T(8,128)(2,1)S(1)}, bf16[384,2048]{1,0:T(8,128)(2,1)S(1)}, u32[]{:S(2)}, u32[]{:S(2)}) %collective-permute-start.44) | collective-permute-done | bytes 1572896 | tf_op jit(solution)/shard_map/ppermute | solution.py:29
  798.7 21.9 %attend_back.1 = (bf16[2,3,128,512]{3,2,1,0:T(8,128)(2,1)S(1)}, f32[2,3,128,128]{3,2,1,0:T(8,128)S(1)}, bf16[2,3,128,128]{3,2,1,0:T(8,128)(2,1)S(1)}, bf16[2,3,1...) custom-call(s32[1024,1]{1,0:T(8,128)S(1)} %copy.56.kpos_ref, s32[3,2,256]{2,1,0:T(2,128)S(1)} %pad_add_fusion.row_ref, ...), custom_call_target="tpu_custom_call" | custom-call | flops 16106127360 | bytes 3145728 | tf_op jit(solution)/shard_map/attend_back/pallas_call | solution.py:241
  868.4 11.4 %collective-permute-done.65 = bf16[256,512]{1,0:T(8,128)(2,1)S(1)} collective-permute-done((bf16[256,512]{1,0:T(8,128)(2,1)S(1)}, bf16[256,512]{1,0:T(8,128)(2,1)S(1)}, u32[]{:S(2)}, u32[]{:S(2)}) %collective-permute-start.65) | collective-permute-done | bytes 262176 | tf_op jit(solution)/shard_map/ppermute | solution.py:25
  907.1 11.2 %collective-permute-done.50 = bf16[384,2048]{1,0:T(8,128)(2,1)} collective-permute-done((bf16[384,2048]{1,0:T(8,128)(2,1)S(1)}, bf16[384,2048]{1,0:T(8,128)(2,1)}, u32[]{:S(2)}, u32[]{:S(2)}) %collective-permute-start.50) | collective-permute-done | bytes 1572896 | tf_op jit(solution)/shard_map/ppermute | solution.py:29
  926.8 54.3 %reduce-scatter.4.cloned.1.call-done = f32[128,2]{1,0:T(8,128)} async-done(((f32[2048,2]{1,0:T(8,128)}), f32[128,2]{1,0:T(8,128)}) %reduce-scatter.4.cloned.1.call-update) | async-done | bytes 1040
  (463 shorter events, 360.7 us)
Async XLA Ops:
  7.2 973.9 %reduce-scatter.4.cloned.1.call-start = ((), (), s32[]{:S(2)}) async-start(), calls=%async_computation.1 | async-start | bytes 1114112
  7.2 56.2 %collective-permute-start = (s32[3,128]{1,0:T(4,128)}, s32[3,128]{1,0:T(4,128)}, u32[]{:S(2)}, u32[]{:S(2)}) collective-permute-start(s32[3,128]{1,0:T(4,128)} %param.16), channel_id=1, source_target_pairs={{0,2},{2,0},{4,6},{6,4},{8,10},{10,8},{12,14},{14,12},{16,18},{18,... | collective-permute-start | bytes 4616 | tf_op jit(solution)/shard_map/ppermute | solution.py:20
  12.9 57.9 %collective-permute-start.2 = (bf16[128,1152]{1,0:T(8,128)(2,1)}, bf16[128,1152]{1,0:T(8,128)(2,1)}, u32[]{:S(2)}, u32[]{:S(2)}) collective-permute-start(bf16[128,1152]{1,0:T(8,128)(2,1)} %concatenate.125), channel_id=1, source_target_pairs={{0,2},{2,0},{4,6},{6,4},{8,10},{10,8},{12,14},{14,12},{16,18},{18,... | collective-permute-start | bytes 884744 | tf_op jit(solution)/shard_map/ppermute | solution.py:20
  14.2 62.0 %collective-permute-start.32 = (bf16[128,1408]{1,0:T(8,128)(2,1)}, bf16[128,1408]{1,0:T(8,128)(2,1)}, u32[]{:S(2)}, u32[]{:S(2)}) collective-permute-start(bf16[128,1408]{1,0:T(8,128)(2,1)} %get-tuple-element.120), channel_id=1, source_target_pairs={{0,2},{2,0},{4,6},{6,4},{8,10},{10,8},{12,14},{14,12},{16,18},{18,... | collective-permute-start | bytes 1081352 | tf_op jit(solution)/shard_map/ppermute | solution.py:20
  16.6 57.3 %collective-permute-start.16 = (bf16[128,1408]{1,0:T(8,128)(2,1)}, bf16[128,1408]{1,0:T(8,128)(2,1)}, u32[]{:S(2)}, u32[]{:S(2)}) collective-permute-start(bf16[128,1408]{1,0:T(8,128)(2,1)} %get-tuple-element.122), channel_id=1, source_target_pairs={{0,2},{2,0},{4,6},{6,4},{8,10},{10,8},{12,14},{14,12},{16,18},{18,... | collective-permute-start | bytes 1081352 | tf_op jit(solution)/shard_map/ppermute | solution.py:20
  18.7 53.6 %collective-permute-start.24 = (bf16[128,1408]{1,0:T(8,128)(2,1)}, bf16[128,1408]{1,0:T(8,128)(2,1)}, u32[]{:S(2)}, u32[]{:S(2)}) collective-permute-start(bf16[128,1408]{1,0:T(8,128)(2,1)} %get-tuple-element.124), channel_id=1, source_target_pairs={{0,2},{2,0},{4,6},{6,4},{8,10},{10,8},{12,14},{14,12},{16,18},{18,... | collective-permute-start | bytes 1081352 | tf_op jit(solution)/shard_map/ppermute | solution.py:20
  63.4 127.1 %collective-permute-start.1 = (bf16[384,2048]{1,0:T(8,128)(2,1)S(1)}, bf16[384,2048]{1,0:T(8,128)(2,1)}, u32[]{:S(2)}, u32[]{:S(2)}) collective-permute-start(bf16[384,2048]{1,0:T(8,128)(2,1)S(1)} %fusion.5), channel_id=1, source_target_pairs={{0,2},{2,0},{4,6},{6,4},{8,10},{10,8},{12,14},{14,12},{16,18},{18,... | collective-permute-start | bytes 4718600 | tf_op jit(solution)/shard_map/ppermute | solution.py:20
  70.8 375.9 %collective-permute-start.42 = (bf16[384,2048]{1,0:T(8,128)(2,1)}, bf16[384,2048]{1,0:T(8,128)(2,1)}, u32[]{:S(2)}, u32[]{:S(2)}) collective-permute-start(bf16[384,2048]{1,0:T(8,128)(2,1)} %dynamic-slice_dynamic-update-slice_fusion.8), channel_id=1, source_target_pairs={{0,2},{2,0},{4,6},{6,4},{8,10},{10,8},{12,14},{14,12},{16,18},{18,... | collective-permute-start | bytes 4718600 | tf_op jit(solution)/shard_map/ppermute | solution.py:20
  76.2 55.1 %collective-permute-start.25 = (bf16[256,1408]{1,0:T(8,128)(2,1)S(1)}, bf16[256,1408]{1,0:T(8,128)(2,1)S(1)}, u32[]{:S(2)}, u32[]{:S(2)}) collective-permute-start(bf16[256,1408]{1,0:T(8,128)(2,1)S(1)} %get-tuple-element.75), channel_id=1, source_target_pairs={{0,16},{2,18},{4,20},{6,22},{8,24},{10,26},{12,28},{14,30},{16,0},... | collective-permute-start | bytes 2162696 | tf_op jit(solution)/shard_map/ppermute | solution.py:25
  102.2 59.4 %collective-permute-start.17 = (bf16[256,1408]{1,0:T(8,128)(2,1)S(1)}, bf16[256,1408]{1,0:T(8,128)(2,1)S(1)}, u32[]{:S(2)}, u32[]{:S(2)}) collective-permute-start(bf16[256,1408]{1,0:T(8,128)(2,1)S(1)} %get-tuple-element.71), channel_id=1, source_target_pairs={{0,16},{2,18},{4,20},{6,22},{8,24},{10,26},{12,28},{14,30},{16,0},... | collective-permute-start | bytes 2162696 | tf_op jit(solution)/shard_map/ppermute | solution.py:25
  164.7 117.0 %collective-permute-start.28 = (bf16[256,1408]{1,0:T(8,128)(2,1)S(1)}, bf16[256,1408]{1,0:T(8,128)(2,1)}, u32[]{:S(2)}, u32[]{:S(2)}) collective-permute-start(bf16[256,1408]{1,0:T(8,128)(2,1)S(1)} %get-tuple-element.75), channel_id=1, source_target_pairs={{0,4},{2,6},{4,0},{6,2},{8,12},{10,14},{12,8},{14,10},{16,20},{18,... | collective-permute-start | bytes 2162696 | tf_op jit(solution)/shard_map/ppermute | solution.py:25
  305.2 48.9 %collective-permute-start.22 = (bf16[256,1408]{1,0:T(8,128)(2,1)}, bf16[256,1408]{1,0:T(8,128)(2,1)S(1)}, u32[]{:S(2)}, u32[]{:S(2)}) collective-permute-start(bf16[256,1408]{1,0:T(8,128)(2,1)} %collective-permute-done.18), channel_id=1, source_target_pairs={{0,4},{2,6},{4,0},{6,2},{8,12},{10,14},{12,8},{14,10},{16,20},{18,... | collective-permute-start | bytes 2162696 | tf_op jit(solution)/shard_map/ppermute | solution.py:25
  308.4 47.0 %collective-permute-start.35 = (bf16[256,1408]{1,0:T(8,128)(2,1)S(1)}, bf16[256,1408]{1,0:T(8,128)(2,1)S(1)}, u32[]{:S(2)}, u32[]{:S(2)}) collective-permute-start(bf16[256,1408]{1,0:T(8,128)(2,1)S(1)} %collective-permute-done.33), channel_id=1, source_target_pairs={{0,8},{2,10},{4,12},{6,14},{8,0},{10,2},{12,4},{14,6},{16,24},{18,... | collective-permute-start | bytes 2162696 | tf_op jit(solution)/shard_map/ppermute | solution.py:25
  320.7 82.5 %collective-permute-start.14 = (bf16[384,2048]{1,0:T(8,128)(2,1)S(1)}, bf16[384,2048]{1,0:T(8,128)(2,1)S(1)}, u32[]{:S(2)}, u32[]{:S(2)}) collective-permute-start(bf16[384,2048]{1,0:T(8,128)(2,1)S(1)} %add_convert_fusion.5), channel_id=1, source_target_pairs={{0,1},{1,0},{2,3},{3,2},{4,5},{5,4},{6,7},{7,6},{8,9},{9,8},{10,11... | collective-permute-start | bytes 4718600 | tf_op jit(solution)/shard_map/ppermute | solution.py:29
  370.4 46.3 %collective-permute-start.31 = (bf16[256,1408]{1,0:T(8,128)(2,1)S(1)}, bf16[256,1408]{1,0:T(8,128)(2,1)S(1)}, u32[]{:S(2)}, u32[]{:S(2)}) collective-permute-start(bf16[256,1408]{1,0:T(8,128)(2,1)S(1)} %collective-permute-done.27), channel_id=1, source_target_pairs={{0,4},{2,6},{4,0},{6,2},{8,12},{10,14},{12,8},{14,10},{16,20},{18,... | collective-permute-start | bytes 2162696 | tf_op jit(solution)/shard_map/ppermute | solution.py:25
  385.9 46.3 %collective-permute-start.23 = (bf16[256,1408]{1,0:T(8,128)(2,1)S(1)}, bf16[256,1408]{1,0:T(8,128)(2,1)S(1)}, u32[]{:S(2)}, u32[]{:S(2)}) collective-permute-start(bf16[256,1408]{1,0:T(8,128)(2,1)S(1)} %collective-permute-done.19), channel_id=1, source_target_pairs={{0,4},{2,6},{4,0},{6,2},{8,12},{10,14},{12,8},{14,10},{16,20},{18,... | collective-permute-start | bytes 2162696 | tf_op jit(solution)/shard_map/ppermute | solution.py:25
  404.6 53.2 %collective-permute-start.15 = (bf16[384,2048]{1,0:T(8,128)(2,1)S(1)}, bf16[384,2048]{1,0:T(8,128)(2,1)}, u32[]{:S(2)}, u32[]{:S(2)}) collective-permute-start(bf16[384,2048]{1,0:T(8,128)(2,1)S(1)} %multiply_convert_fusion.3), channel_id=1, source_target_pairs={{0,2},{2,0},{4,6},{6,4},{8,10},{10,8},{12,14},{14,12},{16,18},{18,... | collective-permute-start | bytes 4718600 | tf_op jit(solution)/shard_map/ppermute | solution.py:20
  491.2 158.3 %collective-permute-start.40 = (bf16[384,2048]{1,0:T(8,128)(2,1)S(1)}, bf16[384,2048]{1,0:T(8,128)(2,1)S(1)}, u32[]{:S(2)}, u32[]{:S(2)}) collective-permute-start(bf16[384,2048]{1,0:T(8,128)(2,1)S(1)} %slice.415), channel_id=1, source_target_pairs={{0,2},{2,0},{4,6},{6,4},{8,10},{10,8},{12,14},{14,12},{16,18},{18,... | collective-permute-start | bytes 4718600 | tf_op jit(solution)/shard_map/ppermute | solution.py:20
  504.9 70.5 %collective-permute-start.71 = (bf16[256,1408]{1,0:T(8,128)(2,1)S(1)}, bf16[256,1408]{1,0:T(8,128)(2,1)S(1)}, u32[]{:S(2)}, u32[]{:S(2)}) collective-permute-start(bf16[256,1408]{1,0:T(8,128)(2,1)S(1)} %get-tuple-element.97), channel_id=1, source_target_pairs={{0,4},{2,6},{4,0},{6,2},{8,12},{10,14},{12,8},{14,10},{16,20},{18,... | collective-permute-start | bytes 2162696 | tf_op jit(solution)/shard_map/ppermute | solution.py:25
  506.5 69.4 %collective-permute-start.68 = (bf16[256,1408]{1,0:T(8,128)(2,1)S(1)}, bf16[256,1408]{1,0:T(8,128)(2,1)S(1)}, u32[]{:S(2)}, u32[]{:S(2)}) collective-permute-start(bf16[256,1408]{1,0:T(8,128)(2,1)S(1)} %get-tuple-element.99), channel_id=1, source_target_pairs={{0,4},{2,6},{4,0},{6,2},{8,12},{10,14},{12,8},{14,10},{16,20},{18,... | collective-permute-start | bytes 2162696 | tf_op jit(solution)/shard_map/ppermute | solution.py:25
  519.6 50.7 %collective-permute-start.84 = (bf16[256,1408]{1,0:T(8,128)(2,1)}, bf16[256,1408]{1,0:T(8,128)(2,1)S(1)}, u32[]{:S(2)}, u32[]{:S(2)}) collective-permute-start(bf16[256,1408]{1,0:T(8,128)(2,1)} %get-tuple-element.91), channel_id=1, source_target_pairs={{0,4},{2,6},{4,0},{6,2},{8,12},{10,14},{12,8},{14,10},{16,20},{18,... | collective-permute-start | bytes 2162696 | tf_op jit(solution)/shard_map/ppermute | solution.py:25
  632.1 49.4 %collective-permute-start.67 = (bf16[256,1408]{1,0:T(8,128)(2,1)}, bf16[256,1408]{1,0:T(8,128)(2,1)S(1)}, u32[]{:S(2)}, u32[]{:S(2)}) collective-permute-start(bf16[256,1408]{1,0:T(8,128)(2,1)} %get-tuple-element.96), channel_id=1, source_target_pairs={{0,4},{2,6},{4,0},{6,2},{8,12},{10,14},{12,8},{14,10},{16,20},{18,... | collective-permute-start | bytes 2162696 | tf_op jit(solution)/shard_map/ppermute | solution.py:25
  676.6 46.3 %collective-permute-start.69 = (bf16[256,1408]{1,0:T(8,128)(2,1)}, bf16[256,1408]{1,0:T(8,128)(2,1)S(1)}, u32[]{:S(2)}, u32[]{:S(2)}) collective-permute-start(bf16[256,1408]{1,0:T(8,128)(2,1)} %get-tuple-element.85), channel_id=1, source_target_pairs={{0,8},{2,10},{4,12},{6,14},{8,0},{10,2},{12,4},{14,6},{16,24},{18,... | collective-permute-start | bytes 2162696 | tf_op jit(solution)/shard_map/ppermute | solution.py:25
  676.6 47.8 %collective-permute-start.73 = (bf16[256,1408]{1,0:T(8,128)(2,1)S(1)}, bf16[256,1408]{1,0:T(8,128)(2,1)S(1)}, u32[]{:S(2)}, u32[]{:S(2)}) collective-permute-start(bf16[256,1408]{1,0:T(8,128)(2,1)S(1)} %fusion.53), channel_id=1, source_target_pairs={{0,16},{2,18},{4,20},{6,22},{8,24},{10,26},{12,28},{14,30},{16,0},... | collective-permute-start | bytes 2162696 | tf_op jit(solution)/shard_map/ppermute | solution.py:25
  678.4 48.1 %collective-permute-start.75 = (bf16[256,1408]{1,0:T(8,128)(2,1)S(1)}, bf16[256,1408]{1,0:T(8,128)(2,1)S(1)}, u32[]{:S(2)}, u32[]{:S(2)}) collective-permute-start(bf16[256,1408]{1,0:T(8,128)(2,1)S(1)} %copy-done.17), channel_id=1, source_target_pairs={{0,4},{2,6},{4,0},{6,2},{8,12},{10,14},{12,8},{14,10},{16,20},{18,... | collective-permute-start | bytes 2162696 | tf_op jit(solution)/shard_map/ppermute | solution.py:25
  681.2 57.7 %collective-permute-start.77 = (bf16[256,1408]{1,0:T(8,128)(2,1)S(1)}, bf16[256,1408]{1,0:T(8,128)(2,1)S(1)}, u32[]{:S(2)}, u32[]{:S(2)}) collective-permute-start(bf16[256,1408]{1,0:T(8,128)(2,1)S(1)} %copy-done.18), channel_id=1, source_target_pairs={{0,8},{2,10},{4,12},{6,14},{8,0},{10,2},{12,4},{14,6},{16,24},{18,... | collective-permute-start | bytes 2162696 | tf_op jit(solution)/shard_map/ppermute | solution.py:25
  681.5 60.3 %collective-permute-start.81 = (bf16[256,1408]{1,0:T(8,128)(2,1)S(1)}, bf16[256,1408]{1,0:T(8,128)(2,1)S(1)}, u32[]{:S(2)}, u32[]{:S(2)}) collective-permute-start(bf16[256,1408]{1,0:T(8,128)(2,1)S(1)} %fusion.47), channel_id=1, source_target_pairs={{0,16},{2,18},{4,20},{6,22},{8,24},{10,26},{12,28},{14,30},{16,0},... | collective-permute-start | bytes 2162696 | tf_op jit(solution)/shard_map/ppermute | solution.py:25
  722.9 55.5 %collective-permute-start.41 = (bf16[384,2048]{1,0:T(8,128)(2,1)S(1)}, bf16[384,2048]{1,0:T(8,128)(2,1)S(1)}, u32[]{:S(2)}, u32[]{:S(2)}) collective-permute-start(bf16[384,2048]{1,0:T(8,128)(2,1)S(1)} %add_convert_fusion.4), channel_id=1, source_target_pairs={{0,1},{1,0},{2,3},{3,2},{4,5},{5,4},{6,7},{7,6},{8,9},{9,8},{10,11... | collective-permute-start | bytes 4718600 | tf_op jit(solution)/shard_map/ppermute | solution.py:29
  724.4 52.9 %collective-permute-start.44 = (bf16[384,2048]{1,0:T(8,128)(2,1)S(1)}, bf16[384,2048]{1,0:T(8,128)(2,1)S(1)}, u32[]{:S(2)}, u32[]{:S(2)}) collective-permute-start(bf16[384,2048]{1,0:T(8,128)(2,1)S(1)} %add_convert_fusion.2), channel_id=1, source_target_pairs={{0,1},{1,0},{2,3},{3,2},{4,5},{5,4},{6,7},{7,6},{8,9},{9,8},{10,11... | collective-permute-start | bytes 4718600 | tf_op jit(solution)/shard_map/ppermute | solution.py:29
  726.5 57.6 %collective-permute-start.90 = (f32[128,1408]{1,0:T(8,128)S(1)}, f32[128,1408]{1,0:T(8,128)S(1)}, u32[]{:S(2)}, u32[]{:S(2)}) collective-permute-start(f32[128,1408]{1,0:T(8,128)S(1)} %get-tuple-element.105), channel_id=1, source_target_pairs={{0,2},{2,0},{4,6},{6,4},{8,10},{10,8},{12,14},{14,12},{16,18},{18,... | collective-permute-start | bytes 2162696 | tf_op jit(solution)/shard_map/ppermute | solution.py:20
  739.0 49.3 %collective-permute-start.74 = (f32[128,1408]{1,0:T(8,128)}, f32[128,1408]{1,0:T(8,128)}, u32[]{:S(2)}, u32[]{:S(2)}) collective-permute-start(f32[128,1408]{1,0:T(8,128)} %get-tuple-element.109), channel_id=1, source_target_pairs={{0,2},{2,0},{4,6},{6,4},{8,10},{10,8},{12,14},{14,12},{16,18},{18,... | collective-permute-start | bytes 2162696 | tf_op jit(solution)/shard_map/ppermute | solution.py:20
  743.4 47.9 %collective-permute-start.82 = (f32[128,1408]{1,0:T(8,128)}, f32[128,1408]{1,0:T(8,128)}, u32[]{:S(2)}, u32[]{:S(2)}) collective-permute-start(f32[128,1408]{1,0:T(8,128)} %get-tuple-element.107), channel_id=1, source_target_pairs={{0,2},{2,0},{4,6},{6,4},{8,10},{10,8},{12,14},{14,12},{16,18},{18,... | collective-permute-start | bytes 2162696 | tf_op jit(solution)/shard_map/ppermute | solution.py:20
  (114 other events, 2723.6 us)
Sparse Core Ops, SparseCore 0:
  923.1 57.9 reduce-scatter.3

commit v2 on v1

--- a/solution.py
+++ b/solution.py
@@ -47,6 +47,190 @@
                 kept[key ^ bit] = came
         held = {key: held[key].astype(F32) + came.astype(F32) for key, came in kept.items()}
     return held[0]
+
+
+def flipped(index, distance):
+    return index + distance * (1 - 2 * ((index // distance) % 2))
+
+
+def peer(distance=0, core=False, tensor=False):
+    place = lax.axis_index("dp")
+    bit = 1
+    while bit <= distance:
+        if distance & bit:
+            place = flipped(place, 2 * bit)
+        bit *= 2
+    if core:
+        place = flipped(place, 1)
+    half = lax.axis_index("tensor")
+    if tensor:
+        half = 1 - half
+    return (place, half)
+
+
+def greet(peers):
+    barrier = pltpu.get_barrier_semaphore()
+    for device in peers:
+        pl.semaphore_signal(barrier, inc=1, device_id=device, device_id_type=pl.DeviceIdType.MESH)
+    pl.semaphore_wait(barrier, len(peers))
+
+
+def remote(src, dst, send, recv, device):
+    return pltpu.make_async_remote_copy(
+        src_ref=src,
+        dst_ref=dst,
+        send_sem=send,
+        recv_sem=recv,
+        device_id=device,
+        device_id_type=pl.DeviceIdType.MESH,
+    )
+
+
+def cuts(cols, parts):
+    tiles = cols // 128
+    edges = [tiles * part // parts * 128 for part in range(parts + 1)]
+    return [(edges[i], edges[i + 1] - edges[i]) for i in range(parts)]
+
+
+class Spread:
+    def __init__(self, src, dst, rows, start, cols, order, places, sems):
+        self.src, self.dst, self.rows = src, dst, rows
+        self.start, self.cols = start, cols
+        self.order, self.places = order, places
+        self.sems = sems
+        self.copies = []
+        self.count = 0
+        self.core = lax.axis_index("dp") % 2
+
+    def sem(self):
+        self.count += 1
+        return self.sems[0].at[self.count - 1], self.sems[1].at[self.count - 1]
+
+    def begin(self):
+        half = self.rows // 2
+        width = self.dst.shape[1]
+        if self.src.shape[1] == width:
+            own = other = self.src
+        else:
+            span = pl.ds(pl.multiple_of(self.core * width + self.start, 128), self.cols)
+            own = self.src.at[:, span]
+            span = pl.ds(pl.multiple_of((1 - self.core) * width + self.start, 128), self.cols)
+            other = self.src.at[:, span]
+        mine = self.dst.at[
+            pl.ds(pl.multiple_of(self.core * half, half), half), pl.ds(self.start, self.cols)
+        ]
+        send, recv = self.sem()
+        self.local = pltpu.make_async_copy(own, mine, self.sems[2])
+        self.local.start()
+        copy = remote(other, mine, send, recv, peer(core=True))
+        copy.start()
+        self.stage = [copy]
+        self.copies.append(copy)
+        self.held = [0]
+        self.level = 0
+
+    def wait(self):
+        for copy in self.stage:
+            copy.wait_recv()
+        if self.level == 0:
+            self.local.wait()
+
+    def block(self, key):
+        return self.dst.at[
+            pl.ds(self.places[key] * self.rows, self.rows), pl.ds(self.start, self.cols)
+        ]
+
+    def step(self):
+        self.wait()
+        if self.level == len(self.order):
+            return False
+        bit = self.order[self.level]
+        self.stage = []
+        for key in self.held:
+            send, recv = self.sem()
+            copy = remote(self.block(key), self.block(key | bit), send, recv, peer(bit))
+            copy.start()
+            self.stage.append(copy)
+            self.copies.append(copy)
+        self.held = self.held + [key | bit for key in self.held]
+        self.level += 1
+        return True
+
+    def close(self):
+        for copy in self.copies:
+            copy.wait_send()
+
+
+def gather_kernel(order, places, pieces, *refs):
+    chips = len(places)
+    n = len(pieces)
+    srcs, (hid_src, cot_src) = refs[:n], refs[n : n + 2]
+    dsts, (hid_dst, cot_dst) = refs[n + 2 : 2 * n + 2], refs[2 * n + 2 : 2 * n + 4]
+    send, recv, local, side = refs[2 * n + 4 :]
+    bits = [1 << place for place in range(chips.bit_length() - 1)]
+    greet([peer(core=True)] + [peer(bit) for bit in bits])
+
+    spreads = []
+    for src, dst, (parts, rows, way) in zip(srcs, dsts, pieces):
+        for start, cols in cuts(dst.shape[1], parts):
+            at = len(spreads)
+            spreads.append(
+                Spread(
+                    src, dst, rows, start, cols, way, places,
+                    (send.at[at], recv.at[at], local.at[at]),
+                )
+            )
+    count = hid_src.shape[0]
+    extra = []
+    for at, (src, dst) in enumerate(((hid_src, hid_dst), (cot_src, cot_dst))):
+        own = pltpu.make_async_copy(src, dst.at[pl.ds(0, count)], side.at[3 * at])
+        own.start()
+        other = remote(
+            src, dst.at[pl.ds(count, count)], side.at[3 * at + 1], side.at[3 * at + 2],
+            peer(core=True),
+        )
+        other.start()
+        extra += [own, other]
+    for spread in spreads:
+        spread.begin()
+    levels = len(order)
+    for tick in range(len(spreads) + levels):
+        for level in range(levels + 1):
+            if 0 <= tick - level < len(spreads):
+                spreads[tick - level].step()
+    for spread in spreads:
+        spread.close()
+    for copy in extra:
+        copy.wait()
+
+
+def gather_all(chips, order, places, sources, parts, ways, hidden, cotangent):
+    pieces = []
+    shapes = []
+    for source, part, way in zip(sources, parts, ways):
+        same = source.shape[1] == 128
+        rows = 2 * source.shape[0]
+        cols = source.shape[1] if same else source.shape[1] // 2
+        pieces.append((part, rows, way))
+        shapes.append(jax.ShapeDtypeStruct((rows * chips, cols), source.dtype))
+    count, width = hidden.shape
+    shapes += [jax.ShapeDtypeStruct((2 * count, width), BF)] * 2
+    total = sum(parts)
+    any_spec = pl.BlockSpec(memory_space=pl.ANY)
+    return pl.pallas_call(
+        functools.partial(gather_kernel, order, places, pieces),
+        in_specs=[any_spec] * (len(sources) + 2),
+        out_specs=[any_spec] * len(shapes),
+        out_shape=shapes,
+        scratch_shapes=[
+            pltpu.SemaphoreType.DMA((total, chips)),
+            pltpu.SemaphoreType.DMA((total, chips)),
+            pltpu.SemaphoreType.DMA((total,)),
+            pltpu.SemaphoreType.DMA((6,)),
+        ],
+        compiler_params=pltpu.CompilerParams(collective_id=0, has_side_effects=True),
+        name="gather",
+    )(*sources, hidden, cotangent)
 
 
 def dot_plain(left, right):
@@ -340,33 +524,45 @@
             jnp.concatenate([came, mine], axis=0),
         )
 
-    attn_parts = [split_core(w) for w in (w_query, w_key, w_value, w_out.T)]
-    attn_mine = jnp.concatenate([p[0] for p in attn_parts], axis=1)
-    attn_other = jnp.concatenate([p[1] for p in attn_parts], axis=1)
-    attn_own = joined_core(attn_mine, swap_core(attn_other))
-    gate_parts = split_core(w_gate)
-    gate_own = joined_core(gate_parts[0], swap_core(gate_parts[1]))
-    up_parts = split_core(w_up)
-    up_own = joined_core(up_parts[0], swap_core(up_parts[1]))
-    down_parts = split_core(w_down.T)
-    down_own = joined_core(down_parts[0], swap_core(down_parts[1]))
-
-    def whole(own, order):
-        held = gather_blocks(own, order)
-        return jnp.concatenate([held[key] for key in keys_order], axis=0)
-
-    gains = jnp.stack([attn_gain, ffn_gain])
-    gains = lax.all_gather(gains, "dp", axis=1, tiled=True).astype(F32)
-    gains = rearranged(gains)
-    gain_one, gain_two = gains[0:1], gains[1:2]
-
+    def interleaved(arrays):
+        return jnp.concatenate(
+            [
+                w[:, side * (w.shape[1] // 2) : (side + 1) * (w.shape[1] // 2)]
+                for side in range(2)
+                for w in arrays
+            ],
+            axis=1,
+        )
+
+    attn_pack = interleaved((w_query, w_key, w_value, w_out.T))
+    own_block = block // 2
+    gain_pack = jnp.zeros((16, 128), BF).at[0, :own_block].set(attn_gain)
+    gain_pack = gain_pack.at[1, :own_block].set(ffn_gain)
     hidden = rearranged(tokens.reshape(count, width))
     grad_final = rearranged(cotangent.reshape(count, width))
+    places = {key: place for place, key in enumerate(keys_order)}
+    early = [bits[0]] + late_first[:-1]
+    gains_all, attn_w, gate_w, up_w, down_wt, hidden_both, grad_final_both = gather_all(
+        chips,
+        late_first,
+        places,
+        (gain_pack, attn_pack, w_gate, w_up, w_down.T),
+        (1, 2, 2, 2, 2),
+        (early, early, late_first, late_first, late_first),
+        hidden,
+        grad_final,
+    )
+    gains = gains_all.reshape(chips, 2, 16, 128)[:, :, :2, :own_block]
+    gains = gains.transpose(2, 0, 1, 3).reshape(2, width).astype(F32)
+    gain_one, gain_two = gains[0:1], gains[1:2]
+
+    hidden_both_f = hidden_both.astype(F32)
+    ratio_both = lax.rsqrt(
+        jnp.mean(hidden_both_f * hidden_both_f, axis=-1, keepdims=True) + epsilon
+    )
+    normed = (hidden_both_f * ratio_both * gain_one).astype(BF)
     hidden_f = hidden.astype(F32)
-    ratio_one = lax.rsqrt(jnp.mean(hidden_f * hidden_f, axis=-1, keepdims=True) + epsilon)
-    normed_own = (hidden_f * ratio_one * gain_one).astype(BF)
-    normed = jnp.concatenate([normed_own, swap_core(normed_own)], axis=0)
-    grad_final_both = jnp.concatenate([grad_final, swap_core(grad_final)], axis=0)
+    ratio_one = ratio_both[:count]
     position_both = jnp.stack([doc_position, swap_core(doc_position)])
 
     power = jnp.arange(HEAD_DIM // 2, dtype=F32) * (2.0 / HEAD_DIM)
@@ -383,7 +579,6 @@
     row_places = jnp.broadcast_to(row_place[None, :], row_position.shape)
     rowinfo = jnp.stack([row_places, row_places - row_position], axis=1)
 
-    attn_w = whole(attn_own, late_first)
     n_q = w_query.shape[1] // 2
     n_kv = w_key.shape[1] // 2
     qkv_w = attn_w[:, : n_q + 2 * n_kv]
@@ -408,9 +603,6 @@
     normed_two_own = (middle * ratio_two * gain_two).astype(BF)
     normed_two = jnp.concatenate([normed_two_own, swap_core(normed_two_own)], axis=0)
 
-    gate_w = whole(gate_own, late_first)
-    up_w = whole(up_own, late_first)
-    down_wt = whole(down_own, late_first)
     gate = dot_plain(normed_two, gate_w)
     upward = dot_plain(normed_two, up_w)
     sigmoid = jax.nn.sigmoid(gate)

time: 999 us -> 1120 us (1.12)
  Pallas kernels: 44.9 us -> 465 us
  waiting for transfers between devices: 611 us -> 378 us
  blocking collectives: 22.6 us -> 0 us
  starting transfers between devices: 79.1 us -> 56.5 us
  other arithmetic: 66.3 us -> 45.7 us
    pallas_call x0 -> x1, Pallas kernels: none -> 421 us  [gather_all(): pl.pallas_call(functools.partial(gather_kernel, order, places, pieces), i...]
    ppermute x69 -> x41, waiting for transfers between devices: 511 us -> 235 us  [swap_chip(): lax.ppermute(block, 'dp', [(i, i ^ 2 * distance) for i in range(size)])]
    ppermute x4, waiting for transfers between devices: 45 us -> 83 us  [swap_tensor(): return lax.ppermute(block, 'tensor', [(0, 1), (1, 0)])]
    all_gather x1 -> x0, blocking collectives: 22.6 us -> none  [body(): gains = lax.all_gather(gains, 'dp', axis=1, tiled=True).astype(F32)]
    ppermute x69 -> x41, starting transfers between devices: 71.4 us -> 49.4 us  [swap_chip(): lax.ppermute(block, 'dp', [(i, i ^ 2 * distance) for i in range(size)])]
    unnamed x173 -> x134, local copies, waits for them, and re-layouts: 36.5 us -> 29.9 us
  transfers between devices with their start and end apart: 92 -> 58, of which waited for: 46 -> 35; matrix products, arithmetic and copies ran while one was open for 17% -> 10% of each run, Pallas kernels for 2% -> 38%
where the time goes in v2:
time: 1120 us; the launch traced here: 1110 us
  Pallas kernels  465 us (42%)
  waiting for transfers between devices  378 us (34%)
  matrix products  95.3 us (9%)
  starting transfers between devices  56.5 us (5%)
  local copies, waits for them, and re-layouts  46.6 us (4%)
  other arithmetic  45.7 us (4%)
  between operations  21 us (2%)
    pallas_call x1, Pallas kernels, gather_all(): pl.pallas_call(functools.partial(gather_kernel, order, places, pieces), i...  421 us
    ppermute x41, waiting for transfers between devices, swap_chip(): lax.ppermute(block, 'dp', [(i, i ^ 2 * distance) for i in range(size)])  235 us
    ppermute x4, waiting for transfers between devices, swap_tensor(): return lax.ppermute(block, 'tensor', [(0, 1), (1, 0)])  83 us
    unnamed x2, waiting for transfers between devices  55.9 us
    ppermute x41, starting transfers between devices, swap_chip(): lax.ppermute(block, 'dp', [(i, i ^ 2 * distance) for i in range(size)])  49.4 us
    dot_general x4, matrix products, dot_plain(): return jnp.dot(left, right, preferred_element_type=F32)  36.8 us
    dot_general x10, matrix products, dot_first(): lax.dot_general(left, right, (((0,), (0,)), ((), ())), preferred_element_...  31.1 us
    unnamed x134, local copies, waits for them, and re-layouts  29.9 us
  transfers between devices with their start and end apart: 58, of which 35 were waited for; matrix products, arithmetic and copies ran while one was open for 10% of the time, Pallas kernels for 38%

profile of v2, /device:TPU:0, one launch (start us, length us, event | category | flops | bytes accessed | tf_op | source)
XLA Modules:
  0.0 1108.8 jit_solution(10221804142635476742)
XLA Ops:
  30.6 421.2 %gather.1 = (bf16[256,128]{1,0:T(8,128)(2,1)}, bf16[2048,1152]{1,0:T(8,128)(2,1)}, bf16[2048,1408]{1,0:T(8,128)(2,1)}, bf16[2048,1408]{1,0:T(8,128)(2,1)}, bf16[...) custom-call(bf16[16,128]{1,0:T(8,128)(2,1)} %copy-done.29, ...), custom_call_target="tpu_custom_call" | custom-call | tf_op jit(solution)/shard_map/gather/pallas_call | solution.py:220
  475.9 17.3 %attend.1 = (bf16[2,3,128,512]{3,2,1,0:T(8,128)(2,1)S(1)}, f32[3,8,256]{2,1,0:T(8,128)S(1)}) custom-call(s32[1024,1]{1,0:T(8,128)S(1)} %copy.49.kpos_ref, s32[3,2,256]{2,1,0:T(2,128)S(1)} %pad_add_fusion.row_ref, bf16[2,3,128,512]{3,2,1,0:T(8,128)(2,1)S(1)} %bitcast.87, bf16[2,3,128,128]{3,2,1,0:T(8,128)(2,1)S(1)} %bitcast.73, ...), custom_call_target="tpu_custom_call" | custom-call | flops 6442450944 | bytes 1572864 | tf_op jit(solution)/shard_map/attend/pallas_call | solution.py:351
  502.8 34.9 %collective-permute-done.5 = bf16[384,2048]{1,0:T(8,128)(2,1)S(1)} collective-permute-done((bf16[384,2048]{1,0:T(8,128)(2,1)S(1)}, bf16[384,2048]{1,0:T(8,128)(2,1)S(1)}, u32[]{:S(2)}, u32[]{:S(2)}) %collective-permute-start.5) | collective-permute-done | bytes 1572896 | tf_op jit(solution)/shard_map/ppermute | solution.py:29
  547.4 9.8 fusion.113
  558.6 10.8 fusion.13
  569.4 11.8 %multiply_convert_fusion = (bf16[768,1408]{1,0:T(8,128)(2,1)}, bf16[768,1408]{1,0:T(8,128)(2,1)}, bf16[768,1408]{1,0:T(8,128)(2,1)S(1)}) fusion(f32[768,1408]{1,0:T(8,128)} %fusion.113, f32[768,1408]{1,0:T(8,128)} %fusion.13, bf16[2048,1408]{1,0:T(8,128)(2,1)S(1)} %bitcast.151, bf16[384,2048]{1,0:T(8,128)(2,1)} %collective-permute-done.6, ...), kind=kOutput, calls=%fused_computation.10 | convolution fusion | flops 4451696640 | bytes 24051712 | tf_op jit(solution)/shard_map/dot_general | solution.py:237
  581.3 5.3 convolution_convert_fusion.5
  594.0 6.9 fusion.114
  601.0 8.3 add_convert_fusion
  636.5 14.3 %collective-permute-done.37 = bf16[256,1408]{1,0:T(8,128)(2,1)} collective-permute-done((bf16[256,1408]{1,0:T(8,128)(2,1)S(1)}, bf16[256,1408]{1,0:T(8,128)(2,1)}, u32[]{:S(2)}, u32[]{:S(2)}) %collective-permute-start.37) | collective-permute-done | bytes 720928 | tf_op jit(solution)/shard_map/ppermute | solution.py:25
  653.5 12.6 %collective-permute-done.42 = bf16[256,1408]{1,0:T(8,128)(2,1)S(1)} collective-permute-done((bf16[256,1408]{1,0:T(8,128)(2,1)}, bf16[256,1408]{1,0:T(8,128)(2,1)S(1)}, u32[]{:S(2)}, u32[]{:S(2)}) %collective-permute-start.42) | collective-permute-done | bytes 720928 | tf_op jit(solution)/shard_map/ppermute | solution.py:25
  667.4 14.1 %collective-permute-done.45 = bf16[256,1408]{1,0:T(8,128)(2,1)S(1)} collective-permute-done((bf16[256,1408]{1,0:T(8,128)(2,1)S(1)}, bf16[256,1408]{1,0:T(8,128)(2,1)S(1)}, u32[]{:S(2)}, u32[]{:S(2)}) %collective-permute-start.45) | collective-permute-done | bytes 720928 | tf_op jit(solution)/shard_map/ppermute | solution.py:25
  684.5 12.5 %collective-permute-done.50 = bf16[256,1408]{1,0:T(8,128)(2,1)S(1)} collective-permute-done((bf16[256,1408]{1,0:T(8,128)(2,1)}, bf16[256,1408]{1,0:T(8,128)(2,1)S(1)}, u32[]{:S(2)}, u32[]{:S(2)}) %collective-permute-start.50) | collective-permute-done | bytes 720928 | tf_op jit(solution)/shard_map/ppermute | solution.py:25
  698.3 14.1 %collective-permute-done.53 = bf16[256,1408]{1,0:T(8,128)(2,1)S(1)} collective-permute-done((bf16[256,1408]{1,0:T(8,128)(2,1)S(1)}, bf16[256,1408]{1,0:T(8,128)(2,1)S(1)}, u32[]{:S(2)}, u32[]{:S(2)}) %collective-permute-start.53) | collective-permute-done | bytes 720928 | tf_op jit(solution)/shard_map/ppermute | solution.py:25
  716.4 11.5 %collective-permute-done.36 = bf16[256,1408]{1,0:T(8,128)(2,1)S(1)} collective-permute-done((bf16[256,1408]{1,0:T(8,128)(2,1)S(1)}, bf16[256,1408]{1,0:T(8,128)(2,1)S(1)}, u32[]{:S(2)}, u32[]{:S(2)}) %collective-permute-start.36) | collective-permute-done | bytes 720928 | tf_op jit(solution)/shard_map/ppermute | solution.py:25
  729.5 13.8 %collective-permute-done.44 = bf16[256,1408]{1,0:T(8,128)(2,1)S(1)} collective-permute-done((bf16[256,1408]{1,0:T(8,128)(2,1)S(1)}, bf16[256,1408]{1,0:T(8,128)(2,1)S(1)}, u32[]{:S(2)}, u32[]{:S(2)}) %collective-permute-start.44) | collective-permute-done | bytes 720928 | tf_op jit(solution)/shard_map/ppermute | solution.py:25
  744.9 13.9 %collective-permute-done.52 = bf16[256,1408]{1,0:T(8,128)(2,1)S(1)} collective-permute-done((bf16[256,1408]{1,0:T(8,128)(2,1)S(1)}, bf16[256,1408]{1,0:T(8,128)(2,1)S(1)}, u32[]{:S(2)}, u32[]{:S(2)}) %collective-permute-start.52) | collective-permute-done | bytes 720928 | tf_op jit(solution)/shard_map/ppermute | solution.py:25
  764.7 9.5 collective-permute-done.33
  779.6 16.8 %collective-permute-done.35 = bf16[256,1408]{1,0:T(8,128)(2,1)S(1)} collective-permute-done((bf16[256,1408]{1,0:T(8,128)(2,1)S(1)}, bf16[256,1408]{1,0:T(8,128)(2,1)S(1)}, u32[]{:S(2)}, u32[]{:S(2)}) %collective-permute-start.35) | collective-permute-done | bytes 720928 | tf_op jit(solution)/shard_map/ppermute | solution.py:25
  797.7 12.7 %collective-permute-start.55 = (bf16[256,1408]{1,0:T(8,128)(2,1)S(1)}, bf16[256,1408]{1,0:T(8,128)(2,1)S(1)}, u32[]{:S(2)}, u32[]{:S(2)}) collective-permute-start(bf16[256,1408]{1,0:T(8,128)(2,1)S(1)} %fusion.36), channel_id=1, source_target_pairs={{0,16},{2,18},{4,20},{6,22},{8,24},{10,26},{12,28},{14,30},{16,0},... | collective-permute-start | bytes 2162696 | tf_op jit(solution)/shard_map/ppermute | solution.py:25
  810.4 16.8 %collective-permute-done.43 = bf16[256,1408]{1,0:T(8,128)(2,1)S(1)} collective-permute-done((bf16[256,1408]{1,0:T(8,128)(2,1)S(1)}, bf16[256,1408]{1,0:T(8,128)(2,1)S(1)}, u32[]{:S(2)}, u32[]{:S(2)}) %collective-permute-start.43) | collective-permute-done | bytes 720928 | tf_op jit(solution)/shard_map/ppermute | solution.py:25
  831.7 22.7 %collective-permute-done.51 = bf16[256,1408]{1,0:T(8,128)(2,1)S(1)} collective-permute-done((bf16[256,1408]{1,0:T(8,128)(2,1)S(1)}, bf16[256,1408]{1,0:T(8,128)(2,1)S(1)}, u32[]{:S(2)}, u32[]{:S(2)}) %collective-permute-start.51) | collective-permute-done | bytes 720928 | tf_op jit(solution)/shard_map/ppermute | solution.py:25
  855.5 9.1 collective-permute-done.10
  865.7 26.1 %collective-permute-done.8 = bf16[384,2048]{1,0:T(8,128)(2,1)S(1)} collective-permute-done((bf16[384,2048]{1,0:T(8,128)(2,1)S(1)}, bf16[384,2048]{1,0:T(8,128)(2,1)S(1)}, u32[]{:S(2)}, u32[]{:S(2)}) %collective-permute-start.8) | collective-permute-done | bytes 1572896 | tf_op jit(solution)/shard_map/ppermute | solution.py:29
  910.5 22.1 %attend_back.1 = (bf16[2,3,128,512]{3,2,1,0:T(8,128)(2,1)S(1)}, f32[2,3,128,128]{3,2,1,0:T(8,128)S(1)}, bf16[2,3,128,128]{3,2,1,0:T(8,128)(2,1)S(1)}, bf16[2,3,1...) custom-call(s32[1024,1]{1,0:T(8,128)S(1)} %copy.49.kpos_ref, s32[3,2,256]{2,1,0:T(2,128)S(1)} %pad_add_fusion.row_ref, ...), custom_call_target="tpu_custom_call" | custom-call | flops 16106127360 | bytes 3145728 | tf_op jit(solution)/shard_map/attend_back/pallas_call | solution.py:425
  969.0 7.0 collective-permute-done.21
  976.2 5.4 collective-permute-done.25
  982.6 7.2 collective-permute-done.31
  989.9 6.8 collective-permute-done.22
  1003.6 9.4 collective-permute-done.23
  1020.7 12.8 %collective-permute-done.16 = bf16[384,2048]{1,0:T(8,128)(2,1)} collective-permute-done((bf16[384,2048]{1,0:T(8,128)(2,1)S(1)}, bf16[384,2048]{1,0:T(8,128)(2,1)}, u32[]{:S(2)}, u32[]{:S(2)}) %collective-permute-start.16) | collective-permute-done | bytes 1572896 | tf_op jit(solution)/shard_map/ppermute | solution.py:29
  1043.5 55.8 %reduce-scatter.4.cloned.1.call-done = f32[128,2]{1,0:T(8,128)} async-done(((f32[2048,2]{1,0:T(8,128)}), f32[128,2]{1,0:T(8,128)}) %reduce-scatter.4.cloned.1.call-update) | async-done | bytes 1040
  (344 shorter events, 214.3 us)
Async XLA Ops:
  7.2 1092.2 %reduce-scatter.4.cloned.1.call-start = ((), (), s32[]{:S(2)}) async-start(), calls=%async_computation.1 | async-start | bytes 1114112
  7.2 453.0 %collective-permute-start = (s32[3,128]{1,0:T(4,128)}, s32[3,128]{1,0:T(4,128)S(1)}, u32[]{:S(2)}, u32[]{:S(2)}) collective-permute-start(s32[3,128]{1,0:T(4,128)} %param.20), channel_id=1, source_target_pairs={{0,2},{2,0},{4,6},{6,4},{8,10},{10,8},{12,14},{14,12},{16,18},{18,... | collective-permute-start | bytes 4616 | tf_op jit(solution)/shard_map/ppermute | solution.py:20
  501.2 36.5 %collective-permute-start.5 = (bf16[384,2048]{1,0:T(8,128)(2,1)S(1)}, bf16[384,2048]{1,0:T(8,128)(2,1)S(1)}, u32[]{:S(2)}, u32[]{:S(2)}) collective-permute-start(bf16[384,2048]{1,0:T(8,128)(2,1)S(1)} %add_convert_fusion.5), channel_id=1, source_target_pairs={{0,1},{1,0},{2,3},{3,2},{4,5},{5,4},{6,7},{7,6},{8,9},{9,8},{10,11... | collective-permute-start | bytes 4718600 | tf_op jit(solution)/shard_map/ppermute | solution.py:29
  609.5 151.0 %collective-permute-start.9 = (bf16[384,2048]{1,0:T(8,128)(2,1)S(1)}, bf16[384,2048]{1,0:T(8,128)(2,1)S(1)}, u32[]{:S(2)}, u32[]{:S(2)}) collective-permute-start(bf16[384,2048]{1,0:T(8,128)(2,1)S(1)} %slice.433), channel_id=1, source_target_pairs={{0,2},{2,0},{4,6},{6,4},{8,10},{10,8},{12,14},{14,12},{16,18},{18,... | collective-permute-start | bytes 4718600 | tf_op jit(solution)/shard_map/ppermute | solution.py:20
  617.3 33.4 %collective-permute-start.37 = (bf16[256,1408]{1,0:T(8,128)(2,1)S(1)}, bf16[256,1408]{1,0:T(8,128)(2,1)}, u32[]{:S(2)}, u32[]{:S(2)}) collective-permute-start(bf16[256,1408]{1,0:T(8,128)(2,1)S(1)} %get-tuple-element.127), channel_id=1, source_target_pairs={{0,4},{2,6},{4,0},{6,2},{8,12},{10,14},{12,8},{14,10},{16,20},{18,... | collective-permute-start | bytes 2162696 | tf_op jit(solution)/shard_map/ppermute | solution.py:25
  623.2 42.9 %collective-permute-start.42 = (bf16[256,1408]{1,0:T(8,128)(2,1)}, bf16[256,1408]{1,0:T(8,128)(2,1)S(1)}, u32[]{:S(2)}, u32[]{:S(2)}) collective-permute-start(bf16[256,1408]{1,0:T(8,128)(2,1)} %get-tuple-element.125), channel_id=1, source_target_pairs={{0,4},{2,6},{4,0},{6,2},{8,12},{10,14},{12,8},{14,10},{16,20},{18,... | collective-permute-start | bytes 2162696 | tf_op jit(solution)/shard_map/ppermute | solution.py:25
  624.6 57.0 %collective-permute-start.45 = (bf16[256,1408]{1,0:T(8,128)(2,1)S(1)}, bf16[256,1408]{1,0:T(8,128)(2,1)S(1)}, u32[]{:S(2)}, u32[]{:S(2)}) collective-permute-start(bf16[256,1408]{1,0:T(8,128)(2,1)S(1)} %get-tuple-element.123), channel_id=1, source_target_pairs={{0,4},{2,6},{4,0},{6,2},{8,12},{10,14},{12,8},{14,10},{16,20},{18,... | collective-permute-start | bytes 2162696 | tf_op jit(solution)/shard_map/ppermute | solution.py:25
  635.2 61.8 %collective-permute-start.50 = (bf16[256,1408]{1,0:T(8,128)(2,1)}, bf16[256,1408]{1,0:T(8,128)(2,1)S(1)}, u32[]{:S(2)}, u32[]{:S(2)}) collective-permute-start(bf16[256,1408]{1,0:T(8,128)(2,1)} %get-tuple-element.121), channel_id=1, source_target_pairs={{0,4},{2,6},{4,0},{6,2},{8,12},{10,14},{12,8},{14,10},{16,20},{18,... | collective-permute-start | bytes 2162696 | tf_op jit(solution)/shard_map/ppermute | solution.py:25
  650.7 61.7 %collective-permute-start.53 = (bf16[256,1408]{1,0:T(8,128)(2,1)S(1)}, bf16[256,1408]{1,0:T(8,128)(2,1)S(1)}, u32[]{:S(2)}, u32[]{:S(2)}) collective-permute-start(bf16[256,1408]{1,0:T(8,128)(2,1)S(1)} %get-tuple-element.119), channel_id=1, source_target_pairs={{0,4},{2,6},{4,0},{6,2},{8,12},{10,14},{12,8},{14,10},{16,20},{18,... | collective-permute-start | bytes 2162696 | tf_op jit(solution)/shard_map/ppermute | solution.py:25
  666.1 61.8 %collective-permute-start.36 = (bf16[256,1408]{1,0:T(8,128)(2,1)S(1)}, bf16[256,1408]{1,0:T(8,128)(2,1)S(1)}, u32[]{:S(2)}, u32[]{:S(2)}) collective-permute-start(bf16[256,1408]{1,0:T(8,128)(2,1)S(1)} %get-tuple-element.128), channel_id=1, source_target_pairs={{0,4},{2,6},{4,0},{6,2},{8,12},{10,14},{12,8},{14,10},{16,20},{18,... | collective-permute-start | bytes 2162696 | tf_op jit(solution)/shard_map/ppermute | solution.py:25
  682.4 46.8 %collective-permute-start.38 = (bf16[256,1408]{1,0:T(8,128)(2,1)S(1)}, bf16[256,1408]{1,0:T(8,128)(2,1)S(1)}, u32[]{:S(2)}, u32[]{:S(2)}) collective-permute-start(bf16[256,1408]{1,0:T(8,128)(2,1)S(1)} %get-tuple-element.116), channel_id=1, source_target_pairs={{0,8},{2,10},{4,12},{6,14},{8,0},{10,2},{12,4},{14,6},{16,24},{18,... | collective-permute-start | bytes 2162696 | tf_op jit(solution)/shard_map/ppermute | solution.py:25
  697.0 46.3 %collective-permute-start.44 = (bf16[256,1408]{1,0:T(8,128)(2,1)S(1)}, bf16[256,1408]{1,0:T(8,128)(2,1)S(1)}, u32[]{:S(2)}, u32[]{:S(2)}) collective-permute-start(bf16[256,1408]{1,0:T(8,128)(2,1)S(1)} %get-tuple-element.124), channel_id=1, source_target_pairs={{0,4},{2,6},{4,0},{6,2},{8,12},{10,14},{12,8},{14,10},{16,20},{18,... | collective-permute-start | bytes 2162696 | tf_op jit(solution)/shard_map/ppermute | solution.py:25
  713.3 30.0 %collective-permute-start.46 = (bf16[256,1408]{1,0:T(8,128)(2,1)S(1)}, bf16[256,1408]{1,0:T(8,128)(2,1)S(1)}, u32[]{:S(2)}, u32[]{:S(2)}) collective-permute-start(bf16[256,1408]{1,0:T(8,128)(2,1)S(1)} %get-tuple-element.114), channel_id=1, source_target_pairs={{0,8},{2,10},{4,12},{6,14},{8,0},{10,2},{12,4},{14,6},{16,24},{18,... | collective-permute-start | bytes 2162696 | tf_op jit(solution)/shard_map/ppermute | solution.py:25
  727.9 30.9 %collective-permute-start.52 = (bf16[256,1408]{1,0:T(8,128)(2,1)S(1)}, bf16[256,1408]{1,0:T(8,128)(2,1)S(1)}, u32[]{:S(2)}, u32[]{:S(2)}) collective-permute-start(bf16[256,1408]{1,0:T(8,128)(2,1)S(1)} %get-tuple-element.120), channel_id=1, source_target_pairs={{0,4},{2,6},{4,0},{6,2},{8,12},{10,14},{12,8},{14,10},{16,20},{18,... | collective-permute-start | bytes 2162696 | tf_op jit(solution)/shard_map/ppermute | solution.py:25
  729.2 30.9 %collective-permute-start.54 = (bf16[256,1408]{1,0:T(8,128)(2,1)}, bf16[256,1408]{1,0:T(8,128)(2,1)S(1)}, u32[]{:S(2)}, u32[]{:S(2)}) collective-permute-start(bf16[256,1408]{1,0:T(8,128)(2,1)} %get-tuple-element.112), channel_id=1, source_target_pairs={{0,8},{2,10},{4,12},{6,14},{8,0},{10,2},{12,4},{14,6},{16,24},{18,... | collective-permute-start | bytes 2162696 | tf_op jit(solution)/shard_map/ppermute | solution.py:25
  743.3 31.6 %collective-permute-start.7 = (bf16[384,2048]{1,0:T(8,128)(2,1)S(1)}, bf16[384,2048]{1,0:T(8,128)(2,1)S(1)}, u32[]{:S(2)}, u32[]{:S(2)}) collective-permute-start(bf16[384,2048]{1,0:T(8,128)(2,1)S(1)} %slice.431), channel_id=1, source_target_pairs={{0,2},{2,0},{4,6},{6,4},{8,10},{10,8},{12,14},{14,12},{16,18},{18,... | collective-permute-start | bytes 4718600 | tf_op jit(solution)/shard_map/ppermute | solution.py:20
  743.3 30.9 %collective-permute-start.33 = (bf16[256,1408]{1,0:T(8,128)(2,1)S(1)}, bf16[256,1408]{1,0:T(8,128)(2,1)S(1)}, u32[]{:S(2)}, u32[]{:S(2)}) collective-permute-start(bf16[256,1408]{1,0:T(8,128)(2,1)S(1)} %get-tuple-element.126), channel_id=1, source_target_pairs={{0,4},{2,6},{4,0},{6,2},{8,12},{10,14},{12,8},{14,10},{16,20},{18,... | collective-permute-start | bytes 2162696 | tf_op jit(solution)/shard_map/ppermute | solution.py:25
  758.8 39.0 %collective-permute-start.41 = (bf16[256,1408]{1,0:T(8,128)(2,1)S(1)}, bf16[256,1408]{1,0:T(8,128)(2,1)S(1)}, u32[]{:S(2)}, u32[]{:S(2)}) collective-permute-start(bf16[256,1408]{1,0:T(8,128)(2,1)S(1)} %get-tuple-element.122), channel_id=1, source_target_pairs={{0,4},{2,6},{4,0},{6,2},{8,12},{10,14},{12,8},{14,10},{16,20},{18,... | collective-permute-start | bytes 2162696 | tf_op jit(solution)/shard_map/ppermute | solution.py:25
  760.1 36.3 %collective-permute-start.35 = (bf16[256,1408]{1,0:T(8,128)(2,1)S(1)}, bf16[256,1408]{1,0:T(8,128)(2,1)S(1)}, u32[]{:S(2)}, u32[]{:S(2)}) collective-permute-start(bf16[256,1408]{1,0:T(8,128)(2,1)S(1)} %get-tuple-element.115), channel_id=1, source_target_pairs={{0,8},{2,10},{4,12},{6,14},{8,0},{10,2},{12,4},{14,6},{16,24},{18,... | collective-permute-start | bytes 2162696 | tf_op jit(solution)/shard_map/ppermute | solution.py:25
  760.5 35.9 %collective-permute-start.39 = (bf16[256,1408]{1,0:T(8,128)(2,1)S(1)}, bf16[256,1408]{1,0:T(8,128)(2,1)S(1)}, u32[]{:S(2)}, u32[]{:S(2)}) collective-permute-start(bf16[256,1408]{1,0:T(8,128)(2,1)S(1)} %fusion.48), channel_id=1, source_target_pairs={{0,16},{2,18},{4,20},{6,22},{8,24},{10,26},{12,28},{14,30},{16,0},... | collective-permute-start | bytes 2162696 | tf_op jit(solution)/shard_map/ppermute | solution.py:25
  774.2 53.0 %collective-permute-start.43 = (bf16[256,1408]{1,0:T(8,128)(2,1)S(1)}, bf16[256,1408]{1,0:T(8,128)(2,1)S(1)}, u32[]{:S(2)}, u32[]{:S(2)}) collective-permute-start(bf16[256,1408]{1,0:T(8,128)(2,1)S(1)} %get-tuple-element.113), channel_id=1, source_target_pairs={{0,8},{2,10},{4,12},{6,14},{8,0},{10,2},{12,4},{14,6},{16,24},{18,... | collective-permute-start | bytes 2162696 | tf_op jit(solution)/shard_map/ppermute | solution.py:25
  774.9 53.8 %collective-permute-start.47 = (bf16[256,1408]{1,0:T(8,128)(2,1)S(1)}, bf16[256,1408]{1,0:T(8,128)(2,1)S(1)}, u32[]{:S(2)}, u32[]{:S(2)}) collective-permute-start(bf16[256,1408]{1,0:T(8,128)(2,1)S(1)} %fusion.42), channel_id=1, source_target_pairs={{0,16},{2,18},{4,20},{6,22},{8,24},{10,26},{12,28},{14,30},{16,0},... | collective-permute-start | bytes 2162696 | tf_op jit(solution)/shard_map/ppermute | solution.py:25
  796.4 35.3 %collective-permute-start.49 = (bf16[256,1408]{1,0:T(8,128)(2,1)S(1)}, bf16[256,1408]{1,0:T(8,128)(2,1)S(1)}, u32[]{:S(2)}, u32[]{:S(2)}) collective-permute-start(bf16[256,1408]{1,0:T(8,128)(2,1)S(1)} %get-tuple-element.118), channel_id=1, source_target_pairs={{0,4},{2,6},{4,0},{6,2},{8,12},{10,14},{12,8},{14,10},{16,20},{18,... | collective-permute-start | bytes 2162696 | tf_op jit(solution)/shard_map/ppermute | solution.py:25
  796.4 58.0 %collective-permute-start.51 = (bf16[256,1408]{1,0:T(8,128)(2,1)S(1)}, bf16[256,1408]{1,0:T(8,128)(2,1)S(1)}, u32[]{:S(2)}, u32[]{:S(2)}) collective-permute-start(bf16[256,1408]{1,0:T(8,128)(2,1)S(1)} %get-tuple-element.111), channel_id=1, source_target_pairs={{0,8},{2,10},{4,12},{6,14},{8,0},{10,2},{12,4},{14,6},{16,24},{18,... | collective-permute-start | bytes 2162696 | tf_op jit(solution)/shard_map/ppermute | solution.py:25
  797.7 56.7 %collective-permute-start.55 = (bf16[256,1408]{1,0:T(8,128)(2,1)S(1)}, bf16[256,1408]{1,0:T(8,128)(2,1)S(1)}, u32[]{:S(2)}, u32[]{:S(2)}) collective-permute-start(bf16[256,1408]{1,0:T(8,128)(2,1)S(1)} %fusion.36), channel_id=1, source_target_pairs={{0,16},{2,18},{4,20},{6,22},{8,24},{10,26},{12,28},{14,30},{16,0},... | collective-permute-start | bytes 2162696 | tf_op jit(solution)/shard_map/ppermute | solution.py:25
  827.2 37.3 %collective-permute-start.10 = (bf16[384,2048]{1,0:T(8,128)(2,1)S(1)}, bf16[384,2048]{1,0:T(8,128)(2,1)S(1)}, u32[]{:S(2)}, u32[]{:S(2)}) collective-permute-start(bf16[384,2048]{1,0:T(8,128)(2,1)S(1)} %add_convert_fusion.2), channel_id=1, source_target_pairs={{0,1},{1,0},{2,3},{3,2},{4,5},{5,4},{6,7},{7,6},{8,9},{9,8},{10,11... | collective-permute-start | bytes 4718600 | tf_op jit(solution)/shard_map/ppermute | solution.py:29
  828.7 63.0 %collective-permute-start.8 = (bf16[384,2048]{1,0:T(8,128)(2,1)S(1)}, bf16[384,2048]{1,0:T(8,128)(2,1)S(1)}, u32[]{:S(2)}, u32[]{:S(2)}) collective-permute-start(bf16[384,2048]{1,0:T(8,128)(2,1)S(1)} %add_convert_fusion.4), channel_id=1, source_target_pairs={{0,1},{1,0},{2,3},{3,2},{4,5},{5,4},{6,7},{7,6},{8,9},{9,8},{10,11... | collective-permute-start | bytes 4718600 | tf_op jit(solution)/shard_map/ppermute | solution.py:29
  831.7 68.3 %collective-permute-start.40 = (f32[128,1408]{1,0:T(8,128)}, f32[128,1408]{1,0:T(8,128)}, u32[]{:S(2)}, u32[]{:S(2)}) collective-permute-start(f32[128,1408]{1,0:T(8,128)} %get-tuple-element.139), channel_id=1, source_target_pairs={{0,2},{2,0},{4,6},{6,4},{8,10},{10,8},{12,14},{14,12},{16,18},{18,... | collective-permute-start | bytes 2162696 | tf_op jit(solution)/shard_map/ppermute | solution.py:20
  854.4 48.6 %collective-permute-start.48 = (f32[128,1408]{1,0:T(8,128)}, f32[128,1408]{1,0:T(8,128)}, u32[]{:S(2)}, u32[]{:S(2)}) collective-permute-start(f32[128,1408]{1,0:T(8,128)} %get-tuple-element.137), channel_id=1, source_target_pairs={{0,2},{2,0},{4,6},{6,4},{8,10},{10,8},{12,14},{14,12},{16,18},{18,... | collective-permute-start | bytes 2162696 | tf_op jit(solution)/shard_map/ppermute | solution.py:20
  854.9 41.0 %collective-permute-start.56 = (f32[128,1408]{1,0:T(8,128)S(1)}, f32[128,1408]{1,0:T(8,128)S(1)}, u32[]{:S(2)}, u32[]{:S(2)}) collective-permute-start(f32[128,1408]{1,0:T(8,128)S(1)} %get-tuple-element.135), channel_id=1, source_target_pairs={{0,2},{2,0},{4,6},{6,4},{8,10},{10,8},{12,14},{14,12},{16,18},{18,... | collective-permute-start | bytes 2162696 | tf_op jit(solution)/shard_map/ppermute | solution.py:20
  950.3 46.7 %collective-permute-start.15 = (bf16[384,2048]{1,0:T(8,128)(2,1)S(1)}, bf16[384,2048]{1,0:T(8,128)(2,1)S(1)}, u32[]{:S(2)}, u32[]{:S(2)}) collective-permute-start(bf16[384,2048]{1,0:T(8,128)(2,1)S(1)} %slice.440), channel_id=1, source_target_pairs={{0,2},{2,0},{4,6},{6,4},{8,10},{10,8},{12,14},{14,12},{16,18},{18,... | collective-permute-start | bytes 4718600 | tf_op jit(solution)/shard_map/ppermute | solution.py:20
  997.7 35.9 %collective-permute-start.16 = (bf16[384,2048]{1,0:T(8,128)(2,1)S(1)}, bf16[384,2048]{1,0:T(8,128)(2,1)}, u32[]{:S(2)}, u32[]{:S(2)}) collective-permute-start(bf16[384,2048]{1,0:T(8,128)(2,1)S(1)} %add_convert_fusion.1), channel_id=1, source_target_pairs={{0,1},{1,0},{2,3},{3,2},{4,5},{5,4},{6,7},{7,6},{8,9},{9,8},{10,11... | collective-permute-start | bytes 4718600 | tf_op jit(solution)/shard_map/ppermute | solution.py:29
  (75 other events, 878.9 us)
Sparse Core Ops, SparseCore 0:
  1042.6 56.7 reduce-scatter.3

commit v3 on v1

--- a/solution.py
+++ b/solution.py
@@ -13,6 +13,10 @@
 F32 = jnp.float32
 epsilon = 1e-05
 VMEM_LIMIT = 48 * 1024 * 1024
+VMEM_BIG = 62 * 1024 * 1024
+
+
+LOW = 2
 
 
 def swap_core(block):
@@ -25,28 +29,192 @@
     return lax.ppermute(block, "dp", [(i, i ^ (2 * distance)) for i in range(size)])
 
 
-def swap_tensor(block):
-    return lax.ppermute(block, "tensor", [(0, 1), (1, 0)])
-
-
-def gather_blocks(own, order):
-    held = {0: own}
-    for bit in order:
-        came = {key | bit: swap_chip(block, bit) for key, block in held.items()}
-        held.update(came)
-    return held
-
-
-def scatter_blocks(blocks, order):
-    held = dict(blocks)
-    for bit in reversed(order):
-        kept = {}
-        for key in sorted(held):
-            if key & bit:
-                came = swap_chip(held[key].astype(BF), bit)
-                kept[key ^ bit] = came
-        held = {key: held[key].astype(F32) + came.astype(F32) for key, came in kept.items()}
-    return held[0]
+def flipped(index, distance):
+    return index + distance * (1 - 2 * ((index // distance) % 2))
+
+
+def peer(distance=0, core=False, tensor=False):
+    place = lax.axis_index("dp")
+    bit = 1
+    while bit <= distance:
+        if distance & bit:
+            place = flipped(place, 2 * bit)
+        bit *= 2
+    if core:
+        place = flipped(place, 1)
+    half = lax.axis_index("tensor")
+    if tensor:
+        half = 1 - half
+    return (place, half)
+
+
+def greet(peers):
+    barrier = pltpu.get_barrier_semaphore()
+    for device in peers:
+        pl.semaphore_signal(barrier, inc=1, device_id=device, device_id_type=pl.DeviceIdType.MESH)
+    pl.semaphore_wait(barrier, len(peers))
+
+
+class Links:
+    def __init__(self, send, recv, local):
+        self.send, self.recv, self.local = send, recv, local
+        self.used = 0
+        self.used_local = 0
+        self.sent = []
+
+    def push(self, src, dst, device):
+        copy = pltpu.make_async_remote_copy(
+            src_ref=src,
+            dst_ref=dst,
+            send_sem=self.send.at[self.used],
+            recv_sem=self.recv.at[self.used],
+            device_id=device,
+            device_id_type=pl.DeviceIdType.MESH,
+        )
+        self.used += 1
+        copy.start()
+        self.sent.append(copy)
+        return copy
+
+    def copy(self, src, dst):
+        copy = pltpu.make_async_copy(src, dst, self.local.at[self.used_local])
+        self.used_local += 1
+        copy.start()
+        return copy
+
+    def close(self):
+        for copy in self.sent:
+            copy.wait_send()
+
+
+def link_scratch(copies, locals_):
+    return [
+        pltpu.SemaphoreType.DMA((copies,)),
+        pltpu.SemaphoreType.DMA((copies,)),
+        pltpu.SemaphoreType.DMA((locals_,)),
+    ]
+
+
+def low_bit():
+    return (lax.axis_index("dp") // (2 * LOW)) % 2
+
+
+def core_bit():
+    return lax.axis_index("dp") % 2
+
+
+def group_rows(height, low, core):
+    return pl.ds(pl.multiple_of((low * 2 + core) * height, height), height)
+
+
+class Spread:
+    def __init__(self, links, src, column, dst, height, start, cols, far):
+        self.links, self.src, self.column, self.dst = links, src, column, dst
+        self.height, self.start, self.cols, self.far = height, start, cols, far
+        self.level = 0
+
+    def begin(self):
+        low, core = low_bit(), core_bit()
+        mine = self.dst.at[group_rows(self.height, low, core), pl.ds(self.start, self.cols)]
+
+        def part(low, core):
+            return self.src.at[:, pl.ds(pl.multiple_of(self.column(low, core), 128), self.cols)]
+
+        self.local = self.links.copy(part(low, core), mine)
+        self.stage = [
+            self.links.push(part(1 - low, core), mine, peer(LOW)),
+            self.links.push(part(1 - low, 1 - core), mine, peer(LOW, core=True)),
+            self.links.push(part(low, 1 - core), mine, peer(core=True)),
+        ]
+
+    def step(self):
+        for copy in self.stage:
+            copy.wait_recv()
+        if self.level == 0:
+            self.local.wait()
+        self.stage = []
+        if self.level < len(self.far):
+            unit = 4 * self.height * 2**self.level
+            columns = pl.ds(self.start, self.cols)
+            self.stage.append(
+                self.links.push(
+                    self.dst.at[pl.ds(0, unit), columns],
+                    self.dst.at[pl.ds(unit, unit), columns],
+                    peer(self.far[self.level]),
+                )
+            )
+        self.level += 1
+
+
+class Ticks:
+    def __init__(self, spreads, levels):
+        self.spreads, self.levels, self.now, self.begun = spreads, levels, 0, 0
+        self.begin(2)
+
+    def begin(self, upto):
+        while self.begun < min(upto, len(self.spreads)):
+            self.spreads[self.begun].begin()
+            self.begun += 1
+
+    def tick(self):
+        self.begin(self.now + 3)
+        for level in range(self.levels):
+            if 0 <= self.now - level < len(self.spreads):
+                self.spreads[self.now - level].step()
+        self.now += 1
+
+    def rest(self):
+        while self.now < len(self.spreads) + self.levels - 1:
+            self.tick()
+
+
+class TokenSpread:
+    def __init__(self, links, whole, count):
+        self.links, self.whole, self.count = links, whole, count
+
+    def rows(self, slot, half=None):
+        if half is None:
+            return self.whole.at[pl.ds(slot * self.count, self.count)]
+        size = self.count // 2
+        return self.whole.at[pl.ds(pl.multiple_of(slot * self.count + half * size, size), size)]
+
+    def begin(self):
+        half = lax.axis_index("tensor")
+        self.side = self.links.push(self.rows(0), self.rows(1), peer(core=True))
+        self.low = self.links.push(self.rows(0, half), self.rows(2, half), peer(LOW))
+
+    def second(self):
+        half = lax.axis_index("tensor")
+        self.low.wait_recv()
+        self.across = self.links.push(self.rows(2, half), self.rows(2, half), peer(tensor=True))
+        self.first = self.links.push(self.rows(2, half), self.rows(3, half), peer(core=True))
+
+    def third(self):
+        other = 1 - lax.axis_index("tensor")
+        self.across.wait_recv()
+        self.last = self.links.push(self.rows(2, other), self.rows(3, other), peer(core=True))
+
+    def wait(self):
+        self.side.wait_recv()
+        self.first.wait_recv()
+        self.last.wait_recv()
+
+
+def cuts(start, tiles, parts):
+    edges = [start + tiles * part // parts * 128 for part in range(parts + 1)]
+    return [(edges[i], edges[i + 1] - edges[i]) for i in range(parts)]
+
+
+def by_rows(start, total, step, work):
+    def go(i, carry):
+        work(pl.multiple_of(start + i * step, step))
+        return carry
+
+    lax.fori_loop(0, total // step, go, 0)
+
+
+ANY = pl.BlockSpec(memory_space=pl.ANY)
+VMEM = pl.BlockSpec(memory_space=pltpu.VMEM)
 
 
 def dot_plain(left, right):
@@ -272,6 +440,536 @@
     )(kpos, rowinfo, cosine, sine, queries, grads, lse, *kvs)
 
 
+def gather_kernel(far, gain_src, pack_src, hid_src, cot_src, gains, attn_w, hid, cot, *sems):
+    links = Links(*sems)
+    greet(
+        [peer(core=True), peer(LOW), peer(LOW, core=True), peer(tensor=True)]
+        + [peer(bit) for bit in far]
+    )
+    count = hid_src.shape[0]
+    width = attn_w.shape[1]
+    spreads = [
+        Spread(links, gain_src, lambda low, core: 0, gains, gain_src.shape[0], 0, 128, far)
+    ]
+    for start, cols in cuts(0, width // 128, 3):
+        spreads.append(
+            Spread(
+                links,
+                pack_src,
+                lambda low, core, start=start: core * width + start,
+                attn_w,
+                pack_src.shape[0],
+                start,
+                cols,
+                far,
+            )
+        )
+    ticks = Ticks(spreads, len(far) + 1)
+    own_hid = links.copy(hid_src, hid.at[pl.ds(0, count)])
+    own_cot = links.copy(cot_src, cot.at[pl.ds(0, count)])
+    side = links.push(hid_src, hid.at[pl.ds(count, count)], peer(core=True))
+    own_cot.wait()
+    tokens = TokenSpread(links, cot, count)
+    ticks.tick()
+    tokens.begin()
+    ticks.tick()
+    ticks.tick()
+    tokens.second()
+    ticks.tick()
+    ticks.tick()
+    tokens.third()
+    ticks.rest()
+    tokens.wait()
+    own_hid.wait()
+    side.wait_recv()
+    links.close()
+
+
+def gather_attention(far, gain_pack, attn_pack, hidden, cotangent):
+    units = 2 ** len(far)
+    count, width = hidden.shape
+    shapes = [
+        jax.ShapeDtypeStruct((units * 4 * gain_pack.shape[0], 128), BF),
+        jax.ShapeDtypeStruct((units * 4 * attn_pack.shape[0], attn_pack.shape[1] // 2), BF),
+        jax.ShapeDtypeStruct((2 * count, width), BF),
+        jax.ShapeDtypeStruct((4 * count, width), BF),
+    ]
+    return pl.pallas_call(
+        functools.partial(gather_kernel, far),
+        in_specs=[ANY] * 4,
+        out_specs=[VMEM] * 4,
+        out_shape=shapes,
+        scratch_shapes=link_scratch(64, 16),
+        compiler_params=pltpu.CompilerParams(
+            collective_id=0, has_side_effects=True, vmem_limit_bytes=VMEM_LIMIT
+        ),
+        name="gather_attention",
+    )(gain_pack, attn_pack, hidden, cotangent)
+
+
+def silu_parts(gate, upward):
+    sigmoid = 1.0 / (1.0 + jnp.exp(-gate))
+    silu = gate * sigmoid
+    return silu * upward, upward * sigmoid * (1.0 + gate * (1.0 - sigmoid)), silu
+
+
+def ffn_forward_kernel(
+    far,
+    main,
+    mixed,
+    out_wt,
+    hidden,
+    gain,
+    pack,
+    middle,
+    act,
+    slope,
+    n2_out,
+    gu_out,
+    down_out,
+    gu_w,
+    down_w,
+    n2,
+    part,
+    land,
+    summ,
+    across,
+    *sems,
+):
+    links = Links(*sems)
+    greet(
+        [peer(core=True), peer(LOW), peer(LOW, core=True), peer(tensor=True)]
+        + [peer(bit) for bit in far]
+    )
+    height = pack.shape[0]
+    count = hidden.shape[0]
+    gu_cols, down_cols = gu_w.shape[1], down_w.shape[1]
+    total = gu_cols + down_cols
+    spreads = []
+    for dst, base, parts in ((gu_w, 0, 4), (down_w, gu_cols, 2)):
+        for start, cols in cuts(0, dst.shape[1] // 128, parts):
+            spreads.append(
+                Spread(
+                    links,
+                    pack,
+                    lambda low, core, at=base + start: (low * 2 + core) * total + at,
+                    dst,
+                    height,
+                    start,
+                    cols,
+                    far,
+                )
+            )
+    ticks = Ticks(spreads, len(far) + 1)
+    micro = 3
+    rows = count // micro
+    side = []
+    for m in range(micro):
+        span = pl.ds(m * rows, rows)
+        part[span] = dot_last(mixed[pl.ds(count + m * rows, rows)], out_wt[...]).astype(BF)
+        side.append(links.push(part.at[span], land.at[span], peer(core=True)))
+    half = []
+    for m in range(micro):
+        span = pl.ds(m * rows, rows)
+        own = dot_last(mixed[span], out_wt[...])
+        side[m].wait_recv()
+        summ[span] = (own + land[span].astype(F32)).astype(BF)
+        half.append(links.push(summ.at[span], across.at[span], peer(tensor=True)))
+    ticks.tick()
+
+    def finish(start):
+        span = pl.ds(start, 32)
+        value = (
+            hidden[span].astype(F32) + summ[span].astype(F32) + across[span].astype(F32)
+        )
+        middle[span] = value
+        ratio = lax.rsqrt(jnp.mean(value * value, axis=-1, keepdims=True) + epsilon)
+        n2[span] = (value * ratio * gain[...]).astype(BF)
+
+    for m in range(micro):
+        half[m].wait_recv()
+        by_rows(m * rows, rows, 32, finish)
+        if m < 2:
+            ticks.tick()
+    tokens = TokenSpread(links, n2, count)
+    tokens.begin()
+    ticks.tick()
+    tokens.second()
+    ticks.tick()
+    tokens.third()
+    ticks.tick()
+    tokens.wait()
+    outs = [links.copy(n2, n2_out), links.copy(gu_w, gu_out)]
+
+    def gates(start):
+        span = pl.ds(start, 256)
+        raw = dot_plain(n2[span], gu_w[...])
+        parts = silu_parts(raw[:, :main], raw[:, main : 2 * main])
+        last = raw[:, 2 * main :]
+        lane = lax.broadcasted_iota(jnp.int32, last.shape, 1)
+        ends = silu_parts(last, pltpu.roll(last, 64, 1))
+        for ref, base, body, end in (
+            (act, 0, parts[0], ends[0]),
+            (slope, 0, parts[1], ends[1]),
+            (slope, main + 128, parts[2], ends[2]),
+        ):
+            ref[span, base : base + main] = body.astype(BF)
+            ref[span, base + main : base + main + 128] = jnp.where(lane < 64, end, 0.0).astype(BF)
+
+    by_rows(0, 2 * count, 256, gates)
+    ticks.tick()
+    by_rows(2 * count, 2 * count, 256, gates)
+    ticks.rest()
+    outs.append(links.copy(down_w, down_out))
+    for copy in outs:
+        copy.wait()
+    links.close()
+
+
+def ffn_forward(far, main, mixed, out_wt, hidden, gain, pack):
+    units = 2 ** len(far)
+    count, width = hidden.shape
+    gu_cols, down_cols = 2 * main + 128, main + 128
+    group = 4 * count
+    shapes = [
+        jax.ShapeDtypeStruct((count, width), F32),
+        jax.ShapeDtypeStruct((group, down_cols), BF),
+        jax.ShapeDtypeStruct((group, 2 * down_cols), BF),
+        jax.ShapeDtypeStruct((group, width), BF),
+        jax.ShapeDtypeStruct((width, gu_cols), BF),
+        jax.ShapeDtypeStruct((width, down_cols), BF),
+    ]
+    return pl.pallas_call(
+        functools.partial(ffn_forward_kernel, far, main),
+        in_specs=[VMEM] * 4 + [ANY],
+        out_specs=[VMEM] * 3 + [ANY] * 3,
+        out_shape=shapes,
+        scratch_shapes=[
+            pltpu.VMEM((width, gu_cols), BF),
+            pltpu.VMEM((width, down_cols), BF),
+            pltpu.VMEM((group, width), BF),
+            pltpu.VMEM((count, width), BF),
+            pltpu.VMEM((count, width), BF),
+            pltpu.VMEM((count, width), BF),
+            pltpu.VMEM((count, width), BF),
+        ]
+        + link_scratch(64, 16),
+        compiler_params=pltpu.CompilerParams(
+            collective_id=1, has_side_effects=True, vmem_limit_bytes=VMEM_BIG
+        ),
+        name="ffn_forward",
+    )(mixed, out_wt, hidden, gain, pack)
+
+
+class Collect:
+    TILE = 256
+
+    def __init__(self, links, far, width, sent, came, held, came_far, total, more):
+        self.links, self.far, self.half = links, far, width // 2
+        self.sent, self.came, self.held, self.came_far = sent, came, held, came_far
+        self.total, self.more = total, more
+        self.tiles = self.half // self.TILE
+        self.arrivals = {}
+
+    def send_half(self, name, job, which=None):
+        columns, left, right = job
+        tiles, tile = self.tiles, self.TILE
+        if which is None:
+            which = [i for i in range(tiles // 2, tiles)] + [i for i in range(tiles // 2)]
+        for i in which:
+            rows = pl.ds(i * tile, tile)
+            start = self.half + i * tile
+            self.sent[rows, columns] = dot_first(left[:, start : start + tile], right[...]).astype(
+                BF
+            )
+            self.arrivals[name, i] = self.links.push(
+                self.sent.at[rows, columns], self.came.at[rows, columns], peer(self.far[-1])
+            )
+
+    def own_half(self, name, job, which):
+        columns, left, right = job
+        tiles, tile = self.tiles, self.TILE
+        for i in which:
+            rows = pl.ds(i * tile, tile)
+            self.arrivals[name, i].wait_recv()
+            term = dot_first(left[:, i * tile : (i + 1) * tile], right[...])
+            term = term + self.came[rows, columns].astype(F32)
+            if i >= tiles // 2:
+                place = pl.ds((i - tiles // 2) * tile, tile)
+                self.held[place, columns] = term.astype(BF)
+                self.arrivals[name, "far", i - tiles // 2] = self.links.push(
+                    self.held.at[place, columns],
+                    self.came_far.at[place, columns],
+                    peer(self.far[-2]),
+                )
+            else:
+                self.total[rows, columns] = term
+
+    def upper(self):
+        return range(self.tiles // 2, self.tiles)
+
+    def lower(self):
+        return range(self.tiles // 2)
+
+    def finish(self, name, job):
+        columns = job[0]
+        for i in self.lower():
+            rows = pl.ds(i * self.TILE, self.TILE)
+            self.arrivals[name, "far", i].wait_recv()
+            self.total[rows, columns] = self.total[rows, columns] + self.came_far[
+                rows, columns
+            ].astype(F32)
+
+    def finish_more(self):
+        kept = self.half // 2
+        for bit, (sent, came) in zip(self.far[-3::-1], self.more):
+            kept //= 2
+            sent[...] = self.total[pl.ds(kept, kept)].astype(BF)
+            copy = self.links.push(sent, came, peer(bit))
+            copy.wait_recv()
+            self.total[pl.ds(0, kept)] = self.total[pl.ds(0, kept)] + came[...].astype(F32)
+
+
+def collect_scratch(far, width, cols):
+    shapes = [
+        pltpu.VMEM((width // 2, cols), BF),
+        pltpu.VMEM((width // 2, cols), BF),
+        pltpu.VMEM((width // 4, cols), BF),
+        pltpu.VMEM((width // 4, cols), BF),
+    ]
+    kept = width // 4
+    for _ in far[2:]:
+        kept //= 2
+        shapes += [pltpu.VMEM((kept, cols), BF)] * 2
+    return shapes
+
+
+def paired(refs):
+    return [(refs[i], refs[i + 1]) for i in range(0, len(refs), 2)]
+
+
+def group_sum_parts(links, count, rows_of, part, land, low_part, land_low):
+    step = 128
+    flight = {}
+
+    def outer(slot):
+        def work(start):
+            dst = pl.ds(pl.multiple_of(start - (slot // 2 + 1) * count, step), step)
+            part[dst] = rows_of(start, step).astype(BF)
+
+        by_rows(slot * count, count, step, work)
+        rows = pl.ds((slot // 2) * count, count)
+        flight[slot] = links.push(part.at[rows], land.at[rows], peer(core=True))
+
+    def to_low():
+        flight[3].wait_recv()
+
+        def work(start):
+            dst = pl.ds(pl.multiple_of(start - 2 * count, step), step)
+            came = land[pl.ds(pl.multiple_of(start - count, step), step)].astype(F32)
+            low_part[dst] = (rows_of(start, step) + came).astype(BF)
+
+        by_rows(2 * count, count, step, work)
+        flight["low"] = links.push(low_part, land_low, peer(LOW))
+
+    def to_half(summ, across):
+        flight["low"].wait_recv()
+        flight[1].wait_recv()
+
+        def work(start):
+            span = pl.ds(start, step)
+            value = rows_of(start, step) + land[span].astype(F32) + land_low[span].astype(F32)
+            summ[span] = value.astype(BF)
+
+        by_rows(0, count, step, work)
+        flight["half"] = links.push(summ, across, peer(tensor=True))
+
+    return outer, to_low, to_half, flight
+
+
+def group_sum_scratch(count, width):
+    return [
+        pltpu.VMEM((2 * count, width), BF),
+        pltpu.VMEM((2 * count, width), BF),
+        pltpu.VMEM((count, width), BF),
+        pltpu.VMEM((count, width), BF),
+    ]
+
+
+def ffn_backward_kernel(far, main, *refs):
+    cot_in, act_in, down_in, slope_in, n2_in, gu_in = refs[:6]
+    summ, across, total = refs[6:9]
+    cot, act, down_w, slope, n2, gu_w = refs[9:15]
+    part, land, low_part, land_low = refs[15:19]
+    sent, came, held, came_far = refs[19:23]
+    more = paired(refs[23:-3])
+    links = Links(*refs[-3:])
+    loads = [
+        links.copy(src, dst)
+        for src, dst in (
+            (cot_in, cot),
+            (act_in, act),
+            (down_in, down_w),
+            (slope_in, slope),
+            (n2_in, n2),
+            (gu_in, gu_w),
+        )
+    ]
+    greet([peer(core=True), peer(LOW), peer(tensor=True)] + [peer(bit) for bit in far])
+    group, width = cot.shape
+    count = group // 4
+    down_cols, gu_cols = down_w.shape[1], gu_w.shape[1]
+    grads = slope.at[:, pl.ds(0, gu_cols)]
+    down_job = (pl.ds(0, down_cols), cot, act)
+    gu_job = (pl.ds(down_cols, gu_cols), n2, grads)
+    collect = Collect(links, far, width, sent, came, held, came_far, total, more)
+
+    loads[0].wait()
+    loads[1].wait()
+    collect.send_half("d", down_job)
+    loads[2].wait()
+    loads[3].wait()
+    lane = lax.broadcasted_iota(jnp.int32, (128, 128), 1)
+
+    def slopes(start):
+        span = pl.ds(start, 128)
+        grad_act = dot_plain(cot[span], down_w[...])
+        gate = grad_act * slope[span, 0:down_cols].astype(F32)
+        upward = grad_act * slope[span, down_cols : 2 * down_cols].astype(F32)
+        slope[span, 0:main] = gate[:, :main].astype(BF)
+        slope[span, main : 2 * main] = upward[:, :main].astype(BF)
+        last = jnp.where(lane < 64, gate[:, main:], pltpu.roll(upward[:, main:], 64, 1))
+        slope[span, 2 * main : 2 * main + 128] = last.astype(BF)
+
+    by_rows(0, group, 128, slopes)
+    loads[4].wait()
+    collect.send_half("g", gu_job)
+
+    loads[5].wait()
+
+    def rows_of(start, size):
+        return dot_last(slope[pl.ds(start, size), 0:gu_cols], gu_w[...])
+
+    outer, to_low, to_half, flight = group_sum_parts(
+        links, count, rows_of, part, land, low_part, land_low
+    )
+    outer(3)
+    outer(1)
+    to_low()
+    collect.own_half("d", down_job, collect.upper())
+    collect.own_half("d", down_job, collect.lower())
+    to_half(summ, across)
+    collect.own_half("g", gu_job, collect.upper())
+    collect.own_half("g", gu_job, collect.lower())
+    collect.finish("d", down_job)
+    collect.finish("g", gu_job)
+    collect.finish_more()
+    flight["half"].wait_recv()
+    links.close()
+
+
+def ffn_backward(far, main, cot, act, down_w, slope, n2, gu_w):
+    group, width = cot.shape
+    count = group // 4
+    cols = gu_w.shape[1] + down_w.shape[1]
+    inputs = (cot, act, down_w, slope, n2, gu_w)
+    return pl.pallas_call(
+        functools.partial(ffn_backward_kernel, far, main),
+        in_specs=[ANY] * 6,
+        out_specs=[VMEM] * 3,
+        out_shape=[
+            jax.ShapeDtypeStruct((count, width), BF),
+            jax.ShapeDtypeStruct((count, width), BF),
+            jax.ShapeDtypeStruct((width // 4, cols), F32),
+        ],
+        scratch_shapes=[pltpu.VMEM(a.shape, BF) for a in inputs]
+        + group_sum_scratch(count, width)
+        + collect_scratch(far, width, cols)
+        + link_scratch(64, 16),
+        compiler_params=pltpu.CompilerParams(
+            collective_id=2, has_side_effects=True, vmem_limit_bytes=VMEM_BIG
+        ),
+        name="ffn_backward",
+    )(*inputs)
+
+
+def attention_grads_kernel(far, *refs):
+    n1, raw, gmid, mixed, qkv_w, act, down_w = refs[:7]
+    summ, across, feed, feed_across, total = refs[7:12]
+    side, land_side = refs[12:14]
+    part, land, low_part, land_low = refs[14:18]
+    sent, came, held, came_far = refs[18:22]
+    more = paired(refs[22:-3])
+    links = Links(*refs[-3:])
+    greet([peer(core=True), peer(LOW), peer(tensor=True)] + [peer(bit) for bit in far])
+    width = n1.shape[1]
+    count = n1.shape[0] // 2
+    qkv_cols, out_cols = raw.shape[1], mixed.shape[1]
+    collect = Collect(links, far, width, sent, came, held, came_far, total, more)
+    qkv_job = (pl.ds(0, qkv_cols), n1, raw)
+    out_job = (pl.ds(qkv_cols, out_cols), gmid, mixed)
+    for which in ([i for i in collect.upper()], [i for i in collect.lower()]):
+        collect.send_half("o", out_job, which)
+        collect.send_half("q", qkv_job, which)
+
+    def side_rows(start):
+        dst = pl.ds(pl.multiple_of(start - count, 128), 128)
+        side[dst] = dot_last(raw[pl.ds(start, 128)], qkv_w[...]).astype(BF)
+
+    by_rows(count, count, 128, side_rows)
+    to_core = links.push(side, land_side, peer(core=True))
+
+    def rows_of(start, size):
+        return dot_last(act[pl.ds(start, size)], down_w[...])
+
+    outer, to_low, to_half, flight = group_sum_parts(
+        links, count, rows_of, part, land, low_part, land_low
+    )
+    outer(3)
+    to_core.wait_recv()
+
+    def own_rows(start):
+        span = pl.ds(start, 128)
+        value = dot_last(raw[span], qkv_w[...]) + land_side[span].astype(F32)
+        summ[span] = value.astype(BF)
+
+    by_rows(0, count, 128, own_rows)
+    over = links.push(summ, across, peer(tensor=True))
+    to_low()
+    outer(1)
+    for which in (collect.upper(), collect.lower()):
+        collect.own_half("o", out_job, which)
+        collect.own_half("q", qkv_job, which)
+    to_half(feed, feed_across)
+    collect.finish("o", out_job)
+    collect.finish("q", qkv_job)
+    collect.finish_more()
+    over.wait_recv()
+    flight["half"].wait_recv()
+    links.close()
+
+
+def attention_grads(far, n1, raw, gmid, mixed, qkv_w, act, down_w):
+    both, width = n1.shape
+    count = both // 2
+    cols = raw.shape[1] + mixed.shape[1]
+    rows = jax.ShapeDtypeStruct((count, width), BF)
+    return pl.pallas_call(
+        functools.partial(attention_grads_kernel, far),
+        in_specs=[VMEM] * 7,
+        out_specs=[VMEM] * 5,
+        out_shape=[rows, rows, rows, rows, jax.ShapeDtypeStruct((width // 4, cols), F32)],
+        scratch_shapes=[pltpu.VMEM((count, width), BF)] * 2
+        + group_sum_scratch(count, width)
+        + collect_scratch(far, width, cols)
+        + link_scratch(64, 16),
+        compiler_params=pltpu.CompilerParams(
+            collective_id=3, has_side_effects=True, vmem_limit_bytes=VMEM_BIG
+        ),
+        name="attention_grads",
+    )(n1, raw, gmid, mixed, qkv_w, act, down_w)
+
+
 def body(
     tokens,
     doc_position,
@@ -288,85 +986,110 @@
 ):
     size = lax.axis_size("dp")
     chips = size // 2
-    bits = [1 << place for place in range(chips.bit_length() - 1)]
+    far = [1 << place for place in range(chips.bit_length() - 1) if 1 << place != LOW][::-1]
     me = lax.axis_index("dp")
     core = me % 2
     chip = me // 2
+    low = (chip // LOW) % 2
     micro, stretch, width = tokens.shape
     count = micro * stretch
     block = width // chips
-
-    late_first = bits[::-1]
+    own_block = block // 2
     span_chips = SEQ_LEN // (2 * stretch)
     in_span = chip % span_chips
 
-    keys_order = [0]
-    for bit in late_first:
-        keys_order = keys_order + [key | bit for key in keys_order]
+    keys = [0]
+    for bit in far:
+        keys = keys + [key | bit for key in keys]
 
     def rearranged(array):
+        base = chip - LOW * low
         return jnp.concatenate(
             [
-                lax.dynamic_slice_in_dim(array, (chip ^ key) * block, block, array.ndim - 1)
-                for key in keys_order
+                lax.dynamic_slice_in_dim(
+                    array, ((base ^ key) + LOW * side) * block, block, array.ndim - 1
+                )
+                for key in keys
+                for side in range(2)
             ],
             axis=-1,
         )
 
     def restored(array):
-        where = [keys_order.index(key) for key in range(chips)]
-        places = jnp.array(where, jnp.int32)
+        unit_of = jnp.array([keys.index(other & ~LOW) for other in range(chips)], jnp.int32)
         return jnp.concatenate(
             [
                 lax.dynamic_slice_in_dim(
-                    array, places[chip ^ natural] * block, block, array.ndim - 1
+                    array,
+                    (unit_of[chip ^ natural] * 2 + (natural // LOW) % 2) * block,
+                    block,
+                    array.ndim - 1,
                 )
                 for natural in range(chips)
             ],
             axis=-1,
         )
 
-    def split_core(weight):
-        half = weight.shape[1] // 2
-        first, second = weight[:, :half], weight[:, half:]
-        mine = jnp.where(core == 0, first, second)
-        other = jnp.where(core == 0, second, first)
-        return mine, other
-
-    def joined_core(mine, came):
-        return jnp.where(
-            core == 0,
-            jnp.concatenate([mine, came], axis=0),
-            jnp.concatenate([came, mine], axis=0),
-        )
-
-    attn_parts = [split_core(w) for w in (w_query, w_key, w_value, w_out.T)]
-    attn_mine = jnp.concatenate([p[0] for p in attn_parts], axis=1)
-    attn_other = jnp.concatenate([p[1] for p in attn_parts], axis=1)
-    attn_own = joined_core(attn_mine, swap_core(attn_other))
-    gate_parts = split_core(w_gate)
-    gate_own = joined_core(gate_parts[0], swap_core(gate_parts[1]))
-    up_parts = split_core(w_up)
-    up_own = joined_core(up_parts[0], swap_core(up_parts[1]))
-    down_parts = split_core(w_down.T)
-    down_own = joined_core(down_parts[0], swap_core(down_parts[1]))
-
-    def whole(own, order):
-        held = gather_blocks(own, order)
-        return jnp.concatenate([held[key] for key in keys_order], axis=0)
-
-    gains = jnp.stack([attn_gain, ffn_gain])
-    gains = lax.all_gather(gains, "dp", axis=1, tiled=True).astype(F32)
-    gains = rearranged(gains)
-    gain_one, gain_two = gains[0:1], gains[1:2]
-
+    def halves(array):
+        n = array.shape[1] // 2
+        return array[:, :n], array[:, n:]
+
+    attn_pack = jnp.concatenate(
+        [
+            halves(w)[side]
+            for side in range(2)
+            for w in (w_query, w_key, w_value, w_out.T)
+        ],
+        axis=1,
+    )
+    hidden_units = w_gate.shape[1] // 4
+    main = hidden_units // 128 * 128
+    rest = hidden_units - main
+    assert rest == 64
+
+    def mains(array, place):
+        return array[:, place * main : (place + 1) * main]
+
+    def rests(array, place):
+        return array[:, 4 * main + place * rest : 4 * main + (place + 1) * rest]
+
+    w_down_t = w_down.T
+    empty = jnp.zeros((own_block, 128 - rest), BF)
+    ffn_pack = jnp.concatenate(
+        [
+            piece
+            for place in range(4)
+            for piece in (
+                mains(w_gate, place),
+                mains(w_up, place),
+                rests(w_gate, place),
+                rests(w_up, place),
+                mains(w_down_t, place),
+                rests(w_down_t, place),
+                empty,
+            )
+        ],
+        axis=1,
+    )
+    gain_pack = jnp.zeros((16, 128), BF).at[0, :own_block].set(attn_gain)
+    gain_pack = gain_pack.at[1, :own_block].set(ffn_gain)
     hidden = rearranged(tokens.reshape(count, width))
     grad_final = rearranged(cotangent.reshape(count, width))
+
+    gains, attn_w, hidden_both, grad_final_all = gather_attention(
+        far, gain_pack, attn_pack, hidden, grad_final
+    )
+    gains = gains.reshape(2 ** len(far), 4, 16, 128)[:, :, :2, :own_block]
+    gains = gains.transpose(2, 0, 1, 3).reshape(2, width).astype(F32)
+    gain_one, gain_two = gains[0:1], gains[1:2]
+
+    hidden_both_f = hidden_both.astype(F32)
+    ratio_both = lax.rsqrt(
+        jnp.mean(hidden_both_f * hidden_both_f, axis=-1, keepdims=True) + epsilon
+    )
+    normed = (hidden_both_f * ratio_both * gain_one).astype(BF)
     hidden_f = hidden.astype(F32)
-    ratio_one = lax.rsqrt(jnp.mean(hidden_f * hidden_f, axis=-1, keepdims=True) + epsilon)
-    normed_own = (hidden_f * ratio_one * gain_one).astype(BF)
-    normed = jnp.concatenate([normed_own, swap_core(normed_own)], axis=0)
-    grad_final_both = jnp.concatenate([grad_final, swap_core(grad_final)], axis=0)
+    ratio_one = ratio_both[:count]
     position_both = jnp.stack([doc_position, swap_core(doc_position)])
 
     power = jnp.arange(HEAD_DIM // 2, dtype=F32) * (2.0 / HEAD_DIM)
@@ -383,11 +1106,11 @@
     row_places = jnp.broadcast_to(row_place[None, :], row_position.shape)
     rowinfo = jnp.stack([row_places, row_places - row_position], axis=1)
 
-    attn_w = whole(attn_own, late_first)
     n_q = w_query.shape[1] // 2
     n_kv = w_key.shape[1] // 2
-    qkv_w = attn_w[:, : n_q + 2 * n_kv]
-    out_wt = attn_w[:, n_q + 2 * n_kv :]
+    n_qkv = n_q + 2 * n_kv
+    qkv_w = attn_w[:, :n_qkv]
+    out_wt = attn_w[:, n_qkv:]
     queries, kv_own = project(normed, qkv_w, cosine, sine)
     kv_shape = (2, micro, stretch, 2 * n_kv)
     kvs = [kv_own.reshape(kv_shape)] + [
@@ -397,63 +1120,14 @@
     mixed, lse = attend(kpos, rowinfo, queries, kvs)
     mixed = mixed.reshape(2 * count, n_q)
 
-    def summed(partial):
-        partial = partial.astype(BF)
-        mine = (partial[:count].astype(F32) + swap_core(partial[count:]).astype(F32)).astype(BF)
-        return mine.astype(F32) + swap_tensor(mine).astype(F32)
-
-    attended = summed(dot_last(mixed, out_wt))
-    middle = hidden_f + attended
+    middle, activated, slopes, normed_two, gu_w, down_wt = ffn_forward(
+        far, main, mixed, out_wt, hidden, gain_two, ffn_pack
+    )
+    grad_two, grad_two_across, ffn_grad = ffn_backward(
+        far, main, grad_final_all, activated, down_wt, slopes, normed_two, gu_w
+    )
+    grad_normed_two = grad_two.astype(F32) + grad_two_across.astype(F32)
     ratio_two = lax.rsqrt(jnp.mean(middle * middle, axis=-1, keepdims=True) + epsilon)
-    normed_two_own = (middle * ratio_two * gain_two).astype(BF)
-    normed_two = jnp.concatenate([normed_two_own, swap_core(normed_two_own)], axis=0)
-
-    gate_w = whole(gate_own, late_first)
-    up_w = whole(up_own, late_first)
-    down_wt = whole(down_own, late_first)
-    gate = dot_plain(normed_two, gate_w)
-    upward = dot_plain(normed_two, up_w)
-    sigmoid = jax.nn.sigmoid(gate)
-    silu = gate * sigmoid
-    activated = (silu * upward).astype(BF)
-
-    def weight_grad(left, right, order):
-        first = order[-1]
-        top = [place for place, key in enumerate(keys_order) if key & first]
-        half = chips // 2
-        assert top == list(range(half, chips))
-        sent = dot_first(left[:, half * block :], right).astype(BF)
-        kept = dot_first(left[:, : half * block], right)
-        blocks = {}
-        for place in range(half):
-            blocks[keys_order[place]] = kept[place * block : (place + 1) * block]
-            blocks[keys_order[place + half]] = sent[place * block : (place + 1) * block]
-        return scatter_blocks(blocks, order)
-
-    def unsplit_core(total):
-        half = block // 2
-        mine = jnp.where(core == 0, total[:half], total[half:])
-        other = jnp.where(core == 0, total[half:], total[:half])
-        came = swap_core(other)
-        return mine, came
-
-    def columns(mine, came):
-        return jnp.where(
-            core == 0,
-            jnp.concatenate([mine, came], axis=1),
-            jnp.concatenate([came, mine], axis=1),
-        )
-
-    grad_down = weight_grad(grad_final_both, activated, late_first)
-    feed = summed(dot_last(activated, down_wt))
-    output = restored((middle + feed).astype(BF))
-
-    grad_act = dot_plain(grad_final_both, down_wt)
-    grad_gate_low = (grad_act * upward * sigmoid * (1.0 + gate * (1.0 - sigmoid))).astype(BF)
-    grad_up_low = (grad_act * silu).astype(BF)
-    grad_normed_two = summed(dot_last(grad_gate_low, gate_w) + dot_last(grad_up_low, up_w))
-    grad_gate = weight_grad(normed_two, grad_gate_low, late_first)
-    grad_up = weight_grad(normed_two, grad_up_low, late_first)
     grad_mid_norm, grad_gain_two = norm_back(grad_normed_two, middle, ratio_two, gain_two)
     grad_middle = grad_final.astype(F32) + grad_mid_norm
     grad_middle_low = grad_middle.astype(BF)
@@ -489,26 +1163,56 @@
         ],
         axis=1,
     )
-    grad_out_t = weight_grad(grad_middle_both, mixed, late_first)
-    grad_qkv = weight_grad(normed, grad_raw, late_first)
-    grad_normed = summed(dot_last(grad_raw, qkv_w))
+    grad_one, grad_one_across, feed, feed_across, attn_grad = attention_grads(
+        far, normed, grad_raw, grad_middle_both, mixed, qkv_w, activated, down_wt
+    )
+    output = restored((middle + (feed.astype(F32) + feed_across.astype(F32))).astype(BF))
+    grad_normed = grad_one.astype(F32) + grad_one_across.astype(F32)
     grad_in_norm, grad_gain_one = norm_back(grad_normed, hidden_f, ratio_one, gain_one)
     grad_tokens = restored(grad_middle + grad_in_norm)
 
     grad_gains = restored(jnp.stack([grad_gain_one, grad_gain_two]))
     grad_gains = lax.psum_scatter(grad_gains, "dp", scatter_dimension=1, tiled=True)
 
-    def split_cols(pair, start, stop):
-        return columns(pair[0][:, start:stop], pair[1][:, start:stop])
-
-    pair = unsplit_core(grad_qkv)
-    grad_w_query = split_cols(pair, 0, n_q)
-    grad_w_key = split_cols(pair, n_q, n_q + n_kv)
-    grad_w_value = split_cols(pair, n_q + n_kv, n_q + 2 * n_kv)
-    grad_w_out = columns(*unsplit_core(grad_out_t)).T
-    grad_w_gate = columns(*unsplit_core(grad_gate))
-    grad_w_up = columns(*unsplit_core(grad_up))
-    grad_w_down = columns(*unsplit_core(grad_down)).T
+    def picked(pair, side):
+        return jnp.where(side == 0, pair[0], pair[1]), jnp.where(side == 0, pair[1], pair[0])
+
+    attn_grad = attn_grad[: 2 * block].reshape(2, 2, own_block, -1)
+    mine, other = picked(attn_grad, low)
+    mine = mine + swap_chip(other.astype(BF), LOW).astype(F32)
+    mine, other = picked(mine, core)
+    came = swap_core(other)
+    parts = picked((mine, came), core)
+
+    def columns(start, stop):
+        return jnp.concatenate([part[:, start:stop] for part in parts], axis=1)
+
+    grad_w_query = columns(0, n_q)
+    grad_w_key = columns(n_q, n_q + n_kv)
+    grad_w_value = columns(n_q + n_kv, n_qkv)
+    grad_w_out = columns(n_qkv, n_qkv + n_q).T
+
+    ffn_grad = ffn_grad[: 2 * block].reshape(2, 2, own_block, -1)
+    mine, other = picked(ffn_grad, low)
+    came = swap_chip(other.astype(BF), LOW).astype(F32)
+    by_low = jnp.stack(picked((mine, came), low))
+    mine, other = picked((by_low[:, 0], by_low[:, 1]), core)
+    came = swap_core(other)
+    by_core = picked((mine, came), core)
+    places = [by_core[place % 2][place // 2] for place in range(4)]
+    down_cols = main + 128
+    gu = down_cols
+
+    def gathered(main_start, rest_start):
+        return jnp.concatenate(
+            [part[:, main_start : main_start + main] for part in places]
+            + [part[:, rest_start : rest_start + rest] for part in places],
+            axis=1,
+        )
+
+    grad_w_down = gathered(0, main).T
+    grad_w_gate = gathered(gu, gu + 2 * main)
+    grad_w_up = gathered(gu + main, gu + 2 * main + rest)
     return (
         output.reshape(tokens.shape),
         grad_tokens.reshape(tokens.shape),

time: 999 us -> 816 us (0.82)
  waiting for transfers between devices: 611 us -> 64.3 us
  Pallas kernels: 44.9 us -> 580 us
  matrix products: 95.3 us -> 4.45 us
  starting transfers between devices: 79.1 us -> 14.4 us
  local copies, waits for them, and re-layouts: 50.8 us -> 75.3 us
  blocking collectives: 22.6 us -> 0 us
  other arithmetic: 66.3 us -> 48.9 us
    pallas_call x0 -> x4, Pallas kernels: none -> 535 us  [the longest x1 157 us: ffn_backward(): pl.pallas_call(functools.partial(ffn_backward_kernel, far, main), in_spec...]
    ppermute x69 -> x8, waiting for transfers between devices: 511 us -> 23.4 us  [swap_chip(): lax.ppermute(block, 'dp', [(i, i ^ 2 * distance) for i in range(size)])]
    dot_general x15 -> x0, matrix products: 61.5 us -> none  [the longest x10 34.5 us: dot_first(): lax.dot_general(left, right, (((0,), (0,)), ((), ())), preferred_element_...]
    ppermute x69 -> x8, starting transfers between devices: 71.4 us -> 13.7 us  [swap_chip(): lax.ppermute(block, 'dp', [(i, i ^ 2 * distance) for i in range(size)])]
    ppermute x4 -> x0, waiting for transfers between devices: 45 us -> none  [swap_tensor(): return lax.ppermute(block, 'tensor', [(0, 1), (1, 0)])]
    dot_general x4 -> x1, matrix products: 33.8 us -> 4.45 us  [dot_plain(): return jnp.dot(left, right, preferred_element_type=F32)]
    all_gather x1 -> x0, blocking collectives: 22.6 us -> none  [body(): gains = lax.all_gather(gains, 'dp', axis=1, tiled=True).astype(F32)]
    unnamed x2, waiting for transfers between devices: 54.3 us -> 41 us
  transfers between devices with their start and end apart: 92 -> 13, of which waited for: 46 -> 6; matrix products, arithmetic and copies ran while one was open for 17% -> 13% of each run, Pallas kernels for 2% -> 31%
where the time goes in v3:
time: 816 us; the launch traced here: 807 us
  Pallas kernels  580 us (71%)
  local copies, waits for them, and re-layouts  75.3 us (9%)
  waiting for transfers between devices  64.3 us (8%)
  other arithmetic  48.9 us (6%)
  between operations  20.4 us (2%)
  starting transfers between devices  14.4 us (2%)
    pallas_call x1, Pallas kernels, ffn_backward(): pl.pallas_call(functools.partial(ffn_backward_kernel, far, main), in_spec...  157 us
    pallas_call x1, Pallas kernels, ffn_forward(): pl.pallas_call(functools.partial(ffn_forward_kernel, far, main), in_specs...  153 us
    pallas_call x1, Pallas kernels, attention_grads(): pl.pallas_call(functools.partial(attention_grads_kernel, far), in_specs=[...  129 us
    pallas_call x1, Pallas kernels, gather_attention(): pl.pallas_call(functools.partial(gather_kernel, far), in_specs=[ANY] * 4,...  96.8 us
    unnamed x2, waiting for transfers between devices  41 us
    unnamed x140, local copies, waits for them, and re-layouts  37.9 us
    ppermute x8, waiting for transfers between devices, swap_chip(): lax.ppermute(block, 'dp', [(i, i ^ 2 * distance) for i in range(size)])  23.4 us
    pallas_call x1, Pallas kernels, attend_back(): pl.pallas_call(functools.partial(attend_back_kernel, len(kvs)), grid=(mic...  22.3 us
  transfers between devices with their start and end apart: 13, of which 6 were waited for; matrix products, arithmetic and copies ran while one was open for 13% of the time, Pallas kernels for 31%

profile of v3, /device:TPU:0, one launch (start us, length us, event | category | flops | bytes accessed | tf_op | source)
XLA Modules:
  0.0 807.4 jit_solution(8182634269205902209)
XLA Ops:
  29.8 96.8 %gather_attention.1 = (bf16[256,128]{1,0:T(8,128)(2,1)S(1)}, bf16[2048,1152]{1,0:T(8,128)(2,1)}, bf16[768,2048]{1,0:T(8,128)(2,1)}, bf16[1536,2048]{1,0:T(8,128)(2,1)}) custom-call(bf16[16,128]{1,0:T(8,128)(2,1)S(1)} %scatter.9.gain_src, bf16[128,2304]{1,0:T(8,128)(2,1)S(1)} %copy-done.6, ...), custom_call_target="tpu_custom_call" | custom-call | tf_op jit(solution)/shard_map/gather_attention/pallas_call | solution.py:497
  128.6 4.0 slice.328.out_wt
  132.6 2.2 copy.62
  134.9 2.3 fusion.34
  146.7 2.7 fusion
  149.6 2.4 fusion.2.n_ref.refs_0_
  153.7 4.9 concatenate.59.pack
  161.5 4.7 project.1
  166.8 8.6 %collective-permute-start.2 = (bf16[768,128]{1,0:T(8,128)(2,1)S(1)}, bf16[768,128]{1,0:T(8,128)(2,1)S(1)}, u32[]{:S(2)}, u32[]{:S(2)}) collective-permute-start(bf16[768,128]{1,0:T(8,128)(2,1)S(1)} %get-tuple-element.66), channel_id=1, source_target_pairs={{0,8},{2,10},{4,12},{6,14},{8,0},{10,2},{12,4},{14,6},{16,24},{18,... | collective-permute-start | bytes 589832 | tf_op jit(solution)/shard_map/ppermute | solution.py:29
  177.8 3.3 collective-permute-done.2
  181.1 2.7 collective-permute-done.3
  183.8 17.3 %attend.1 = (bf16[2,3,128,512]{3,2,1,0:T(8,128)(2,1)S(1)}, f32[3,8,256]{2,1,0:T(8,128)S(1)}) custom-call(s32[1024,1]{1,0:T(8,128)S(1)} %copy-done.7, s32[3,2,256]{2,1,0:T(2,128)S(1)} %pad_add_fusion.row_ref, bf16[2,3,128,512]{3,2,1,0:T(8,128)(2,1)S(1)} %bitcast.97, bf16[2,3,128,128]{3,2,1,0:T(8,128)(2,1)S(1)} %bitcast.86, ...), custom_call_target="tpu_custom_call" | custom-call | flops 6442450944 | bytes 1572864 | tf_op jit(solution)/shard_map/attend/pallas_call | solution.py:335
  202.1 152.8 %ffn_forward.1 = (f32[384,2048]{1,0:T(8,128)}, bf16[1536,768]{1,0:T(8,128)(2,1)}, bf16[1536,1536]{1,0:T(8,128)(2,1)}, bf16[1536,2048]{1,0:T(8,128)(2,1)}, bf16[2...) custom-call(bf16[768,512]{1,0:T(8,128)(2,1)} %bitcast.82, bf16[2048,512]{1,0:T(8,128)(2,1)} %slice.328.out_wt, ...), custom_call_target="tpu_custom_call" | custom-call | tf_op jit(solution)/shard_map/ffn_forward/pallas_call | solution.py:642
  354.9 156.8 %ffn_backward.1 = (bf16[384,2048]{1,0:T(8,128)(2,1)}, bf16[384,2048]{1,0:T(8,128)(2,1)}, f32[512,2176]{1,0:T(8,128)}) custom-call(bf16[1536,2048]{1,0:T(8,128)(2,1)} %get-tuple-element.69.refs_0_, bf16[1536,768]{1,0:T(8,128)(2,1)} %get-tuple-element.70.refs_1_.refs_5_, bf16[2048,768]{1,0:T(8,128)(2,1)} %get-tuple-element.71.refs_2_.refs_6_, ...), custom_call_target="tpu_custom_call" | custom-call | tf_op jit(solution)/shard_map/ffn_backward/pallas_call | solution.py:876
  511.7 2.5 select_convert_fusion
  515.7 2.3 multiply_reduce_fusion.2
  518.5 3.1 multiply_reduce_fusion
  521.8 3.5 fusion.32
  526.9 3.0 copy.67
  529.9 12.4 %collective-permute-done.10 = bf16[2,128,2176]{1,2,0:T(8,128)(2,1)S(1)} collective-permute-done((bf16[2,128,2176]{1,2,0:T(8,128)(2,1)}, bf16[2,128,2176]{1,2,0:T(8,128)(2,1)S(1)}, u32[]{:S(2)}, u32[]{:S(2)}) %collective-permute-start.10) | collective-permute-done | bytes 1114144 | tf_op jit(solution)/shard_map/ppermute | solution.py:29
  546.6 4.4 convolution_convert_fusion
  551.1 22.3 %attend_back.1 = (bf16[2,3,128,512]{3,2,1,0:T(8,128)(2,1)S(1)}, f32[2,3,128,128]{3,2,1,0:T(8,128)S(1)}, bf16[2,3,128,128]{3,2,1,0:T(8,128)(2,1)S(1)}, bf16[2,3,1...) custom-call(s32[1024,1]{1,0:T(8,128)S(1)} %copy-done.8, s32[3,2,256]{2,1,0:T(2,128)S(1)} %pad_add_fusion.row_ref, ...), custom_call_target="tpu_custom_call" | custom-call | flops 16106127360 | bytes 3145728 | tf_op jit(solution)/shard_map/attend_back/pallas_call | solution.py:409
  574.6 2.4 collective-permute-start.7
  577.0 4.1 pad_maximum_fusion.refs_2_
  582.1 4.0 collective-permute-done.7
  587.6 129.0 %attention_grads.1 = (bf16[384,2048]{1,0:T(8,128)(2,1)}, bf16[384,2048]{1,0:T(8,128)(2,1)}, bf16[384,2048]{1,0:T(8,128)(2,1)}, bf16[384,2048]{1,0:T(8,128)(2,1)}, f32[512,1152]{1,0:T(8,128)}) custom-call(bf16[768,2048]{1,0:T(8,128)(2,1)} %fusion.2.n_ref.refs_0_, bf16[768,640]{1,0:T(8,128)(2,1)} %pad_maximum_fusion.2.refs_1_, ...), custom_call_target="tpu_custom_call" | custom-call | tf_op jit(solution)/shard_map/attention_grads/pallas_call | solution.py:957
  716.6 2.9 slice_select_fusion.1
  720.5 2.8 copy.65
  725.4 2.6 fusion.8
  730.1 3.6 fusion.5
  745.9 40.9 %reduce-scatter.4.cloned.1.call-done = f32[128,2]{1,0:T(8,128)} async-done(((f32[2048,2]{1,0:T(8,128)}), f32[128,2]{1,0:T(8,128)}) %reduce-scatter.4.cloned.1.call-update) | async-done | bytes 1040
  792.6 2.9 bitcast_select_fusion
  (233 shorter events, 76.7 us)
Async XLA Ops:
  7.2 779.7 %reduce-scatter.4.cloned.1.call-start = ((), (), s32[]{:S(2)}) async-start(), calls=%async_computation.1 | async-start | bytes 1114112
  7.2 151.4 %collective-permute-start = (s32[3,128]{1,0:T(4,128)}, s32[3,128]{1,0:T(4,128)}, u32[]{:S(2)}, u32[]{:S(2)}) collective-permute-start(s32[3,128]{1,0:T(4,128)} %param.20), channel_id=1, source_target_pairs={{0,2},{2,0},{4,6},{6,4},{8,10},{10,8},{12,14},{14,12},{16,18},{18,... | collective-permute-start | bytes 4616 | tf_op jit(solution)/shard_map/ppermute | solution.py:24
  19.8 7.0 copy-start.43
  19.9 7.1 copy-start.45
  21.8 104.8 %copy-start.3 = (bf16[384,2048]{1,0:T(8,128)(2,1)}, bf16[384,2048]{1,0:T(8,128)(2,1)S(1)}, u32[]{:S(2)}) copy-start(bf16[384,2048]{1,0:T(8,128)(2,1)S(1)} %dynamic-slice_dynamic-update-slice_fusion.16.cot_src) | copy-start | bytes 4718596
  23.0 103.7 %copy-start = (bf16[384,2048]{1,0:T(8,128)(2,1)}, bf16[384,2048]{1,0:T(8,128)(2,1)S(1)}, u32[]{:S(2)}) copy-start(bf16[384,2048]{1,0:T(8,128)(2,1)S(1)} %dynamic-slice_dynamic-update-slice_fusion.24.hid_src.hidden) | copy-start | bytes 4718596
  128.6 32.8 %copy-start.2 = (bf16[2048,640]{1,0:T(8,128)(2,1)}, bf16[2048,640]{1,0:T(8,128)(2,1)S(1)}, u32[]{:S(2)}) copy-start(bf16[2048,640]{1,0:T(8,128)(2,1)S(1)} %slice.327.w_ref.refs_4_) | copy-start | bytes 7864324
  153.7 4.9 copy-start.42
  161.5 14.9 %copy-start.40 = (s32[256]{0:T(256)S(1)}, s32[256]{0:T(256)}, u32[]{:S(2)}) copy-start(s32[256]{0:T(256)} %copy-done.39) | copy-start | bytes 3076
  161.5 14.9 %copy-start.41 = (f32[128]{0:T(128)S(1)}, f32[128]{0:T(128)}, u32[]{:S(2)}) copy-start(f32[128]{0:T(128)} %mul.444) | copy-start | bytes 1540
  161.5 22.4 %copy-start.7 = (s32[1024,1]{1,0:T(8,128)S(1)}, s32[1024,1]{1,0:T(8,128)}, u32[]{:S(2)}) copy-start(s32[1024,1]{1,0:T(8,128)} %copy.61.kpos_ref) | copy-start | bytes 12292
  166.1 35.0 %copy-start.9 = (bf16[768,128]{1,0:T(8,128)(2,1)}, bf16[768,128]{1,0:T(8,128)(2,1)S(1)}, u32[]{:S(2)}) copy-start(bf16[768,128]{1,0:T(8,128)(2,1)S(1)} %get-tuple-element.66) | copy-start | bytes 589828
  166.2 35.0 %copy-start.17 = (bf16[768,512]{1,0:T(8,128)(2,1)}, bf16[768,512]{1,0:T(8,128)(2,1)S(1)}, u32[]{:S(2)}) copy-start(bf16[768,512]{1,0:T(8,128)(2,1)S(1)} %get-tuple-element.65) | copy-start | bytes 2359300
  166.2 11.6 %collective-permute-start.1 = (bf16[768,128]{1,0:T(8,128)(2,1)S(1)}, bf16[768,128]{1,0:T(8,128)(2,1)S(1)}, u32[]{:S(2)}, u32[]{:S(2)}) collective-permute-start(bf16[768,128]{1,0:T(8,128)(2,1)S(1)} %get-tuple-element.66), channel_id=1, source_target_pairs={{0,4},{2,6},{4,0},{6,2},{8,12},{10,14},{12,8},{14,10},{16,20},{18,... | collective-permute-start | bytes 589832 | tf_op jit(solution)/shard_map/ppermute | solution.py:29
  166.8 14.3 %collective-permute-start.2 = (bf16[768,128]{1,0:T(8,128)(2,1)S(1)}, bf16[768,128]{1,0:T(8,128)(2,1)S(1)}, u32[]{:S(2)}, u32[]{:S(2)}) collective-permute-start(bf16[768,128]{1,0:T(8,128)(2,1)S(1)} %get-tuple-element.66), channel_id=1, source_target_pairs={{0,8},{2,10},{4,12},{6,14},{8,0},{10,2},{12,4},{14,6},{16,24},{18,... | collective-permute-start | bytes 589832 | tf_op jit(solution)/shard_map/ppermute | solution.py:29
  175.4 8.4 %collective-permute-start.3 = (bf16[768,128]{1,0:T(8,128)(2,1)S(1)}, bf16[768,128]{1,0:T(8,128)(2,1)S(1)}, u32[]{:S(2)}, u32[]{:S(2)}) collective-permute-start(bf16[768,128]{1,0:T(8,128)(2,1)S(1)} %get-tuple-element.66), channel_id=1, source_target_pairs={{0,12},{2,14},{4,8},{6,10},{8,4},{10,6},{12,0},{14,2},{16,28},{18,... | collective-permute-start | bytes 589832 | tf_op jit(solution)/shard_map/ppermute | solution.py:29
  177.8 23.3 %copy-start.11 = (bf16[768,128]{1,0:T(8,128)(2,1)}, bf16[768,128]{1,0:T(8,128)(2,1)S(1)}, u32[]{:S(2)}) copy-start(bf16[768,128]{1,0:T(8,128)(2,1)S(1)} %collective-permute-done.1) | copy-start | bytes 589828
  181.1 20.1 %copy-start.13 = (bf16[768,128]{1,0:T(8,128)(2,1)}, bf16[768,128]{1,0:T(8,128)(2,1)S(1)}, u32[]{:S(2)}) copy-start(bf16[768,128]{1,0:T(8,128)(2,1)S(1)} %collective-permute-done.2) | copy-start | bytes 589828
  183.8 17.3 %copy-start.15 = (bf16[768,128]{1,0:T(8,128)(2,1)}, bf16[768,128]{1,0:T(8,128)(2,1)S(1)}, u32[]{:S(2)}) copy-start(bf16[768,128]{1,0:T(8,128)(2,1)S(1)} %collective-permute-done.3) | copy-start | bytes 589828
  515.6 26.7 %collective-permute-start.10 = (bf16[2,128,2176]{1,2,0:T(8,128)(2,1)}, bf16[2,128,2176]{1,2,0:T(8,128)(2,1)S(1)}, u32[]{:S(2)}, u32[]{:S(2)}) collective-permute-start(bf16[2,128,2176]{1,2,0:T(8,128)(2,1)} %copy.66), channel_id=1, source_target_pairs={{0,8},{2,10},{4,12},{6,14},{8,0},{10,2},{12,4},{14,6},{16,24},{18,... | collective-permute-start | bytes 3342344 | tf_op jit(solution)/shard_map/ppermute | solution.py:29
  525.3 21.3 %collective-permute-start.4 = (bf16[384,2048]{1,0:T(8,128)(2,1)}, bf16[384,2048]{1,0:T(8,128)(2,1)}, u32[]{:S(2)}, u32[]{:S(2)}) collective-permute-start(bf16[384,2048]{1,0:T(8,128)(2,1)} %get-tuple-element.126), channel_id=1, source_target_pairs={{0,2},{2,0},{4,6},{6,4},{8,10},{10,8},{12,14},{14,12},{16,18},{18,... | collective-permute-start | bytes 4718600 | tf_op jit(solution)/shard_map/ppermute | solution.py:24
  544.3 6.8 copy-start.23
  546.5 4.6 copy-start.16
  546.5 4.6 copy-start.18
  546.5 246.1 %collective-permute-start.11 = (f32[2,128,2176]{1,2,0:T(8,128)}, f32[2,128,2176]{1,2,0:T(8,128)}, u32[]{:S(2)}, u32[]{:S(2)}) collective-permute-start(f32[2,128,2176]{1,2,0:T(8,128)} %select_bitcast_fusion), channel_id=1, source_target_pairs={{0,2},{2,0},{4,6},{6,4},{8,10},{10,8},{12,14},{14,12},{16,18},{18,... | collective-permute-start | bytes 6684680 | tf_op jit(solution)/shard_map/ppermute | solution.py:24
  573.4 7.7 collective-permute-start.5
  574.3 7.8 collective-permute-start.6
  574.6 11.5 %collective-permute-start.7 = (bf16[768,128]{1,0:T(8,128)(2,1)S(1)}, bf16[768,128]{1,0:T(8,128)(2,1)S(1)}, u32[]{:S(2)}, u32[]{:S(2)}) collective-permute-start(bf16[768,128]{1,0:T(8,128)(2,1)S(1)} %bitcast.94), channel_id=1, source_target_pairs={{0,12},{2,14},{4,8},{6,10},{8,4},{10,6},{12,0},{14,2},{16,28},{18,... | collective-permute-start | bytes 589832 | tf_op jit(solution)/shard_map/ppermute | solution.py:29
  720.5 4.9 copy-start.1
  720.5 4.9 copy-start.25
  725.4 15.6 %collective-permute-start.8 = (bf16[2,128,1152]{1,2,0:T(8,128)(2,1)}, bf16[2,128,1152]{1,2,0:T(8,128)(2,1)}, u32[]{:S(2)}, u32[]{:S(2)}) collective-permute-start(bf16[2,128,1152]{1,2,0:T(8,128)(2,1)} %copy.64), channel_id=1, source_target_pairs={{0,8},{2,10},{4,12},{6,14},{8,0},{10,2},{12,4},{14,6},{16,24},{18,... | collective-permute-start | bytes 1769480 | tf_op jit(solution)/shard_map/ppermute | solution.py:29
  743.4 45.7 %collective-permute-start.9 = (f32[128,1152]{0,1:T(8,128)S(1)}, f32[128,1152]{0,1:T(8,128)S(1)}, u32[]{:S(2)}, u32[]{:S(2)}) collective-permute-start(f32[128,1152]{0,1:T(8,128)S(1)} %select_bitcast_fusion.1), channel_id=1, source_target_pairs={{0,2},{2,0},{4,6},{6,4},{8,10},{10,8},{12,14},{14,12},{16,18},{18,... | collective-permute-start | bytes 1769480 | tf_op jit(solution)/shard_map/ppermute | solution.py:24
  (29 other events, 84.7 us)
Sparse Core Ops, SparseCore 0:
  730.1 56.6 reduce-scatter.3

commit v4 on v3

v4 whole, which is shorter than its diff:
```python
import functools

import jax
import jax.numpy as jnp
from jax import lax
from jax.experimental import pallas as pl
from jax.experimental.pallas import tpu as pltpu
from jax.sharding import PartitionSpec as P

HEAD_DIM = 64
SEQ_LEN = 1024
BF = jnp.bfloat16
F32 = jnp.float32
epsilon = 1e-05
VMEM_LIMIT = 48 * 1024 * 1024
VMEM_BIG = 62 * 1024 * 1024


LOW = 2


def swap_core(block):
    size = lax.axis_size("dp")
    return lax.ppermute(block, "dp", [(i, i ^ 1) for i in range(size)])


def swap_chip(block, distance):
    size = lax.axis_size("dp")
    return lax.ppermute(block, "dp", [(i, i ^ (2 * distance)) for i in range(size)])


def flipped(index, distance):
    return index + distance * (1 - 2 * ((index // distance) % 2))


def peer(distance=0, core=False, tensor=False):
    place = lax.axis_index("dp")
    bit = 1
    while bit <= distance:
        if distance & bit:
            place = flipped(place, 2 * bit)
        bit *= 2
    if core:
        place = flipped(place, 1)
    half = lax.axis_index("tensor")
    if tensor:
        half = 1 - half
    return (place, half)


def greet(peers):
    barrier = pltpu.get_barrier_semaphore()
    for name in sorted(set(peers)):
        pl.semaphore_signal(
            barrier, inc=1, device_id=peer(*name), device_id_type=pl.DeviceIdType.MESH
        )
    pl.semaphore_wait(barrier, len(set(peers)))


CORE = (0, True, False)
TENSOR = (0, False, True)


def chips_apart(*distances):
    return [(distance, False, False) for distance in distances]


class Links:
    def __init__(self, send, recv, local):
        self.send, self.recv, self.local = send, recv, local
        self.used = 0
        self.used_local = 0
        self.sent = []

    def push(self, src, dst, device):
        copy = pltpu.make_async_remote_copy(
            src_ref=src,
            dst_ref=dst,
            send_sem=self.send.at[self.used],
            recv_sem=self.recv.at[self.used],
            device_id=device,
            device_id_type=pl.DeviceIdType.MESH,
        )
        self.used += 1
        copy.start()
        self.sent.append(copy)
        return copy

    def copy(self, src, dst):
        copy = pltpu.make_async_copy(src, dst, self.local.at[self.used_local])
        self.used_local += 1
        copy.start()
        return copy

    def settle(self, copies):
        for copy in copies:
            copy.wait_send()
            self.sent = [other for other in self.sent if other is not copy]

    def close(self):
        for copy in self.sent:
            copy.wait_send()


def link_scratch(copies, locals_):
    return [
        pltpu.SemaphoreType.DMA((copies,)),
        pltpu.SemaphoreType.DMA((copies,)),
        pltpu.SemaphoreType.DMA((locals_,)),
    ]


def low_bit():
    return (lax.axis_index("dp") // (2 * LOW)) % 2


def core_bit():
    return lax.axis_index("dp") % 2


def group_rows(height, low, core):
    return pl.ds(pl.multiple_of((low * 2 + core) * height, height), height)


class Spread:
    def __init__(self, links, src, column, dst, height, start, cols, far):
        self.links, self.src, self.column, self.dst = links, src, column, dst
        self.height, self.start, self.cols, self.far = height, start, cols, far
        self.level = 0

    def begin(self):
        low, core = low_bit(), core_bit()
        mine = self.dst.at[group_rows(self.height, low, core), pl.ds(self.start, self.cols)]

        def part(low, core):
            return self.src.at[:, pl.ds(pl.multiple_of(self.column(low, core), 128), self.cols)]

        self.local = self.links.copy(part(low, core), mine)
        self.stage = [
            self.links.push(part(1 - low, core), mine, peer(LOW)),
            self.links.push(part(1 - low, 1 - core), mine, peer(LOW, core=True)),
            self.links.push(part(low, 1 - core), mine, peer(core=True)),
        ]

    def unit(self, index):
        size = 4 * self.height
        return self.dst.at[pl.ds(index * size, size), pl.ds(self.start, self.cols)]

    def pass_on(self, index, first):
        for level in range(first, len(self.far)):
            reached = index + 2**level
            self.arrivals[reached] = self.links.push(
                self.unit(index), self.unit(reached), peer(self.far[level])
            )

    def launch(self):
        for copy in self.stage:
            copy.wait_recv()
        self.local.wait()
        self.arrivals = {}
        self.pass_on(0, 0)

    def forward(self):
        for index in range(1, 2 ** (len(self.far) - 1)):
            self.arrivals.pop(index).wait_recv()
            self.pass_on(index, index.bit_length())

    def finish(self):
        for copy in self.arrivals.values():
            copy.wait_recv()
        self.arrivals = {}


class TokenSpread:
    def __init__(self, links, own, others):
        self.links, self.own, self.others = links, own, others
        self.count = own.shape[0]

    def rows(self, slot, half=None):
        ref = self.others if slot else self.own
        base = (slot - 1) * self.count if slot else 0
        if half is None:
            return ref.at[pl.ds(base, self.count)]
        size = self.count // 2
        return ref.at[pl.ds(pl.multiple_of(base + half * size, size), size)]

    def begin(self):
        half = lax.axis_index("tensor")
        self.side = self.links.push(self.rows(0), self.rows(1), peer(core=True))
        self.low = self.links.push(self.rows(0, half), self.rows(2, half), peer(LOW))

    def second(self):
        half = lax.axis_index("tensor")
        self.low.wait_recv()
        self.across = self.links.push(self.rows(2, half), self.rows(2, half), peer(tensor=True))
        self.first = self.links.push(self.rows(2, half), self.rows(3, half), peer(core=True))

    def third(self):
        other = 1 - lax.axis_index("tensor")
        self.across.wait_recv()
        self.last = self.links.push(self.rows(2, other), self.rows(3, other), peer(core=True))

    def wait(self):
        self.side.wait_recv()
        self.first.wait_recv()
        self.last.wait_recv()


def cuts(start, tiles, parts):
    edges = [start + tiles * part // parts * 128 for part in range(parts + 1)]
    return [(edges[i], edges[i + 1] - edges[i]) for i in range(parts)]


def by_rows(start, total, step, work):
    def go(i, carry):
        work(pl.multiple_of(start + i * step, step))
        return carry

    lax.fori_loop(0, total // step, go, 0)


ANY = pl.BlockSpec(memory_space=pl.ANY)
VMEM = pl.BlockSpec(memory_space=pltpu.VMEM)


def dot_plain(left, right):
    return jnp.dot(left, right, preferred_element_type=F32)


def dot_first(left, right):
    return lax.dot_general(left, right, (((0,), (0,)), ((), ())), preferred_element_type=F32)


def dot_last(left, right):
    return lax.dot_general(left, right, (((1,), (1,)), ((), ())), preferred_element_type=F32)


def norm_back(grad, value, ratio, gain):
    scaled = grad * gain
    inner = jnp.mean(scaled * value, axis=-1, keepdims=True)
    return ratio * scaled - value * ratio**3 * inner


def turn(value, cosine, sine, back):
    tiles = []
    lane = lax.broadcasted_iota(jnp.int32, (value.shape[0], 128), 1)
    first = (lane % 64) < 32
    for start in range(0, value.shape[1], 128):
        tile = value[:, start : start + 128]
        up = pltpu.roll(tile, 96, 1)
        down = pltpu.roll(tile, 32, 1)
        if back:
            other = jnp.where(first, up, -down)
        else:
            other = jnp.where(first, -up, down)
        tiles.append(tile * cosine + other * sine)
    return tiles[0] if len(tiles) == 1 else jnp.concatenate(tiles, axis=1)


def mask_bias(kpos, row):
    place, floor = row[0:1, :], row[1:2, :]
    allowed = (kpos <= place) & (kpos >= floor)
    return jnp.where(allowed, 0.0, -1e30).astype(F32)


def attend(bias_ref, queries, kv):
    keys = kv[:, :HEAD_DIM]
    values_t = kv.T[HEAD_DIM:, :]
    parts = []
    sums = []
    for head in range(queries.shape[1] // HEAD_DIM):
        q_head = queries[:, head * HEAD_DIM : (head + 1) * HEAD_DIM]
        scores = dot_last(keys, q_head) + bias_ref[...]
        peak = jnp.max(scores, axis=0, keepdims=True)
        expon = jnp.exp(scores - peak)
        total = jnp.sum(expon, axis=0, keepdims=True)
        parts.append(dot_plain(values_t, expon.astype(BF)) * (1.0 / total))
        sums.append(peak + jnp.log(total))
    return jnp.concatenate(parts, axis=0), jnp.concatenate(sums, axis=0)


def attend_back(bias_ref, queries, grads, lse, kv, dk_ref, dv_ref):
    keys = kv[:, :HEAD_DIM]
    values = kv[:, HEAD_DIM:]
    keys_t = kv.T[:HEAD_DIM, :]
    parts = []
    for head in range(queries.shape[1] // HEAD_DIM):
        q_head = queries[:, head * HEAD_DIM : (head + 1) * HEAD_DIM]
        g_head = grads[:, head * HEAD_DIM : (head + 1) * HEAD_DIM]
        scores = dot_last(keys, q_head) + bias_ref[...]
        probs = jnp.exp(scores - lse[head : head + 1, :])
        grad_probs = dot_last(values, g_head)
        inner = jnp.sum(probs * grad_probs, axis=0, keepdims=True)
        grad_scores = (probs * (grad_probs - inner)).astype(BF)
        grad_values = dot_plain(probs.astype(BF), g_head)
        grad_keys = dot_plain(grad_scores, q_head)
        if head == 0:
            dv_ref[...] = grad_values
            dk_ref[...] = grad_keys
        else:
            dv_ref[...] += grad_values
            dk_ref[...] += grad_keys
        parts.append(dot_plain(keys_t, grad_scores))
    return jnp.concatenate(parts, axis=0).T * HEAD_DIM ** (-0.5)


def silu_parts(gate, upward):
    sigmoid = 1.0 / (1.0 + jnp.exp(-gate))
    silu = gate * sigmoid
    return silu * upward, upward * sigmoid * (1.0 + gate * (1.0 - sigmoid)), silu


def forward_kernel(far, main, micro, *refs):
    gain_src, attn_src, ffn_src, hid_src, cot_src, cosine, sine, kpos, rowinfo = refs[:9]
    (
        gain_rows,
        lse,
        middle,
        act,
        slope,
        mixed,
        queries,
        kvs,
        n1_out,
        attn_out,
        n2_out,
        gu_out,
        down_out,
        cot_out,
    ) = refs[9:23]
    gains, attn_w, gu_w, down_w, hid, n1, n2, bias, ratios, part, land, summ, across = refs[23:36]
    links = Links(*refs[36:])
    count = hid_src.shape[0]
    rows = count // micro
    span_chips = kvs.shape[0]
    greet(
        [CORE, TENSOR, (LOW, True, False)] + chips_apart(LOW, *far) + chips_apart(*range(1, span_chips))
    )
    attn_cols, gu_cols, down_cols = attn_w.shape[1], gu_w.shape[1], down_w.shape[1]
    total = gu_cols + down_cols
    height = attn_src.shape[0]

    def core_column(start):
        return lambda low, core: core * attn_cols + start

    def group_column(start):
        return lambda low, core: (low * 2 + core) * total + start

    spreads = [
        Spread(links, gain_src, lambda low, core: 0, gains, gain_src.shape[0], 0, 128, far)
    ]
    n_q = queries.shape[1]
    n_qkv = n_q + 128
    for base, tiles, parts in ((0, n_qkv // 128, 2), (n_qkv, n_q // 128, 2)):
        for start, cols in cuts(base, tiles, parts):
            spreads.append(
                Spread(links, attn_src, core_column(start), attn_w, height, start, cols, far)
            )
        if base == 0:
            qkv_spreads = len(spreads)
    attn_spreads = len(spreads)
    for start, cols in cuts(0, gu_cols // 128, 4):
        spreads.append(Spread(links, ffn_src, group_column(start), gu_w, height, start, cols, far))
    gu_spreads = len(spreads)
    for start, cols in cuts(0, down_cols // 128, 2):
        spreads.append(
            Spread(links, ffn_src, group_column(gu_cols + start), down_w, height, start, cols, far)
        )
    attn = spreads[:attn_spreads]
    gu = spreads[attn_spreads:gu_spreads]
    down = spreads[gu_spreads:]
    for spread in attn:
        spread.begin()
    own_hid = links.copy(hid_src, hid.at[pl.ds(0, count)])
    side_hid = links.push(hid_src, hid.at[pl.ds(count, count)], peer(core=True))
    tokens = TokenSpread(links, cot_src, cot_out)
    own_hid.wait()
    side_hid.wait_recv()

    def first_ratio(start):
        span = pl.ds(start, 64)
        value = hid[span].astype(F32)
        ratio = lax.rsqrt(jnp.mean(value * value, axis=-1, keepdims=True) + epsilon)
        ratios[span] = jnp.broadcast_to(ratio, (64, 128))

    by_rows(0, 2 * count, 64, first_ratio)
    for spread in attn:
        spread.launch()
    for spread in gu[:2]:
        spread.begin()
    tokens.begin()
    spreads[0].forward()

    spreads[0].finish()
    n_units = 2 ** len(far)
    own_block = gain_rows.shape[1] // (4 * n_units)
    both_gains = gains[...].astype(F32)
    for place in range(4 * n_units):
        gain_rows[0:2, place * own_block : (place + 1) * own_block] = both_gains[
            place * 16 : place * 16 + 2, :own_block
        ]

    def first_norm(start):
        span = pl.ds(start, 64)
        n1[span] = (hid[span].astype(F32) * ratios[span, 0:1] * gain_rows[0:1]).astype(BF)

    by_rows(0, 2 * count, 64, first_norm)
    outs = [links.copy(n1, n1_out)]
    for spread in spreads[1:qkv_spreads]:
        spread.forward()
    for spread in spreads[1:qkv_spreads]:
        spread.finish()

    def project(start):
        span = pl.ds(start, 256)
        raw = dot_plain(n1[span], attn_w[:, 0:n_qkv])
        cos, sin = cosine[span], sine[span]
        queries[span] = (turn(raw[:, :n_q], cos, sin, False) * HEAD_DIM ** (-0.5)).astype(BF)
        pair = raw[:, n_q:]
        lane = lax.broadcasted_iota(jnp.int32, pair.shape, 1)
        kvs[0, span] = jnp.where(lane < HEAD_DIM, turn(pair, cos, sin, False), pair).astype(BF)

    by_rows(0, 2 * count, 256, project)
    came = [
        links.push(kvs.at[0], kvs.at[key], peer(key)) for key in range(1, span_chips)
    ]
    for spread in gu[2:] + down:
        spread.begin()
    gu[0].launch()
    spreads[qkv_spreads].forward()
    gu[1].launch()
    for copy in came:
        copy.wait_recv()

    tokens.second()
    half = []
    for m in range(micro):
        own, other = pl.ds(m * rows, rows), pl.ds(count + m * rows, rows)
        bias[...] = mask_bias(kpos[...], rowinfo[m])
        kv = jnp.concatenate(
            [kvs[key, span] for key in range(span_chips) for span in (own, other)], axis=0
        )
        q_both = jnp.concatenate([queries[own], queries[other]], axis=0)
        mixed_t, sums = attend(bias, q_both, kv)
        lse[m] = sums
        value = mixed_t.T.astype(BF)
        mixed[own] = value[:rows]
        mixed[other] = value[rows:]
        if m == 0:
            for spread in spreads[qkv_spreads + 1 : attn_spreads]:
                spread.forward()
            for spread in spreads[qkv_spreads:attn_spreads]:
                spread.finish()
            outs.append(links.copy(attn_w, attn_out))
        out_w = attn_w.at[:, pl.ds(n_qkv, n_q)]
        term = dot_last(value, out_w[...])
        part[own] = term[rows:].astype(BF)
        side = links.push(part.at[own], land.at[own], peer(core=True))
        side.wait_recv()
        summ[own] = (term[:rows] + land[own].astype(F32)).astype(BF)
        half.append(links.push(summ.at[own], across.at[own], peer(tensor=True)))
        if m == 0:
            for spread in gu[2:]:
                spread.launch()
        if m == 1:
            gu[0].forward()
    for spread in down:
        spread.launch()
    gu[1].forward()
    tokens.third()

    def finish(start):
        span = pl.ds(start, 32)
        value = hid[span].astype(F32) + summ[span].astype(F32) + across[span].astype(F32)
        middle[span] = value
        ratio = lax.rsqrt(jnp.mean(value * value, axis=-1, keepdims=True) + epsilon)
        n2[span] = (value * ratio * gain_rows[1:2]).astype(BF)

    low = []
    for m in range(micro):
        half[m].wait_recv()
        by_rows(m * rows, rows, 32, finish)
        low.append(
            links.push(
                n2.at[pl.ds(m * rows, rows)], n2.at[pl.ds(2 * count + m * rows, rows)], peer(LOW)
            )
        )
    own_n2 = links.push(n2.at[pl.ds(0, count)], n2.at[pl.ds(count, count)], peer(core=True))
    gu[2].forward()
    gu[3].forward()
    for spread in spreads[attn_spreads:gu_spreads]:
        spread.finish()

    def gates(start):
        span = pl.ds(start, 256)
        raw = dot_plain(n2[span], gu_w[...])
        parts = silu_parts(raw[:, :main], raw[:, main : 2 * main])
        last = raw[:, 2 * main :]
        lane = lax.broadcasted_iota(jnp.int32, last.shape, 1)
        ends = silu_parts(last, pltpu.roll(last, 64, 1))
        for ref, base, body, end in (
            (act, 0, parts[0], ends[0]),
            (slope, 0, parts[1], ends[1]),
            (slope, main + 128, parts[2], ends[2]),
        ):
            ref[span, base : base + main] = body.astype(BF)
            ref[span, base + main : base + main + 128] = jnp.where(lane < 64, end, 0.0).astype(BF)

    own_n2.wait_recv()
    by_rows(0, 2 * count, 256, gates)
    for copy in low:
        copy.wait_recv()
    both = links.push(
        n2.at[pl.ds(2 * count, count)], n2.at[pl.ds(3 * count, count)], peer(core=True)
    )
    down[0].forward()
    outs.append(links.copy(gu_w, gu_out))
    both.wait_recv()
    outs.append(links.copy(n2, n2_out))
    by_rows(2 * count, 2 * count, 256, gates)
    down[1].forward()
    for spread in spreads[gu_spreads:]:
        spread.finish()
    outs.append(links.copy(down_w, down_out))
    tokens.wait()
    for copy in outs:
        copy.wait()
    links.close()


def forward(far, main, micro, span_chips, sources, tables):
    gain_pack, attn_pack, ffn_pack, hidden, cotangent = sources
    count, width = hidden.shape
    attn_cols = attn_pack.shape[1] // 2
    gu_cols, down_cols = 2 * main + 128, main + 128
    n_q = (attn_cols - 128) // 2
    group = 4 * count
    heads = n_q // HEAD_DIM
    span, tokens = tables[2].shape[0], tables[3].shape[2]

    def low(*shape):
        return jax.ShapeDtypeStruct(shape, BF)

    shapes = [
        jax.ShapeDtypeStruct((8, width), F32),
        jax.ShapeDtypeStruct((micro, heads, tokens), F32),
        jax.ShapeDtypeStruct((count, width), F32),
        low(group, down_cols),
        low(group, 2 * down_cols),
        low(2 * count, n_q),
        low(2 * count, n_q),
        low(span_chips, 2 * count, 128),
        low(2 * count, width),
        low(width, attn_cols),
        low(group, width),
        low(width, gu_cols),
        low(width, down_cols),
        low(3 * count, width),
    ]
    return pl.pallas_call(
        functools.partial(forward_kernel, far, main, micro),
        in_specs=[ANY] * 5 + [VMEM] * 4,
        out_specs=[VMEM] * 8 + [ANY] * 6,
        out_shape=shapes,
        scratch_shapes=[
            pltpu.VMEM((2 ** len(far) * 4 * gain_pack.shape[0], 128), BF),
            pltpu.VMEM((width, attn_cols), BF),
            pltpu.VMEM((width, gu_cols), BF),
            pltpu.VMEM((width, down_cols), BF),
            pltpu.VMEM((2 * count, width), BF),
            pltpu.VMEM((2 * count, width), BF),
            pltpu.VMEM((group, width), BF),
            pltpu.VMEM((span, tokens), F32),
            pltpu.VMEM((2 * count, 128), F32),
        ]
        + [pltpu.VMEM((count, width), BF)] * 4
        + link_scratch(256, 32),
        compiler_params=pltpu.CompilerParams(
            collective_id=0, has_side_effects=True, vmem_limit_bytes=VMEM_BIG
        ),
        name="forward",
    )(*sources, *tables)


class Collect:
    TILE = 256

    def __init__(self, links, far, width, sent, came, held, came_far, total, more):
        self.links, self.far, self.half = links, far, width // 2
        self.sent, self.came, self.held, self.came_far = sent, came, held, came_far
        self.total, self.more = total, more
        self.tiles = self.half // self.TILE
        self.arrivals = {}

    def send_half(self, name, job, which=None):
        columns, left, right = job
        tiles, tile = self.tiles, self.TILE
        if which is None:
            which = [i for i in range(tiles // 2, tiles)] + [i for i in range(tiles // 2)]
        for i in which:
            rows = pl.ds(i * tile, tile)
            start = self.half + i * tile
            self.sent[rows, columns] = dot_first(left[:, start : start + tile], right[...]).astype(
                BF
            )
            self.arrivals[name, i] = self.links.push(
                self.sent.at[rows, columns], self.came.at[rows, columns], peer(self.far[-1])
            )

    def own_half(self, name, job, which):
        columns, left, right = job
        tiles, tile = self.tiles, self.TILE
        for i in which:
            rows = pl.ds(i * tile, tile)
            self.arrivals[name, i].wait_recv()
            term = dot_first(left[:, i * tile : (i + 1) * tile], right[...])
            term = term + self.came[rows, columns].astype(F32)
            if i >= tiles // 2:
                place = pl.ds((i - tiles // 2) * tile, tile)
                self.held[place, columns] = term.astype(BF)
                self.arrivals[name, "far", i - tiles // 2] = self.links.push(
                    self.held.at[place, columns],
                    self.came_far.at[place, columns],
                    peer(self.far[-2]),
                )
            else:
                self.total[rows, columns] = term

    def upper(self):
        return range(self.tiles // 2, self.tiles)

    def lower(self):
        return range(self.tiles // 2)

    def finish(self, name, job):
        columns = job[0]
        for i in self.lower():
            rows = pl.ds(i * self.TILE, self.TILE)
            self.arrivals[name, "far", i].wait_recv()
            self.total[rows, columns] = self.total[rows, columns] + self.came_far[
                rows, columns
            ].astype(F32)

    def finish_more(self):
        kept = self.half // 2
        for bit, (sent, came) in zip(self.far[-3::-1], self.more):
            kept //= 2
            sent[...] = self.total[pl.ds(kept, kept)].astype(BF)
            copy = self.links.push(sent, came, peer(bit))
            copy.wait_recv()
            self.total[pl.ds(0, kept)] = self.total[pl.ds(0, kept)] + came[...].astype(F32)


def collect_scratch(far, width, cols):
    shapes = [
        pltpu.VMEM((width // 2, cols), BF),
        pltpu.VMEM((width // 2, cols), BF),
        pltpu.VMEM((width // 4, cols), BF),
        pltpu.VMEM((width // 4, cols), BF),
    ]
    kept = width // 4
    for _ in far[2:]:
        kept //= 2
        shapes += [pltpu.VMEM((kept, cols), BF)] * 2
    return shapes


def paired(refs):
    return [(refs[i], refs[i + 1]) for i in range(0, len(refs), 2)]


class GroupSum:
    def __init__(self, links, count, width, chunks, term, part, land, low_part, land_low, summ, across):
        self.links, self.count, self.term = links, count, term
        self.part, self.land, self.low_part, self.land_low = part, land, low_part, land_low
        self.summ, self.across = summ, across
        size = width // chunks
        self.spans = [pl.ds(i * size, size) for i in range(chunks)]
        self.flight = {}

    def outer(self, slot):
        rows = pl.ds((slot // 2) * self.count, self.count)
        own = pl.ds(0, self.count)
        if slot == 1:
            self.links.settle([self.flight[3, i] for i in range(len(self.spans))])
        for i, span in enumerate(self.spans):
            self.part[own, span] = self.term(slot, span).astype(BF)
            self.flight[slot, i] = self.links.push(
                self.part.at[own, span], self.land.at[rows, span], peer(core=True)
            )

    def to_low(self):
        for i, span in enumerate(self.spans):
            value = self.term(2, span)
            self.flight[3, i].wait_recv()
            value = value + self.land[pl.ds(self.count, self.count), span].astype(F32)
            self.low_part[:, span] = value.astype(BF)
            self.flight["low", i] = self.links.push(
                self.low_part.at[:, span], self.land_low.at[:, span], peer(LOW)
            )

    def to_half(self, which=None):
        for i, span in enumerate(self.spans):
            if which is not None and i not in which:
                continue
            value = self.term(0, span)
            self.flight["low", i].wait_recv()
            self.flight[1, i].wait_recv()
            value = value + self.land[pl.ds(0, self.count), span].astype(F32)
            value = value + self.land_low[:, span].astype(F32)
            self.summ[:, span] = value.astype(BF)
            self.flight["half", i] = self.links.push(
                self.summ.at[:, span], self.across.at[:, span], peer(tensor=True)
            )

    def wait(self):
        for i in range(len(self.spans)):
            self.flight["half", i].wait_recv()


def group_sum_scratch(count, width):
    return [
        pltpu.VMEM((count, width), BF),
        pltpu.VMEM((2 * count, width), BF),
        pltpu.VMEM((count, width), BF),
        pltpu.VMEM((count, width), BF),
    ]


def ffn_backward_kernel(far, main, *refs):
    own_in, cot_in, act_in, down_in, slope_in, n2_in, gu_in = refs[:7]
    summ, across, own_out, other_out = refs[7:11]
    cot, act, down_w, slope, n2, gu_w = refs[11:17]
    part, land, low_part, land_low = refs[17:21]
    total, sent, came, held, came_far = refs[21:26]
    more = paired(refs[26:-3])
    links = Links(*refs[-3:])
    loads = [
        links.copy(src, dst)
        for src, dst in (
            (cot_in, cot.at[pl.ds(own_in.shape[0], cot_in.shape[0])]),
            (act_in, act),
            (down_in, down_w),
            (slope_in, slope),
            (n2_in, n2),
            (gu_in, gu_w),
        )
    ]
    own_load = links.copy(own_in, cot.at[pl.ds(0, own_in.shape[0])])
    greet([CORE, TENSOR] + chips_apart(LOW, *far))
    group, width = cot.shape
    count = group // 4
    down_cols, gu_cols = down_w.shape[1], gu_w.shape[1]
    grads = slope.at[:, pl.ds(0, gu_cols)]
    down_job = (pl.ds(0, down_cols), cot, act)
    gu_job = (pl.ds(down_cols, gu_cols), n2, grads)
    collect = Collect(links, far, width, sent, came, held, came_far, total, more)

    own_load.wait()
    loads[0].wait()
    loads[1].wait()
    upper, lower = list(collect.upper()), list(collect.lower())
    collect.send_half("d", down_job, upper)
    loads[2].wait()
    loads[3].wait()
    lane = lax.broadcasted_iota(jnp.int32, (256, 128), 1)

    def slopes(start):
        span = pl.ds(start, 256)
        grad_act = dot_plain(cot[span], down_w[...])
        gate = grad_act * slope[span, 0:down_cols].astype(F32)
        upward = grad_act * slope[span, down_cols : 2 * down_cols].astype(F32)
        slope[span, 0:main] = gate[:, :main].astype(BF)
        slope[span, main : 2 * main] = upward[:, :main].astype(BF)
        last = jnp.where(lane < 64, gate[:, main:], pltpu.roll(upward[:, main:], 64, 1))
        slope[span, 2 * main : 2 * main + 128] = last.astype(BF)

    by_rows(0, group, 256, slopes)
    loads[4].wait()
    collect.send_half("g", gu_job, upper)

    loads[5].wait()

    def term(slot, span):
        return dot_last(slope[pl.ds(slot * count, count), 0:gu_cols], gu_w[span])

    sums = GroupSum(
        links, count, width, 4, term, part, land, low_part, land_low, summ, across
    )
    sums.outer(3)
    collect.own_half("d", down_job, upper)
    sums.to_low()
    sums.outer(1)
    collect.send_half("d", down_job, lower)
    collect.send_half("g", gu_job, lower)
    collect.own_half("g", gu_job, upper[:1])
    sums.to_half([0, 1])
    collect.own_half("g", gu_job, upper[1:])
    sums.to_half([2, 3])
    collect.own_half("d", down_job, lower)
    collect.own_half("g", gu_job, lower)
    collect.finish("d", down_job)
    collect.finish("g", gu_job)
    collect.finish_more()
    half_unit = own_out.shape[0]
    low = low_bit()
    own_out[...] = total[pl.ds(pl.multiple_of(low * half_unit, half_unit), half_unit)]
    other_out[...] = total[
        pl.ds(pl.multiple_of((1 - low) * half_unit, half_unit), half_unit)
    ].astype(BF)
    sums.wait()
    links.close()


def ffn_backward(far, main, own, cot, act, down_w, slope, n2, gu_w):
    group, width = n2.shape
    count = group // 4
    cols = gu_w.shape[1] + down_w.shape[1]
    inputs = (own, cot, act, down_w, slope, n2, gu_w)
    return pl.pallas_call(
        functools.partial(ffn_backward_kernel, far, main),
        in_specs=[ANY] * 7,
        out_specs=[VMEM] * 4,
        out_shape=[
            jax.ShapeDtypeStruct((count, width), BF),
            jax.ShapeDtypeStruct((count, width), BF),
            jax.ShapeDtypeStruct((width // 2 ** (len(far) + 1), cols), F32),
            jax.ShapeDtypeStruct((width // 2 ** (len(far) + 1), cols), BF),
        ],
        scratch_shapes=[pltpu.VMEM((group, width), BF)]
        + [pltpu.VMEM(a.shape, BF) for a in inputs[2:]]
        + group_sum_scratch(count, width)
        + [pltpu.VMEM((width // 4, cols), F32)]
        + collect_scratch(far, width, cols)
        + link_scratch(128, 32),
        compiler_params=pltpu.CompilerParams(
            collective_id=2, has_side_effects=True, vmem_limit_bytes=VMEM_BIG
        ),
        name="ffn_backward",
    )(*inputs)


def finale_kernel(far, micro, *refs):
    (
        gain_rows,
        middle_in,
        cot_in,
        grad_two_in,
        across_two_in,
        hid_in,
        cos_in,
        sin_in,
        kpos,
        rowinfo,
        queries_in,
        lse,
        kvs_in,
        attn_in,
        n1_in,
        mixed_in,
        act_in,
        down_in,
        ffn_own,
        ffn_other,
    ) = refs[:20]
    (
        grad_middle,
        summ,
        across,
        feed,
        feed_across,
        attn_mine,
        attn_came,
        gains,
        ffn_core,
        ffn_low,
        ffn_low_core,
    ) = refs[20:31]
    attn_w, n1, mixed, gmid, raw = refs[31:36]
    dkv_own, dkv_sent, dkv_land, side, land_side = refs[36:41]
    low_sent, low_land = refs[41:43]
    near_gains, far_gains, low_gains, core_gains = refs[43:47]
    part, land, land_low = refs[47:50]
    total, sent, came, held, came_far = refs[50:55]
    queries, kvs, cosine, sine, bias, dk, dv, act, down_w = refs[55:64]
    more = paired(refs[64:-3])
    go = raw.at[:, pl.ds(0, mixed.shape[1])]
    links = Links(*refs[-3:])
    loads = [
        links.copy(src, dst)
        for src, dst in (
            (middle_in, grad_middle),
            (cot_in, summ),
            (grad_two_in, feed),
            (across_two_in, part),
            (attn_in, attn_w),
            (mixed_in, mixed),
            (n1_in, n1),
        )
    ]
    span_chips = kvs_in.shape[0]
    greet([CORE, TENSOR] + chips_apart(LOW, *far) + chips_apart(*range(1, span_chips)))
    count, width = grad_middle.shape
    rows = count // micro
    n_q = queries_in.shape[1]
    n_qkv = n_q + 128
    low, core = low_bit(), core_bit()
    block = ffn_own.shape[0] // 2

    def core_rows(which):
        return pl.ds(pl.multiple_of(which * block, block), block)

    ffn_flight = [
        links.push(ffn_other, ffn_low, peer(LOW)),
        links.push(ffn_own.at[core_rows(1 - core)], ffn_core, peer(core=True)),
    ]

    for load in loads[:4]:
        load.wait()
    near_gains[...] = jnp.zeros_like(near_gains)

    def second_norm(start):
        span = pl.ds(start, 64)
        grad = feed[span].astype(F32) + part[span].astype(F32)
        value = grad_middle[span]
        ratio = lax.rsqrt(jnp.mean(value * value, axis=-1, keepdims=True) + epsilon)
        turned = value * ratio
        near_gains[1:2] += jnp.sum(grad * turned, axis=0, keepdims=True)
        scaled = grad * gain_rows[1:2]
        inner = jnp.mean(scaled * turned, axis=-1, keepdims=True)
        result = summ[span].astype(F32) + ratio * (scaled - turned * inner)
        grad_middle[span] = result
        gmid[span] = result.astype(BF)

    by_rows(0, count, 64, second_norm)
    own = links.push(gmid.at[pl.ds(0, count)], gmid.at[pl.ds(count, count)], peer(core=True))
    collect = Collect(links, far, width, sent, came, held, came_far, total, more)
    out_job = (pl.ds(n_qkv, n_q), gmid, mixed)
    qkv_job = (pl.ds(0, n_qkv), n1, raw)
    upper, lower = list(collect.upper()), list(collect.lower())
    loads[4].wait()
    loads[5].wait()

    def mixed_back(start):
        span = pl.ds(start, 128)
        go[span] = dot_plain(gmid[span], attn_w[:, n_qkv : n_qkv + n_q]).astype(BF)

    by_rows(0, count, 128, mixed_back)
    own.wait_recv()
    by_rows(count, count, 128, mixed_back)
    collect.send_half("o", out_job, upper)
    collect.send_half("o", out_job, lower)

    def attention():
        scoped = [
            links.copy(src, dst)
            for src, dst in (
                (queries_in, queries),
                (kvs_in, kvs),
                (cos_in, cosine),
                (sin_in, sine),
            )
        ]
        for load in scoped:
            load.wait()
        for m in range(micro):
            mine, other = pl.ds(m * rows, rows), pl.ds(count + m * rows, rows)
            bias[...] = mask_bias(kpos[...], rowinfo[m])

            def both(ref):
                return jnp.concatenate([ref[mine], ref[other]], axis=0)

            kv = jnp.concatenate(
                [kvs[key, span] for key in range(span_chips) for span in (mine, other)], axis=0
            )
            grad_q = attend_back(bias, both(queries), both(go), lse[m], kv, dk, dv)
            grad_q = turn(grad_q, both(cosine), both(sine), True).astype(BF)
            raw[mine, 0:n_q] = grad_q[:rows]
            raw[other, 0:n_q] = grad_q[rows:]
            for key in range(span_chips):
                for place, span in ((0, mine), (rows, other)):
                    at = pl.ds(key * 2 * rows + place, rows)
                    pair = jnp.concatenate([dk[at], dv[at]], axis=1)
                    if key == 0:
                        dkv_own[span] = pair
                    else:
                        dkv_sent[key - 1, span] = pair.astype(BF)
        flight = [
            links.push(dkv_sent.at[key - 1], dkv_land.at[key - 1], peer(key))
            for key in range(1, span_chips)
        ]
        collect.own_half("o", out_job, upper)
        for copy in flight:
            copy.wait_recv()

        def key_values(start):
            span = pl.ds(start, 256)
            pair = dkv_own[span]
            for key in range(span_chips - 1):
                pair = pair + dkv_land[key, span].astype(F32)
            lane = lax.broadcasted_iota(jnp.int32, pair.shape, 1)
            turned = turn(pair, cosine[span], sine[span], True)
            raw[span, n_q:n_qkv] = jnp.where(lane < HEAD_DIM, turned, pair).astype(BF)

        by_rows(0, 2 * count, 256, key_values)

    attention()

    loads[6].wait()
    collect.send_half("q", qkv_job, upper)
    collect.send_half("q", qkv_job, lower)
    spans = [pl.ds(i * (width // 4), width // 4) for i in range(4)]
    to_core = []
    for span in spans:
        side[:, span] = dot_last(raw[pl.ds(count, count)], attn_w[span, 0:n_qkv]).astype(BF)
        to_core.append(links.push(side.at[:, span], land_side.at[:, span], peer(core=True)))
    over = []
    for i, span in enumerate(spans):
        value = dot_last(raw[pl.ds(0, count)], attn_w[span, 0:n_qkv])
        to_core[i].wait_recv()
        summ[:, span] = (value + land_side[:, span].astype(F32)).astype(BF)
        over.append(links.push(summ.at[:, span], across.at[:, span], peer(tensor=True)))
    load_hid = links.copy(hid_in, land_side)

    def feed_sums():
        scoped = [links.copy(act_in, act), links.copy(down_in, down_w)]
        collect.own_half("q", qkv_job, upper)
        collect.own_half("o", out_job, lower)
        for load in scoped:
            load.wait()

        def term(slot, span):
            return dot_last(act[pl.ds(slot * count, count)], down_w[span])

        sums = GroupSum(
            links, count, width, 4, term, part, land, side, land_low, feed, feed_across
        )
        links.settle(to_core)
        sums.outer(3)
        sums.to_low()
        sums.outer(1)
        collect.own_half("q", qkv_job, lower)
        sums.to_half()
        return sums

    sums = feed_sums()
    collect.finish("o", out_job)
    collect.finish("q", qkv_job)
    collect.finish_more()

    half_unit = attn_mine.shape[0] * 2

    def low_rows(which):
        return pl.ds(pl.multiple_of(which * half_unit, half_unit), half_unit)

    low_sent[...] = total[low_rows(1 - low)].astype(BF)
    low_flight = links.push(low_sent, low_land, peer(LOW))

    for copy in over:
        copy.wait_recv()
    load_hid.wait()

    def first_norm(start):
        span = pl.ds(start, 64)
        value = land_side[span].astype(F32)
        ratio = lax.rsqrt(jnp.mean(value * value, axis=-1, keepdims=True) + epsilon)
        grad = summ[span].astype(F32) + across[span].astype(F32)
        near_gains[0:1] += jnp.sum(grad * value * ratio, axis=0, keepdims=True)

    by_rows(0, count, 64, first_norm)
    kept, base = width, 0
    for bit in far[::-1]:
        kept //= 2
        landed = far_gains.at[:, pl.ds(base, kept)]
        copy = links.push(near_gains.at[:, pl.ds(kept, kept)], landed, peer(bit))
        copy.wait_recv()
        near_gains[:, 0:kept] = near_gains[:, 0:kept] + landed[...]
        base += kept
    copy = links.push(near_gains.at[:, pl.ds(0, kept)], low_gains, peer(LOW))
    ffn_flight[0].wait_recv()
    ffn_flight.append(
        links.push(ffn_low.at[core_rows(1 - core)], ffn_low_core, peer(core=True))
    )
    copy.wait_recv()
    gains[...] = near_gains[:, 0:kept] + low_gains[...]
    copy = links.push(gains, core_gains, peer(core=True))

    low_flight.wait_recv()
    own_unit = total[low_rows(low)] + low_land[...].astype(F32)
    total[0:half_unit] = own_unit
    core_flight = links.push(total.at[core_rows(1 - core)], attn_came, peer(core=True))
    attn_mine[...] = total[core_rows(core)]
    copy.wait_recv()
    core_flight.wait_recv()
    for flight in ffn_flight[1:]:
        flight.wait_recv()
    sums.wait()
    links.close()
    gains[...] = gains[...] + core_gains[...]


def finale(far, micro, inputs):
    (
        gain_rows,
        middle,
        cot,
        grad_two,
        across_two,
        hid,
        cosine,
        sine,
        kpos,
        rowinfo,
        queries,
        lse,
        kvs,
        attn_w,
        n1,
        mixed,
        act,
        down_w,
        ffn_own,
        ffn_other,
    ) = inputs
    count, width = middle.shape
    n_q = mixed.shape[1]
    attn_cols, ffn_cols = attn_w.shape[1], ffn_own.shape[1]
    unit = width // 2 ** len(far)
    block = unit // 4
    span_chips = kvs.shape[0]

    def shape(dtype, *dims):
        return jax.ShapeDtypeStruct(dims, dtype)

    rows = shape(BF, count, width)
    any_or_vmem = [VMEM] + [ANY] * 7 + [VMEM] * 2 + [ANY] + [VMEM] + [ANY] * 8
    return pl.pallas_call(
        functools.partial(finale_kernel, far, micro),
        in_specs=any_or_vmem,
        out_specs=[VMEM] * 6 + [ANY, VMEM] + [ANY] * 3,
        out_shape=[
            shape(F32, count, width),
            rows,
            rows,
            rows,
            rows,
            shape(F32, block, attn_cols),
            shape(F32, block, attn_cols),
            shape(F32, 8, unit),
            shape(F32, block, ffn_cols),
            shape(BF, 2 * block, ffn_cols),
            shape(BF, block, ffn_cols),
        ],
        scratch_shapes=[
            pltpu.VMEM((width, attn_cols), BF),
            pltpu.VMEM((2 * count, width), BF),
            pltpu.VMEM((2 * count, n_q), BF),
            pltpu.VMEM((2 * count, width), BF),
            pltpu.VMEM((2 * count, n_q + 128), BF),
            pltpu.VMEM((2 * count, 128), F32),
            pltpu.VMEM((span_chips - 1, 2 * count, 128), BF),
            pltpu.VMEM((span_chips - 1, 2 * count, 128), BF),
            pltpu.VMEM((count, width), BF),
            pltpu.VMEM((count, width), BF),
            pltpu.VMEM((2 * block, attn_cols), BF),
            pltpu.VMEM((2 * block, attn_cols), BF),
            pltpu.VMEM((8, width), F32),
            pltpu.VMEM((8, width), F32),
            pltpu.VMEM((8, unit), F32),
            pltpu.VMEM((8, unit), F32),
        ]
        + group_sum_scratch(count, width)[:3]
        + [pltpu.VMEM((width // 4, attn_cols), F32)]
        + collect_scratch(far, width, attn_cols)[:4]
        + [
            pltpu.VMEM(queries.shape, BF),
            pltpu.VMEM(kvs.shape, BF),
            pltpu.VMEM(cosine.shape, F32),
            pltpu.VMEM(sine.shape, F32),
            pltpu.VMEM((kpos.shape[0], rowinfo.shape[2]), F32),
            pltpu.VMEM((kpos.shape[0], HEAD_DIM), F32),
            pltpu.VMEM((kpos.shape[0], HEAD_DIM), F32),
            pltpu.VMEM(act.shape, BF),
            pltpu.VMEM(down_w.shape, BF),
        ]
        + collect_scratch(far, width, attn_cols)[4:]
        + link_scratch(192, 32),
        compiler_params=pltpu.CompilerParams(
            collective_id=3, has_side_effects=True, vmem_limit_bytes=VMEM_BIG
        ),
        name="finale",
    )(*inputs)


def body(
    tokens,
    doc_position,
    attn_gain,
    w_query,
    w_key,
    w_value,
    w_out,
    ffn_gain,
    w_gate,
    w_up,
    w_down,
    cotangent,
):
    size = lax.axis_size("dp")
    chips = size // 2
    far = [1 << place for place in range(chips.bit_length() - 1) if 1 << place != LOW][::-1]
    me = lax.axis_index("dp")
    core = me % 2
    chip = me // 2
    low = (chip // LOW) % 2
    micro, stretch, width = tokens.shape
    count = micro * stretch
    block = width // chips
    own_block = block // 2
    span_chips = SEQ_LEN // (2 * stretch)
    in_span = chip % span_chips

    keys = [0]
    for bit in far:
        keys = keys + [key | bit for key in keys]

    def rearranged(array):
        base = chip - LOW * low
        return jnp.concatenate(
            [
                lax.dynamic_slice_in_dim(
                    array, ((base ^ key) + LOW * side) * block, block, array.ndim - 1
                )
                for key in keys
                for side in range(2)
            ],
            axis=-1,
        )

    def restored(array):
        unit_of = jnp.array([keys.index(other & ~LOW) for other in range(chips)], jnp.int32)
        return jnp.concatenate(
            [
                lax.dynamic_slice_in_dim(
                    array,
                    (unit_of[chip ^ natural] * 2 + (natural // LOW) % 2) * block,
                    block,
                    array.ndim - 1,
                )
                for natural in range(chips)
            ],
            axis=-1,
        )

    def halves(array):
        n = array.shape[1] // 2
        return array[:, :n], array[:, n:]

    attn_pack = jnp.concatenate(
        [
            halves(w)[side]
            for side in range(2)
            for w in (w_query, w_key, w_value, w_out.T)
        ],
        axis=1,
    )
    hidden_units = w_gate.shape[1] // 4
    main = hidden_units // 128 * 128
    rest = hidden_units - main
    assert rest == 64

    def mains(array, place):
        return array[:, place * main : (place + 1) * main]

    def rests(array, place):
        return array[:, 4 * main + place * rest : 4 * main + (place + 1) * rest]

    w_down_t = w_down.T
    empty = jnp.zeros((own_block, 128 - rest), BF)
    ffn_pack = jnp.concatenate(
        [
            piece
            for place in range(4)
            for piece in (
                mains(w_gate, place),
                mains(w_up, place),
                rests(w_gate, place),
                rests(w_up, place),
                mains(w_down_t, place),
                rests(w_down_t, place),
                empty,
            )
        ],
        axis=1,
    )
    gain_pack = jnp.zeros((16, 128), BF).at[0, :own_block].set(attn_gain)
    gain_pack = gain_pack.at[1, :own_block].set(ffn_gain)
    hidden = rearranged(tokens.reshape(count, width))
    grad_final = rearranged(cotangent.reshape(count, width))

    hidden_f = hidden.astype(F32)
    position_both = jnp.stack([doc_position, swap_core(doc_position)])

    power = jnp.arange(HEAD_DIM // 2, dtype=F32) * (2.0 / HEAD_DIM)
    inverse = 10000.0 ** (-power)
    turned = position_both.reshape(2 * count).astype(F32)[:, None] * jnp.tile(inverse, 4)[None, :]
    cosine, sine = jnp.cos(turned), jnp.sin(turned)

    inner = jnp.arange(2 * stretch, dtype=jnp.int32) ^ (core * stretch)
    row_place = in_span * (2 * stretch) + inner
    kpos = jnp.concatenate(
        [(in_span ^ key) * (2 * stretch) + inner for key in range(span_chips)]
    ).reshape(-1, 1)
    row_position = position_both.transpose(1, 0, 2).reshape(micro, 2 * stretch)
    row_places = jnp.broadcast_to(row_place[None, :], row_position.shape)
    rowinfo = jnp.stack([row_places, row_places - row_position], axis=1)

    n_q = w_query.shape[1] // 2
    n_kv = w_key.shape[1] // 2
    n_qkv = n_q + 2 * n_kv
    (
        gain_rows,
        lse,
        middle,
        activated,
        slopes,
        mixed,
        queries,
        kvs,
        normed,
        attn_w,
        normed_two,
        gu_w,
        down_wt,
        grad_final_others,
    ) = forward(
        far,
        main,
        micro,
        span_chips,
        (gain_pack, attn_pack, ffn_pack, hidden, grad_final),
        (cosine, sine, kpos, rowinfo),
    )
    gain_one, gain_two = gain_rows[0:1], gain_rows[1:2]
    grad_two, grad_two_across, ffn_own, ffn_other = ffn_backward(
        far, main, grad_final, grad_final_others, activated, down_wt, slopes, normed_two, gu_w
    )
    (
        grad_middle,
        grad_one,
        grad_one_across,
        feed,
        feed_across,
        attn_mine,
        attn_came,
        grad_gains,
        ffn_core,
        ffn_low,
        ffn_low_core,
    ) = finale(
        far,
        micro,
        (
            gain_rows,
            middle,
            grad_final,
            grad_two,
            grad_two_across,
            hidden,
            cosine,
            sine,
            kpos,
            rowinfo,
            queries,
            lse,
            kvs,
            attn_w,
            normed,
            mixed,
            activated,
            down_wt,
            ffn_own,
            ffn_other,
        ),
    )
    output = restored((middle + (feed.astype(F32) + feed_across.astype(F32))).astype(BF))
    grad_normed = grad_one.astype(F32) + grad_one_across.astype(F32)
    ratio_one = lax.rsqrt(jnp.mean(hidden_f * hidden_f, axis=-1, keepdims=True) + epsilon)
    grad_in_norm = norm_back(grad_normed, hidden_f, ratio_one, gain_rows[0:1])
    grad_tokens = restored(grad_middle + grad_in_norm)
    grad_gains = lax.dynamic_slice_in_dim(grad_gains, (2 * low + core) * own_block, own_block, 1)

    def picked(pair, side):
        return jnp.where(side == 0, pair[0], pair[1]), jnp.where(side == 0, pair[1], pair[0])

    parts = picked((attn_mine, attn_came), core)

    def columns(start, stop):
        return jnp.concatenate([part[:, start:stop] for part in parts], axis=1)

    grad_w_query = columns(0, n_q)
    grad_w_key = columns(n_q, n_q + n_kv)
    grad_w_value = columns(n_q + n_kv, n_qkv)
    grad_w_out = columns(n_qkv, n_qkv + n_q).T

    def own_rows(array):
        return lax.dynamic_slice_in_dim(array, core * own_block, own_block, 0)

    mine_low = picked((own_rows(ffn_own), ffn_core), core)
    other_low = picked((own_rows(ffn_low).astype(F32), ffn_low_core.astype(F32)), core)
    by_low = [
        picked((mine_low[side], other_low[side]), low) for side in range(2)
    ]
    places = [by_low[place % 2][place // 2] for place in range(4)]
    down_cols = main + 128
    gu = down_cols

    def gathered(main_start, rest_start):
        return jnp.concatenate(
            [part[:, main_start : main_start + main] for part in places]
            + [part[:, rest_start : rest_start + rest] for part in places],
            axis=1,
        )

    grad_w_down = gathered(0, main).T
    grad_w_gate = gathered(gu, gu + 2 * main)
    grad_w_up = gathered(gu + main, gu + 2 * main + rest)
    return (
        output.reshape(tokens.shape),
        grad_tokens.reshape(tokens.shape),
        grad_gains[0],
        grad_w_query,
        grad_w_key,
        grad_w_value,
        grad_w_out,
        grad_gains[1],
        grad_w_gate,
        grad_w_up,
        grad_w_down,
    )


def solution(mesh):
    return jax.shard_map(
        body,
        mesh=mesh,
        in_specs=(
            P(None, "dp", None),
            P(None, "dp"),
            P("dp"),
            P("dp", "tensor"),
            P("dp", "tensor"),
            P("dp", "tensor"),
            P("tensor", "dp"),
            P("dp"),
            P("dp", "tensor"),
            P("dp", "tensor"),
            P("tensor", "dp"),
            P(None, "dp", None),
        ),
        out_specs=(
            P(None, "dp", None),
            P(None, "dp", None),
            P("dp"),
            P("dp", "tensor"),
            P("dp", "tensor"),
            P("dp", "tensor"),
            P("tensor", "dp"),
            P("dp"),
            P("dp", "tensor"),
            P("dp", "tensor"),
            P("tensor", "dp"),
        ),
        check_vma=False,
    )
```

time: 816 us -> 560 us (0.69)
  Pallas kernels: 580 us -> 478 us
  waiting for transfers between devices: 64.3 us -> 0.01 us
  other arithmetic: 48.9 us -> 14.2 us
  local copies, waits for them, and re-layouts: 75.3 us -> 54.8 us
  starting transfers between devices: 14.4 us -> 0.52 us
  between operations: 20.4 us -> 6.92 us
    pallas_call x6 -> x2, Pallas kernels: 423 us -> 355 us  [the longest x1 213 us: forward(): pl.pallas_call(functools.partial(forward_kernel, far, main, micro), in_sp...]
    unnamed x2 -> x0, waiting for transfers between devices: 41 us -> none
    pallas_call x1, Pallas kernels: 157 us -> 123 us  [ffn_backward(): pl.pallas_call(functools.partial(ffn_backward_kernel, far, main), in_spec...]
    ppermute x8 -> x0, waiting for transfers between devices: 23.4 us -> none  [swap_chip(): lax.ppermute(block, 'dp', [(i, i ^ 2 * distance) for i in range(size)])]
    unnamed x140 -> x115, local copies, waits for them, and re-layouts: 37.9 us -> 21.3 us
    ppermute x8 -> x0, starting transfers between devices: 13.7 us -> none  [swap_chip(): lax.ppermute(block, 'dp', [(i, i ^ 2 * distance) for i in range(size)])]
    convert_element_type x7 -> x0, other arithmetic: 10.3 us -> none  [the longest x1 3.51 us: body(): grad_middle_low = grad_middle.astype(BF)]
    reduce_sum x4 -> x1, other arithmetic: 10.8 us -> 2.57 us  [body(): jnp.mean(hidden_f * hidden_f, axis=-1, keepdims=True) + epsilon]
  transfers between devices with their start and end apart: 13 -> 1, of which waited for: 6 -> 0; matrix products, arithmetic and copies ran while one was open for 13% -> 6% of each run, Pallas kernels for 31% -> 0%
where the time goes in v4:
time: 560 us; the launch traced here: 554 us
  Pallas kernels  478 us (85%)
  local copies, waits for them, and re-layouts  54.8 us (10%)
  other arithmetic  14.2 us (3%)
  between operations  6.92 us (1%)
    pallas_call x1, Pallas kernels, forward(): pl.pallas_call(functools.partial(forward_kernel, far, main, micro), in_sp...  213 us
    pallas_call x1, Pallas kernels, finale(): pl.pallas_call(functools.partial(finale_kernel, far, micro), in_specs=any...  142 us
    pallas_call x1, Pallas kernels, ffn_backward(): pl.pallas_call(functools.partial(ffn_backward_kernel, far, main), in_spec...  123 us
    unnamed x115, local copies, waits for them, and re-layouts  21.3 us
  transfers between devices with their start and end apart: 1, of which 0 were waited for; matrix products, arithmetic and copies ran while one was open for 6% of the time, Pallas kernels for 0%

profile of v4, /device:TPU:0, one launch (start us, length us, event | category | flops | bytes accessed | tf_op | source)
XLA Modules:
  0.0 554.4 jit_solution(3583310392720762250)
XLA Ops:
  1.2 1.4 copy.31
  2.6 1.1 fusion.24
  11.9 1.1 dynamic-slice_dynamic-update-slice_fusion.23
  13.0 0.9 dynamic-slice_dynamic-update-slice_fusion.22
  13.9 0.9 dynamic-slice_dynamic-update-slice_fusion.30
  14.9 0.9 dynamic-slice_dynamic-update-slice_fusion.21
  15.9 0.9 dynamic-slice_dynamic-update-slice_fusion.29
  16.8 0.9 dynamic-slice_dynamic-update-slice_fusion.20
  17.8 0.9 dynamic-slice_dynamic-update-slice_fusion.28
  19.7 0.9 dynamic-slice_dynamic-update-slice_fusion.27
  21.6 0.9 dynamic-slice_dynamic-update-slice_fusion.26
  22.5 0.9 dynamic-slice_dynamic-update-slice_fusion.17
  23.5 0.9 dynamic-slice_dynamic-update-slice_fusion.25
  25.4 1.2 dynamic-slice_dynamic-update-slice_fusion.24.refs_3_.refs_5_
  26.6 1.3 copy.33.refs_7_.refs_8_
  27.9 1.1 copy.30
  29.1 1.8 fusion.33
  30.9 1.6 fusion.35
  33.8 2.0 concatenate.46.refs_1_
  35.8 4.8 concatenate.47.refs_2_
  41.3 2.5 multiply_sine_fusion
  43.7 212.8 %forward.1 = (f32[8,2048]{1,0:T(8,128)}, f32[3,8,256]{2,1,0:T(8,128)}, f32[384,2048]{1,0:T(8,128)}, bf16[1536,768]{1,0:T(8,128)(2,1)}, bf16[1536,1536]{1,0:T(8,1...) custom-call(bf16[16,128]{1,0:T(8,128)(2,1)} %copy-done.40, ...), custom_call_target="tpu_custom_call" | custom-call | tf_op jit(solution)/shard_map/forward/pallas_call | solution.py:560
  256.5 123.4 %ffn_backward.1 = (bf16[384,2048]{1,0:T(8,128)(2,1)}, bf16[384,2048]{1,0:T(8,128)(2,1)}, f32[256,2176]{1,0:T(8,128)}, bf16[256,2176]{1,0:T(8,128)(2,1)}) custom-call(bf16[384,2048]{1,0:T(8,128)(2,1)} %copy-done.2, bf16[1152,2048]{1,0:T(8,128)(2,1)} %get-tuple-element.66.refs_1_, bf16[1536,768]{1,0:T(8,128)(2,1)} %get-tuple-element.67.refs_2_.refs_16_, ...), custom_call_target="tpu_custom_call" | custom-call | tf_op jit(solution)/shard_map/ffn_backward/pallas_call | solution.py:820
  379.9 141.8 %finale.1 = (f32[384,2048]{1,0:T(8,128)}, bf16[384,2048]{1,0:T(8,128)(2,1)}, bf16[384,2048]{1,0:T(8,128)(2,1)}, bf16[384,2048]{1,0:T(8,128)(2,1)}, bf16[384,2048...) custom-call(f32[8,2048]{1,0:T(8,128)} %get-tuple-element.65.refs_0_,, ...), custom_call_target="tpu_custom_call" | custom-call | tf_op jit(solution)/shard_map/finale/pallas_call | solution.py:1137
  521.7 2.3 fusion.7
  534.8 1.5 copy.36
  536.4 2.0 maximum_bitcast_fusion
  538.4 2.0 copy.35
  540.4 2.6 fusion
  544.2 1.1 fusion.3
  551.5 1.3 concatenate.58
  552.9 1.3 concatenate.57
  (147 shorter events, 26.3 us)
Async XLA Ops:
  0.6 1.9 copy-start.18
  0.7 39.9 %collective-permute-start = (s32[3,128]{1,0:T(4,128)}, s32[3,128]{1,0:T(4,128)S(1)}, u32[]{:S(2)}, u32[]{:S(2)}) collective-permute-start(s32[3,128]{1,0:T(4,128)} %param.19), channel_id=1, source_target_pairs={{0,2},{2,0},{4,6},{6,4},{8,10},{10,8},{12,14},{14,12},{16,18},{18,... | collective-permute-start | bytes 4616 | tf_op jit(solution)/shard_map/ppermute | solution.py:24
  3.6 2.4 copy-start.38
  25.4 18.3 %copy-start.2 = (bf16[384,2048]{1,0:T(8,128)(2,1)}, bf16[384,2048]{1,0:T(8,128)(2,1)S(1)}, u32[]{:S(2)}) copy-start(bf16[384,2048]{1,0:T(8,128)(2,1)S(1)} %dynamic-slice_dynamic-update-slice_fusion.16.refs_4_.refs_0_.refs_2_) | copy-start | bytes 4718596
  26.6 9.2 %copy-start = (bf16[384,2048]{1,0:T(8,128)(2,1)}, bf16[384,2048]{1,0:T(8,128)(2,1)S(1)}, u32[]{:S(2)}) copy-start(bf16[384,2048]{1,0:T(8,128)(2,1)S(1)} %dynamic-slice_dynamic-update-slice_fusion.24.refs_3_.refs_5_) | copy-start | bytes 4718596
  30.9 4.9 copy-start.20
  30.9 4.9 copy-start.21
  33.8 6.8 %copy-start.40 = (bf16[16,128]{1,0:T(8,128)(2,1)}, bf16[16,128]{1,0:T(8,128)(2,1)S(1)}, u32[]{:S(2)}) copy-start(bf16[16,128]{1,0:T(8,128)(2,1)S(1)} %scatter.9.refs_0_) | copy-start | bytes 12292
  35.8 4.8 copy-start.41
  528.0 2.4 copy-start.22
  528.0 2.4 copy-start.23
  530.4 4.0 copy-start.35
  530.5 4.0 copy-start.36
  534.8 5.6 %copy-start.4 = (bf16[384,2048]{1,0:T(8,128)(2,1)S(1)}, bf16[384,2048]{1,0:T(8,128)(2,1)}, u32[]{:S(2)}) copy-start(bf16[384,2048]{1,0:T(8,128)(2,1)} %get-tuple-element.85) | copy-start | bytes 4718596
  536.4 4.0 copy-start.1
  540.4 3.8 copy-start.5
  540.4 3.8 copy-start.6
  544.2 1.9 copy-start.3
  544.2 2.4 copy-start.7
  544.2 2.8 copy-start.8
  548.3 2.3 copy-start.16
  548.3 2.3 copy-start.17
  548.4 3.0 copy-start.11
  548.4 3.0 copy-start.12
  548.4 3.0 copy-start.14
  548.4 3.0 copy-start.15
  548.4 3.0 copy-start.26
  548.4 3.0 copy-start.27
  548.5 3.0 copy-start.29
  548.5 3.0 copy-start.30
  548.6 2.8 copy-start.37
  548.6 1.9 copy-start.39
  (11 other events, 15.2 us)

commit v5 on v4

--- a/solution.py
+++ b/solution.py
@@ -110,6 +110,42 @@
     ]
 
 
+class Joint:
+    def __init__(self, copies):
+        self.copies = copies
+
+    def wait(self):
+        for copy in self.copies:
+            copy.wait()
+
+
+def block_start(far, unit, side, block):
+    place = lax.axis_index("dp") // 2
+    place = place - LOW * ((place // LOW) % 2) + LOW * side
+    for level, bit in enumerate(far):
+        if (unit // 2**level) % 2:
+            place = flipped(place, bit)
+    return pl.multiple_of(place * block, block)
+
+
+def load_rearranged(links, far, src, dst):
+    units = 2 ** len(far)
+    block = src.shape[1] // (2 * units)
+    if block % 128:
+        return links.copy(src, dst)
+    copies = []
+    for unit in range(units):
+        for side in range(2):
+            start = block_start(far, unit, side, block)
+            copies.append(
+                links.copy(
+                    src.at[:, pl.ds(start, block)],
+                    dst.at[:, pl.ds((2 * unit + side) * block, block)],
+                )
+            )
+    return Joint(copies)
+
+
 def low_bit():
     return (lax.axis_index("dp") // (2 * LOW)) % 2
 
@@ -233,12 +269,6 @@
 
 def dot_last(left, right):
     return lax.dot_general(left, right, (((1,), (1,)), ((), ())), preferred_element_type=F32)
-
-
-def norm_back(grad, value, ratio, gain):
-    scaled = grad * gain
-    inner = jnp.mean(scaled * value, axis=-1, keepdims=True)
-    return ratio * scaled - value * ratio**3 * inner
 
 
 def turn(value, cosine, sine, back):
@@ -371,10 +401,12 @@
     down = spreads[gu_spreads:]
     for spread in attn:
         spread.begin()
-    own_hid = links.copy(hid_src, hid.at[pl.ds(0, count)])
-    side_hid = links.push(hid_src, hid.at[pl.ds(count, count)], peer(core=True))
+    own_hid = load_rearranged(links, far, hid_src, hid.at[pl.ds(0, count)])
     tokens = TokenSpread(links, cot_src, cot_out)
     own_hid.wait()
+    side_hid = links.push(
+        hid.at[pl.ds(0, count)], hid.at[pl.ds(count, count)], peer(core=True)
+    )
     side_hid.wait_recv()
 
     def first_ratio(start):
@@ -574,7 +606,7 @@
             pltpu.VMEM((2 * count, 128), F32),
         ]
         + [pltpu.VMEM((count, width), BF)] * 4
-        + link_scratch(256, 32),
+        + link_scratch(256, 64),
         compiler_params=pltpu.CompilerParams(
             collective_id=0, has_side_effects=True, vmem_limit_bytes=VMEM_BIG
         ),
@@ -689,8 +721,10 @@
                 self.part.at[own, span], self.land.at[rows, span], peer(core=True)
             )
 
-    def to_low(self):
+    def to_low(self, which=None):
         for i, span in enumerate(self.spans):
+            if which is not None and i not in which:
+                continue
             value = self.term(2, span)
             self.flight[3, i].wait_recv()
             value = value + self.land[pl.ds(self.count, self.count), span].astype(F32)
@@ -735,10 +769,19 @@
     total, sent, came, held, came_far = refs[21:26]
     more = paired(refs[26:-3])
     links = Links(*refs[-3:])
+    n_own = own_in.shape[0]
+    cot_load = Joint(
+        [load_rearranged(links, far, own_in, cot.at[pl.ds(0, n_own)])]
+        + [
+            load_rearranged(
+                links, far, cot_in.at[pl.ds(i * n_own, n_own)], cot.at[pl.ds((i + 1) * n_own, n_own)]
+            )
+            for i in range(3)
+        ]
+    )
     loads = [
         links.copy(src, dst)
         for src, dst in (
-            (cot_in, cot.at[pl.ds(own_in.shape[0], cot_in.shape[0])]),
             (act_in, act),
             (down_in, down_w),
             (slope_in, slope),
@@ -746,7 +789,6 @@
             (gu_in, gu_w),
         )
     ]
-    own_load = links.copy(own_in, cot.at[pl.ds(0, own_in.shape[0])])
     greet([CORE, TENSOR] + chips_apart(LOW, *far))
     group, width = cot.shape
     count = group // 4
@@ -756,13 +798,12 @@
     gu_job = (pl.ds(down_cols, gu_cols), n2, grads)
     collect = Collect(links, far, width, sent, came, held, came_far, total, more)
 
-    own_load.wait()
+    cot_load.wait()
     loads[0].wait()
-    loads[1].wait()
     upper, lower = list(collect.upper()), list(collect.lower())
     collect.send_half("d", down_job, upper)
+    loads[1].wait()
     loads[2].wait()
-    loads[3].wait()
     lane = lax.broadcasted_iota(jnp.int32, (256, 128), 1)
 
     def slopes(start):
@@ -776,10 +817,10 @@
         slope[span, 2 * main : 2 * main + 128] = last.astype(BF)
 
     by_rows(0, group, 256, slopes)
+    loads[3].wait()
+    collect.send_half("g", gu_job, upper)
+
     loads[4].wait()
-    collect.send_half("g", gu_job, upper)
-
-    loads[5].wait()
 
     def term(slot, span):
         return dot_last(slope[pl.ds(slot * count, count), 0:gu_cols], gu_w[span])
@@ -793,10 +834,8 @@
     sums.outer(1)
     collect.send_half("d", down_job, lower)
     collect.send_half("g", gu_job, lower)
-    collect.own_half("g", gu_job, upper[:1])
-    sums.to_half([0, 1])
-    collect.own_half("g", gu_job, upper[1:])
-    sums.to_half([2, 3])
+    collect.own_half("g", gu_job, upper)
+    sums.to_half()
     collect.own_half("d", down_job, lower)
     collect.own_half("g", gu_job, lower)
     collect.finish("d", down_job)
@@ -832,7 +871,7 @@
         + group_sum_scratch(count, width)
         + [pltpu.VMEM((width // 4, cols), F32)]
         + collect_scratch(far, width, cols)
-        + link_scratch(128, 32),
+        + link_scratch(128, 64),
         compiler_params=pltpu.CompilerParams(
             collective_id=2, has_side_effects=True, vmem_limit_bytes=VMEM_BIG
         ),
@@ -890,7 +929,6 @@
         links.copy(src, dst)
         for src, dst in (
             (middle_in, grad_middle),
-            (cot_in, summ),
             (grad_two_in, feed),
             (across_two_in, part),
             (attn_in, attn_w),
@@ -898,6 +936,7 @@
             (n1_in, n1),
         )
     ]
+    loads.insert(1, load_rearranged(links, far, cot_in, summ))
     span_chips = kvs_in.shape[0]
     greet([CORE, TENSOR] + chips_apart(LOW, *far) + chips_apart(*range(1, span_chips)))
     count, width = grad_middle.shape
@@ -914,6 +953,8 @@
         links.push(ffn_other, ffn_low, peer(LOW)),
         links.push(ffn_own.at[core_rows(1 - core)], ffn_core, peer(core=True)),
     ]
+
+    feed_loads = [links.copy(act_in, act), links.copy(down_in, down_w)]
 
     for load in loads[:4]:
         load.wait()
@@ -936,7 +977,9 @@
     own = links.push(gmid.at[pl.ds(0, count)], gmid.at[pl.ds(count, count)], peer(core=True))
     collect = Collect(links, far, width, sent, came, held, came_far, total, more)
     out_job = (pl.ds(n_qkv, n_q), gmid, mixed)
-    qkv_job = (pl.ds(0, n_qkv), n1, raw)
+    q_job = (pl.ds(0, n_q), n1, go)
+    kv_job = (pl.ds(n_q, 128), n1, raw.at[:, pl.ds(n_q, 128)])
+    jobs = (("o", out_job), ("q", q_job), ("v", kv_job))
     upper, lower = list(collect.upper()), list(collect.lower())
     loads[4].wait()
     loads[5].wait()
@@ -950,6 +993,18 @@
     by_rows(count, count, 128, mixed_back)
     collect.send_half("o", out_job, upper)
     collect.send_half("o", out_job, lower)
+
+    def term(slot, span):
+        return dot_last(act[pl.ds(slot * count, count)], down_w[span])
+
+    sums = GroupSum(
+        links, count, width, 4, term, part, land, side, land_low, feed, feed_across
+    )
+    for load in feed_loads:
+        load.wait()
+    sums.outer(3)
+    sums.to_low([0, 1])
+    sums.outer(1)
 
     def attention():
         scoped = [
@@ -963,8 +1018,9 @@
         ]
         for load in scoped:
             load.wait()
-        for m in range(micro):
-            mine, other = pl.ds(m * rows, rows), pl.ds(count + m * rows, rows)
+        def one(m, carry):
+            mine = pl.ds(pl.multiple_of(m * rows, rows), rows)
+            other = pl.ds(pl.multiple_of(count + m * rows, rows), rows)
             bias[...] = mask_bias(kpos[...], rowinfo[m])
 
             def both(ref):
@@ -985,11 +1041,19 @@
                         dkv_own[span] = pair
                     else:
                         dkv_sent[key - 1, span] = pair.astype(BF)
+            return carry
+
+        lax.fori_loop(0, micro, one, 0)
         flight = [
             links.push(dkv_sent.at[key - 1], dkv_land.at[key - 1], peer(key))
             for key in range(1, span_chips)
         ]
+        for load in loads[6:]:
+            load.wait()
+        collect.send_half("q", q_job, upper)
         collect.own_half("o", out_job, upper)
+        collect.send_half("q", q_job, lower)
+        sums.to_half([0, 1])
         for copy in flight:
             copy.wait_recv()
 
@@ -1006,9 +1070,9 @@
 
     attention()
 
-    loads[6].wait()
-    collect.send_half("q", qkv_job, upper)
-    collect.send_half("q", qkv_job, lower)
+    collect.send_half("v", kv_job, upper)
+    collect.send_half("v", kv_job, lower)
+    links.settle([sums.flight["low", i] for i in range(2)])
     spans = [pl.ds(i * (width // 4), width // 4) for i in range(4)]
     to_core = []
     for span in spans:
@@ -1020,41 +1084,38 @@
         to_core[i].wait_recv()
         summ[:, span] = (value + land_side[:, span].astype(F32)).astype(BF)
         over.append(links.push(summ.at[:, span], across.at[:, span], peer(tensor=True)))
-    load_hid = links.copy(hid_in, land_side)
-
-    def feed_sums():
-        scoped = [links.copy(act_in, act), links.copy(down_in, down_w)]
-        collect.own_half("q", qkv_job, upper)
-        collect.own_half("o", out_job, lower)
-        for load in scoped:
-            load.wait()
-
-        def term(slot, span):
-            return dot_last(act[pl.ds(slot * count, count)], down_w[span])
-
-        sums = GroupSum(
-            links, count, width, 4, term, part, land, side, land_low, feed, feed_across
-        )
-        links.settle(to_core)
-        sums.outer(3)
-        sums.to_low()
-        sums.outer(1)
-        collect.own_half("q", qkv_job, lower)
-        sums.to_half()
-        return sums
-
-    sums = feed_sums()
-    collect.finish("o", out_job)
-    collect.finish("q", qkv_job)
-    collect.finish_more()
-
+    load_hid = load_rearranged(links, far, hid_in, land_side)
+
+    for name, job in jobs[1:]:
+        collect.own_half(name, job, upper)
+    links.settle(to_core)
+    sums.to_low([2, 3])
     half_unit = attn_mine.shape[0] * 2
 
     def low_rows(which):
         return pl.ds(pl.multiple_of(which * half_unit, half_unit), half_unit)
 
-    low_sent[...] = total[low_rows(1 - low)].astype(BF)
-    low_flight = links.push(low_sent, low_land, peer(LOW))
+    low_flight = {}
+
+    def to_low(name, job):
+        columns = job[0]
+        low_sent[:, columns] = total[low_rows(1 - low), columns].astype(BF)
+        low_flight[name] = links.push(low_sent.at[:, columns], low_land.at[:, columns], peer(LOW))
+
+    collect.own_half("o", out_job, lower)
+    collect.finish("o", out_job)
+    if not collect.more:
+        to_low("o", out_job)
+    for name, job in jobs[1:]:
+        collect.own_half(name, job, lower)
+    for name, job in jobs[1:]:
+        collect.finish(name, job)
+        if not collect.more:
+            to_low(name, job)
+    if collect.more:
+        collect.finish_more()
+        for name, job in jobs:
+            to_low(name, job)
 
     for copy in over:
         copy.wait_recv()
@@ -1065,7 +1126,11 @@
         value = land_side[span].astype(F32)
         ratio = lax.rsqrt(jnp.mean(value * value, axis=-1, keepdims=True) + epsilon)
         grad = summ[span].astype(F32) + across[span].astype(F32)
-        near_gains[0:1] += jnp.sum(grad * value * ratio, axis=0, keepdims=True)
+        turned = value * ratio
+        near_gains[0:1] += jnp.sum(grad * turned, axis=0, keepdims=True)
+        scaled = grad * gain_rows[0:1]
+        inner = jnp.mean(scaled * turned, axis=-1, keepdims=True)
+        grad_middle[span] = grad_middle[span] + ratio * (scaled - turned * inner)
 
     by_rows(0, count, 64, first_norm)
     kept, base = width, 0
@@ -1073,6 +1138,8 @@
         kept //= 2
         landed = far_gains.at[:, pl.ds(base, kept)]
         copy = links.push(near_gains.at[:, pl.ds(kept, kept)], landed, peer(bit))
+        if base == 0:
+            sums.to_half([2, 3])
         copy.wait_recv()
         near_gains[:, 0:kept] = near_gains[:, 0:kept] + landed[...]
         base += kept
@@ -1085,13 +1152,22 @@
     gains[...] = near_gains[:, 0:kept] + low_gains[...]
     copy = links.push(gains, core_gains, peer(core=True))
 
-    low_flight.wait_recv()
-    own_unit = total[low_rows(low)] + low_land[...].astype(F32)
-    total[0:half_unit] = own_unit
-    core_flight = links.push(total.at[core_rows(1 - core)], attn_came, peer(core=True))
-    attn_mine[...] = total[core_rows(core)]
+    core_flight = []
+    for name, job in jobs:
+        columns = job[0]
+        low_flight[name].wait_recv()
+        total[0:half_unit, columns] = total[low_rows(low), columns] + low_land[:, columns].astype(
+            F32
+        )
+        core_flight.append(
+            links.push(
+                total.at[core_rows(1 - core), columns], attn_came.at[:, columns], peer(core=True)
+            )
+        )
+        attn_mine[:, columns] = total[core_rows(core), columns]
     copy.wait_recv()
-    core_flight.wait_recv()
+    for flight in core_flight:
+        flight.wait_recv()
     for flight in ffn_flight[1:]:
         flight.wait_recv()
     sums.wait()
@@ -1184,12 +1260,39 @@
             pltpu.VMEM(down_w.shape, BF),
         ]
         + collect_scratch(far, width, attn_cols)[4:]
-        + link_scratch(192, 32),
+        + link_scratch(192, 64),
         compiler_params=pltpu.CompilerParams(
             collective_id=3, has_side_effects=True, vmem_limit_bytes=VMEM_BIG
         ),
         name="finale",
     )(*inputs)
+
+
+def restore_kernel(places, middle, feed, feed_across, grad, output, grad_out):
+    value = middle[...] + (feed[...].astype(F32) + feed_across[...].astype(F32))
+    output[...] = value.astype(BF)
+    grad_out[...] = grad[...]
+
+
+def restore(places, block, middle, feed, feed_across, grad):
+    count, width = middle.shape
+    moved = pl.BlockSpec((count, block), lambda i, places: (0, places[i]))
+    kept = pl.BlockSpec((count, block), lambda i, places: (0, i))
+    return pl.pallas_call(
+        restore_kernel,
+        grid_spec=pltpu.PrefetchScalarGridSpec(
+            num_scalar_prefetch=1,
+            grid=(width // block,),
+            in_specs=[moved] * 4,
+            out_specs=[kept] * 2,
+        ),
+        out_shape=[
+            jax.ShapeDtypeStruct((count, width), BF),
+            jax.ShapeDtypeStruct((count, width), F32),
+        ],
+        compiler_params=pltpu.CompilerParams(vmem_limit_bytes=VMEM_LIMIT),
+        name="restore",
+    )(places, middle, feed, feed_across, grad)
 
 
 def body(
@@ -1237,16 +1340,14 @@
             axis=-1,
         )
 
+    unit_of = jnp.array([keys.index(other & ~LOW) for other in range(chips)], jnp.int32)
+    naturals = jnp.arange(chips, dtype=jnp.int32)
+    places = unit_of[chip ^ naturals] * 2 + (naturals // LOW) % 2
+
     def restored(array):
-        unit_of = jnp.array([keys.index(other & ~LOW) for other in range(chips)], jnp.int32)
         return jnp.concatenate(
             [
-                lax.dynamic_slice_in_dim(
-                    array,
-                    (unit_of[chip ^ natural] * 2 + (natural // LOW) % 2) * block,
-                    block,
-                    array.ndim - 1,
-                )
+                lax.dynamic_slice_in_dim(array, places[natural] * block, block, array.ndim - 1)
                 for natural in range(chips)
             ],
             axis=-1,
@@ -1295,10 +1396,11 @@
     )
     gain_pack = jnp.zeros((16, 128), BF).at[0, :own_block].set(attn_gain)
     gain_pack = gain_pack.at[1, :own_block].set(ffn_gain)
-    hidden = rearranged(tokens.reshape(count, width))
-    grad_final = rearranged(cotangent.reshape(count, width))
-
-    hidden_f = hidden.astype(F32)
+    hidden = tokens.reshape(count, width)
+    grad_final = cotangent.reshape(count, width)
+    if block % 128:
+        hidden, grad_final = rearranged(hidden), rearranged(grad_final)
+
     position_both = jnp.stack([doc_position, swap_core(doc_position)])
 
     power = jnp.arange(HEAD_DIM // 2, dtype=F32) * (2.0 / HEAD_DIM)
@@ -1346,9 +1448,9 @@
         far, main, grad_final, grad_final_others, activated, down_wt, slopes, normed_two, gu_w
     )
     (
-        grad_middle,
-        grad_one,
-        grad_one_across,
+        grad_hidden,
+        _,
+        _,
         feed,
         feed_across,
         attn_mine,
@@ -1383,11 +1485,11 @@
             ffn_other,
         ),
     )
-    output = restored((middle + (feed.astype(F32) + feed_across.astype(F32))).astype(BF))
-    grad_normed = grad_one.astype(F32) + grad_one_across.astype(F32)
-    ratio_one = lax.rsqrt(jnp.mean(hidden_f * hidden_f, axis=-1, keepdims=True) + epsilon)
-    grad_in_norm = norm_back(grad_normed, hidden_f, ratio_one, gain_rows[0:1])
-    grad_tokens = restored(grad_middle + grad_in_norm)
+    if block % 128:
+        output = restored((middle + (feed.astype(F32) + feed_across.astype(F32))).astype(BF))
+        grad_tokens = restored(grad_hidden)
+    else:
+        output, grad_tokens = restore(places, block, middle, feed, feed_across, grad_hidden)
     grad_gains = lax.dynamic_slice_in_dim(grad_gains, (2 * low + core) * own_block, own_block, 1)
 
     def picked(pair, side):

time: 560 us -> 528 us (0.943)
  local copies, waits for them, and re-layouts: 54.8 us -> 35.3 us
  between operations: 6.92 us -> 1.31 us
    unnamed x115 -> x64, local copies, waits for them, and re-layouts: 21.3 us -> 5.91 us
    pallas_call x1, Pallas kernels: 142 us -> 133 us  [finale(): pl.pallas_call(functools.partial(finale_kernel, far, micro), in_specs=any...]
    pallas_call x0 -> x1, Pallas kernels: none -> 7.87 us  [restore(): pl.pallas_call(restore_kernel, grid_spec=pltpu.PrefetchScalarGridSpec(num...]
  transfers between devices with their start and end apart: 1 -> 1, of which waited for: 0 -> 0; matrix products, arithmetic and copies ran while one was open for 6% -> 3% of each run, Pallas kernels for 0% -> 0%
where the time goes in v5:
time: 528 us; the launch traced here: 523 us
  Pallas kernels  475 us (90%)
  local copies, waits for them, and re-layouts  35.3 us (7%)
  other arithmetic  11.1 us (2%)
    pallas_call x1, Pallas kernels, forward(): pl.pallas_call(functools.partial(forward_kernel, far, main, micro), in_sp...  213 us
    pallas_call x1, Pallas kernels, finale(): pl.pallas_call(functools.partial(finale_kernel, far, micro), in_specs=any...  133 us
    pallas_call x1, Pallas kernels, ffn_backward(): pl.pallas_call(functools.partial(ffn_backward_kernel, far, main), in_spec...  120 us
  transfers between devices with their start and end apart: 1, of which 0 were waited for; matrix products, arithmetic and copies ran while one was open for 3% of the time, Pallas kernels for 0%

profile of v5, /device:TPU:0, one launch (start us, length us, event | category | flops | bytes accessed | tf_op | source)
XLA Modules:
  0.0 523.1 jit_solution(11583104043437726499)
XLA Ops:
  1.2 1.6 fusion.24
  2.8 1.3 fusion.26
  4.4 0.7 fusion.21
  6.4 1.1 copy.29
  7.5 1.0 copy.32.refs_7_.refs_8_
  9.5 1.6 concatenate.34.refs_1_
  11.2 5.9 %concatenate.35.refs_2_ = bf16[128,8704]{1,0:T(8,128)(2,1)} concatenate(bf16[128,640]{1,0:T(8,128)(2,1)S(1)} %get-tuple-element.168, bf16[128,640]{1,0:T(8,128)(2,1)S(1)} %get-tuple-element.199, bf16[128,64]{1,0:T(8,128)(2,1)S(1)} %copy-done.23, bf16[128,64]{1,0:T(8,128)(2,1)S(1)} %copy-done.16, bf16[128,640]{1,0:T(8,128)(2,1)S(1)} %get-tuple-element.152, ...), dimensions={1} | concatenate | bytes 4456448 | tf_op jit(solution)/shard_map/concatenate | solution.py:1381
  17.8 2.5 multiply_sine_fusion
  20.3 213.2 %forward.1 = (f32[8,2048]{1,0:T(8,128)}, f32[3,8,256]{2,1,0:T(8,128)}, f32[384,2048]{1,0:T(8,128)}, bf16[1536,768]{1,0:T(8,128)(2,1)}, bf16[1536,1536]{1,0:T(8,1...) custom-call(bf16[16,128]{1,0:T(8,128)(2,1)} %copy-done.26, ...), custom_call_target="tpu_custom_call" | custom-call | tf_op jit(solution)/shard_map/forward/pallas_call | solution.py:592
  233.5 120.5 %ffn_backward.1 = (bf16[384,2048]{1,0:T(8,128)(2,1)}, bf16[384,2048]{1,0:T(8,128)(2,1)}, f32[256,2176]{1,0:T(8,128)}, bf16[256,2176]{1,0:T(8,128)(2,1)}) custom-call(bf16[384,2048]{1,0:T(8,128)(2,1)} %bitcast.24, bf16[1152,2048]{1,0:T(8,128)(2,1)} %get-tuple-element.66.refs_1_, bf16[1536,768]{1,0:T(8,128)(2,1)} %get-tuple-element.67.refs_2_.refs_16_, ...), custom_call_target="tpu_custom_call" | custom-call | tf_op jit(solution)/shard_map/ffn_backward/pallas_call | solution.py:859
  354.0 133.3 %finale.1 = (f32[384,2048]{1,0:T(8,128)}, bf16[384,2048]{1,0:T(8,128)(2,1)}, bf16[384,2048]{1,0:T(8,128)(2,1)}, bf16[384,2048]{1,0:T(8,128)(2,1)}, bf16[384,2048...) custom-call(f32[8,2048]{1,0:T(8,128)} %get-tuple-element.65.refs_0_,, ...), custom_call_target="tpu_custom_call" | custom-call | tf_op jit(solution)/shard_map/finale/pallas_call | solution.py:1213
  487.4 1.4 broadcast_select_fusion.1
  488.8 0.7 fusion.29
  489.5 0.8 fusion.27
  490.3 0.7 fusion.30
  491.0 0.8 fusion.28
  491.8 1.4 fusion.2
  493.9 0.8 fusion.17
  495.4 1.0 fusion.18
  496.3 0.7 fusion.15
  497.0 0.9 fusion.19
  497.9 0.7 fusion.16
  498.7 0.9 fusion.20
  500.8 1.0 copy.34
  501.8 1.3 concatenate.43
  503.1 3.0 copy.35
  506.1 1.6 pad_maximum_fusion.2
  507.7 1.6 pad_maximum_fusion.1
  509.3 1.9 pad_maximum_fusion
  511.2 7.9 %restore.1 = (bf16[384,2048]{1,0:T(8,128)(2,1)}, f32[384,2048]{1,0:T(8,128)}) custom-call(s32[8]{0:T(128)S(1)} %fusion.10.places, f32[384,2048]{1,0:T(8,128)} %get-tuple-element.64.refs_1_.middle, bf16[384,2048]{1,0:T(8,128)(2,1)S(1)} %copy-done, bf16[384,2048]{1,0:T(8,128)(2,1)S(1)} %copy-done.1, f32[384,2048]{1,0:T(8,128)} %get-tuple-element.84.grad), custom_call_target="tpu_custom_call" | custom-call | tf_op jit(solution)/shard_map/restore/pallas_call | solution.py:1281
  519.1 2.4 concatenate.41
  521.6 1.3 concatenate.42
  (90 shorter events, 6.2 us)
Async XLA Ops:
  0.6 3.4 copy-start.9
  0.7 16.5 %collective-permute-start = (s32[3,128]{1,0:T(4,128)}, s32[3,128]{1,0:T(4,128)S(1)}, u32[]{:S(2)}, u32[]{:S(2)}) collective-permute-start(s32[3,128]{1,0:T(4,128)} %param.18), channel_id=1, source_target_pairs={{0,2},{2,0},{4,6},{6,4},{8,10},{10,8},{12,14},{14,12},{16,18},{18,... | collective-permute-start | bytes 4616 | tf_op jit(solution)/shard_map/ppermute | solution.py:24
  2.8 1.6 copy-start.8
  5.1 0.7 copy-start.2
  5.2 3.3 copy-start.28
  5.2 3.3 copy-start.29
  5.3 3.4 copy-start.24
  5.3 3.4 copy-start.25
  5.3 4.1 copy-start.14
  8.6 2.5 copy-start.26
  9.3 1.8 copy-start.15
  9.3 1.8 copy-start.16
  9.4 1.8 copy-start.17
  9.4 1.8 copy-start.18
  9.4 1.8 copy-start.19
  9.4 1.8 copy-start.20
  9.4 1.8 copy-start.21
  9.4 1.8 copy-start.22
  9.4 1.8 copy-start.23
  11.2 5.9 %copy-start.27 = (s32[3,128]{1,0:T(4,128)S(1)}, s32[3,128]{1,0:T(4,128)}, u32[]{:S(2)}) copy-start(s32[3,128]{1,0:T(4,128)} %param.18) | copy-start | bytes 4612
  487.3 4.4 copy-start.7
  487.4 4.4 copy-start.10
  489.5 2.3 copy-start.3
  503.1 8.1 %copy-start = (bf16[384,2048]{1,0:T(8,128)(2,1)S(1)}, bf16[384,2048]{1,0:T(8,128)(2,1)}, u32[]{:S(2)}) copy-start(bf16[384,2048]{1,0:T(8,128)(2,1)} %get-tuple-element.82.feed) | copy-start | bytes 4718596
  503.1 8.1 %copy-start.1 = (bf16[384,2048]{1,0:T(8,128)(2,1)S(1)}, bf16[384,2048]{1,0:T(8,128)(2,1)}, u32[]{:S(2)}) copy-start(bf16[384,2048]{1,0:T(8,128)(2,1)} %get-tuple-element.83.feed_across) | copy-start | bytes 4718596
  519.1 2.5 copy-start.4
  519.1 2.5 copy-start.5
  519.1 2.5 copy-start.6
  519.1 2.5 copy-start.11
  519.1 2.5 copy-start.12
  519.1 2.5 copy-start.13

commit v6 on v5

--- a/solution.py
+++ b/solution.py
@@ -159,24 +159,29 @@
 
 
 class Spread:
-    def __init__(self, links, src, column, dst, height, start, cols, far):
-        self.links, self.src, self.column, self.dst = links, src, column, dst
-        self.height, self.start, self.cols, self.far = height, start, cols, far
-        self.level = 0
+    def __init__(self, links, pieces, dst, height, start, far):
+        self.links, self.pieces, self.dst = links, pieces, dst
+        self.height, self.start, self.far = height, start, far
+        self.cols = sum(cols for _, _, cols in pieces)
 
     def begin(self):
         low, core = low_bit(), core_bit()
-        mine = self.dst.at[group_rows(self.height, low, core), pl.ds(self.start, self.cols)]
-
-        def part(low, core):
-            return self.src.at[:, pl.ds(pl.multiple_of(self.column(low, core), 128), self.cols)]
-
-        self.local = self.links.copy(part(low, core), mine)
-        self.stage = [
-            self.links.push(part(1 - low, core), mine, peer(LOW)),
-            self.links.push(part(1 - low, 1 - core), mine, peer(LOW, core=True)),
-            self.links.push(part(low, 1 - core), mine, peer(core=True)),
-        ]
+        rows = group_rows(self.height, low, core)
+        start = self.start
+        self.local, self.stage = [], []
+        for src, column, cols in self.pieces:
+            mine = self.dst.at[rows, pl.ds(start, cols)]
+
+            def part(low, core, src=src, column=column, cols=cols):
+                return src.at[:, pl.ds(pl.multiple_of(column(low, core), 128), cols)]
+
+            self.local.append(self.links.copy(part(low, core), mine))
+            self.stage += [
+                self.links.push(part(1 - low, core), mine, peer(LOW)),
+                self.links.push(part(1 - low, 1 - core), mine, peer(LOW, core=True)),
+                self.links.push(part(low, 1 - core), mine, peer(core=True)),
+            ]
+            start += cols
 
     def unit(self, index):
         size = 4 * self.height
@@ -192,7 +197,8 @@
     def launch(self):
         for copy in self.stage:
             copy.wait_recv()
-        self.local.wait()
+        for copy in self.local:
+            copy.wait()
         self.arrivals = {}
         self.pass_on(0, 0)
 
@@ -341,7 +347,8 @@
 
 
 def forward_kernel(far, main, micro, *refs):
-    gain_src, attn_src, ffn_src, hid_src, cot_src, cosine, sine, kpos, rowinfo = refs[:9]
+    gain_src, attn_src, gate_src, up_src, down_src, ends_src, hid_src, cot_src = refs[:8]
+    cosine, sine, kpos, rowinfo = refs[8:12]
     (
         gain_rows,
         lse,
@@ -357,9 +364,9 @@
         gu_out,
         down_out,
         cot_out,
-    ) = refs[9:23]
-    gains, attn_w, gu_w, down_w, hid, n1, n2, bias, ratios, part, land, summ, across = refs[23:36]
-    links = Links(*refs[36:])
+    ) = refs[12:26]
+    gains, attn_w, gu_w, down_w, hid, n1, n2, bias, ratios, part, land, summ, across = refs[26:39]
+    links = Links(*refs[39:])
     count = hid_src.shape[0]
     rows = count // micro
     span_chips = kvs.shape[0]
@@ -373,29 +380,37 @@
     def core_column(start):
         return lambda low, core: core * attn_cols + start
 
-    def group_column(start):
-        return lambda low, core: (low * 2 + core) * total + start
+    def group_column(width, start):
+        return lambda low, core: (low * 2 + core) * width + start
 
     spreads = [
-        Spread(links, gain_src, lambda low, core: 0, gains, gain_src.shape[0], 0, 128, far)
+        Spread(links, [(gain_src, lambda low, core: 0, 128)], gains, gain_src.shape[0], 0, far)
     ]
     n_q = queries.shape[1]
     n_qkv = n_q + 128
     for base, tiles, parts in ((0, n_qkv // 128, 2), (n_qkv, n_q // 128, 2)):
         for start, cols in cuts(base, tiles, parts):
             spreads.append(
-                Spread(links, attn_src, core_column(start), attn_w, height, start, cols, far)
+                Spread(links, [(attn_src, core_column(start), cols)], attn_w, height, start, far)
             )
         if base == 0:
             qkv_spreads = len(spreads)
     attn_spreads = len(spreads)
-    for start, cols in cuts(0, gu_cols // 128, 4):
-        spreads.append(Spread(links, ffn_src, group_column(start), gu_w, height, start, cols, far))
+    first, second = cuts(0, main // 128, 2)
+    ends = (ends_src, group_column(256, 0), 128)
+    for src, base in ((gate_src, 0), (up_src, main)):
+        for start, cols in (first, second):
+            pieces = [(src, group_column(main, start), cols)]
+            if base and start:
+                pieces.append(ends)
+            spreads.append(Spread(links, pieces, gu_w, height, base + start, far))
     gu_spreads = len(spreads)
-    for start, cols in cuts(0, down_cols // 128, 2):
-        spreads.append(
-            Spread(links, ffn_src, group_column(gu_cols + start), down_w, height, start, cols, far)
-        )
+    ends = (ends_src, group_column(256, 128), 128)
+    for start, cols in (first, second):
+        pieces = [(down_src, group_column(main, start), cols)]
+        if start:
+            pieces.append(ends)
+        spreads.append(Spread(links, pieces, down_w, height, start, far))
     attn = spreads[:attn_spreads]
     gu = spreads[attn_spreads:gu_spreads]
     down = spreads[gu_spreads:]
@@ -561,7 +576,7 @@
 
 
 def forward(far, main, micro, span_chips, sources, tables):
-    gain_pack, attn_pack, ffn_pack, hidden, cotangent = sources
+    gain_pack, attn_pack, _, _, _, _, hidden, _ = sources
     count, width = hidden.shape
     attn_cols = attn_pack.shape[1] // 2
     gu_cols, down_cols = 2 * main + 128, main + 128
@@ -591,7 +606,7 @@
     ]
     return pl.pallas_call(
         functools.partial(forward_kernel, far, main, micro),
-        in_specs=[ANY] * 5 + [VMEM] * 4,
+        in_specs=[ANY] * 8 + [VMEM] * 4,
         out_specs=[VMEM] * 8 + [ANY] * 6,
         out_shape=shapes,
         scratch_shapes=[
@@ -1268,6 +1283,58 @@
     )(*inputs)
 
 
+def place_kernel(
+    main, where, mine, came, own, own_core, far_low, far_core, query, key, value, out, gate, up, down
+):
+    block = mine.shape[0]
+    n_q = query.shape[1] // 2
+    rest = gate.shape[1] // 4 - main
+    base = main + 128
+    for low in range(2):
+        for core in range(2):
+
+            @pl.when((where[0] == low) & (where[1] == core))
+            def _():
+                rows = pl.ds(core * block, block)
+                attn = {core: mine, 1 - core: came}
+                for side in range(2):
+                    part = attn[side]
+                    query[:, side * n_q : (side + 1) * n_q] = part[:, 0:n_q]
+                    span = slice(side * HEAD_DIM, (side + 1) * HEAD_DIM)
+                    key[:, span] = part[:, n_q : n_q + HEAD_DIM]
+                    value[:, span] = part[:, n_q + HEAD_DIM : n_q + 128]
+                    out[:, side * n_q : (side + 1) * n_q] = part[:, n_q + 128 : 2 * n_q + 128]
+                ffn = {
+                    (low, core): own.at[rows],
+                    (low, 1 - core): own_core,
+                    (1 - low, core): far_low.at[rows],
+                    (1 - low, 1 - core): far_core,
+                }
+                for place in range(4):
+                    part = ffn[place // 2, place % 2]
+                    for ref, start, last in (
+                        (down, 0, main),
+                        (gate, base, base + 2 * main),
+                        (up, base + main, base + 2 * main + rest),
+                    ):
+                        ref[:, place * main : (place + 1) * main] = part[
+                            :, start : start + main
+                        ].astype(F32)
+                        ends = 4 * main + place * rest
+                        ref[:, ends : ends + rest] = part[:, last : last + rest].astype(F32)
+
+
+def place_grads(main, where, shapes, parts):
+    return pl.pallas_call(
+        functools.partial(place_kernel, main),
+        in_specs=[pl.BlockSpec(memory_space=pltpu.SMEM)] + [VMEM] * 6,
+        out_specs=[VMEM] * 7,
+        out_shape=[jax.ShapeDtypeStruct(shape, F32) for shape in shapes],
+        compiler_params=pltpu.CompilerParams(vmem_limit_bytes=VMEM_LIMIT),
+        name="place_grads",
+    )(where, *parts)
+
+
 def restore_kernel(places, middle, feed, feed_across, grad, output, grad_out):
     value = middle[...] + (feed[...].astype(F32) + feed_across[...].astype(F32))
     output[...] = value.astype(BF)
@@ -1370,24 +1437,18 @@
     rest = hidden_units - main
     assert rest == 64
 
-    def mains(array, place):
-        return array[:, place * main : (place + 1) * main]
-
     def rests(array, place):
         return array[:, 4 * main + place * rest : 4 * main + (place + 1) * rest]
 
     w_down_t = w_down.T
     empty = jnp.zeros((own_block, 128 - rest), BF)
-    ffn_pack = jnp.concatenate(
+    ends_pack = jnp.concatenate(
         [
             piece
             for place in range(4)
             for piece in (
-                mains(w_gate, place),
-                mains(w_up, place),
                 rests(w_gate, place),
                 rests(w_up, place),
-                mains(w_down_t, place),
                 rests(w_down_t, place),
                 empty,
             )
@@ -1440,7 +1501,7 @@
         main,
         micro,
         span_chips,
-        (gain_pack, attn_pack, ffn_pack, hidden, grad_final),
+        (gain_pack, attn_pack, w_gate, w_up, w_down_t, ends_pack, hidden, grad_final),
         (cosine, sine, kpos, rowinfo),
     )
     gain_one, gain_two = gain_rows[0:1], gain_rows[1:2]
@@ -1492,41 +1553,23 @@
         output, grad_tokens = restore(places, block, middle, feed, feed_across, grad_hidden)
     grad_gains = lax.dynamic_slice_in_dim(grad_gains, (2 * low + core) * own_block, own_block, 1)
 
-    def picked(pair, side):
-        return jnp.where(side == 0, pair[0], pair[1]), jnp.where(side == 0, pair[1], pair[0])
-
-    parts = picked((attn_mine, attn_came), core)
-
-    def columns(start, stop):
-        return jnp.concatenate([part[:, start:stop] for part in parts], axis=1)
-
-    grad_w_query = columns(0, n_q)
-    grad_w_key = columns(n_q, n_q + n_kv)
-    grad_w_value = columns(n_q + n_kv, n_qkv)
-    grad_w_out = columns(n_qkv, n_qkv + n_q).T
-
-    def own_rows(array):
-        return lax.dynamic_slice_in_dim(array, core * own_block, own_block, 0)
-
-    mine_low = picked((own_rows(ffn_own), ffn_core), core)
-    other_low = picked((own_rows(ffn_low).astype(F32), ffn_low_core.astype(F32)), core)
-    by_low = [
-        picked((mine_low[side], other_low[side]), low) for side in range(2)
-    ]
-    places = [by_low[place % 2][place // 2] for place in range(4)]
-    down_cols = main + 128
-    gu = down_cols
-
-    def gathered(main_start, rest_start):
-        return jnp.concatenate(
-            [part[:, main_start : main_start + main] for part in places]
-            + [part[:, rest_start : rest_start + rest] for part in places],
-            axis=1,
+    grad_w_query, grad_w_key, grad_w_value, grad_out_t, grad_w_gate, grad_w_up, grad_down_t = (
+        place_grads(
+            main,
+            jnp.stack([low, core]),
+            [
+                w_query.shape,
+                w_key.shape,
+                w_value.shape,
+                w_out.shape[::-1],
+                w_gate.shape,
+                w_up.shape,
+                w_down.shape[::-1],
+            ],
+            (attn_mine, attn_came, ffn_own, ffn_core, ffn_low, ffn_low_core),
         )
-
-    grad_w_down = gathered(0, main).T
-    grad_w_gate = gathered(gu, gu + 2 * main)
-    grad_w_up = gathered(gu + main, gu + 2 * main + rest)
+    )
+    grad_w_out, grad_w_down = grad_out_t.T, grad_down_t.T
     return (
         output.reshape(tokens.shape),
         grad_tokens.reshape(tokens.shape),

time: 528 us -> 510 us (0.966)
  local copies, waits for them, and re-layouts: 35.3 us -> 19.9 us
  other arithmetic: 11.1 us -> 3.22 us
  Pallas kernels: 475 us -> 481 us
    slice x14 -> x0, local copies, waits for them, and re-layouts: 10.7 us -> none  [the longest x4 3.58 us: gathered(): part[:, main_start:main_start + main]]
    concatenate x4 -> x1, local copies, waits for them, and re-layouts: 11 us -> 0.95 us  [body(): jnp.concatenate([piece for place in range(4) for piece in (rests(w_gate,...]
    unnamed x64 -> x38, local copies, waits for them, and re-layouts: 5.91 us -> 12.2 us
  transfers between devices with their start and end apart: 1 -> 1, of which waited for: 0 -> 0; matrix products, arithmetic and copies ran while one was open for 3% -> 2% of each run, Pallas kernels for 0% -> 0%
where the time goes in v6:
time: 510 us; the launch traced here: 506 us
  Pallas kernels  481 us (94%)
  local copies, waits for them, and re-layouts  19.9 us (4%)
    pallas_call x1, Pallas kernels, forward(): pl.pallas_call(functools.partial(forward_kernel, far, main, micro), in_sp...  216 us
    pallas_call x1, Pallas kernels, finale(): pl.pallas_call(functools.partial(finale_kernel, far, micro), in_specs=any...  133 us
    pallas_call x1, Pallas kernels, ffn_backward(): pl.pallas_call(functools.partial(ffn_backward_kernel, far, main), in_spec...  120 us
    unnamed x38, local copies, waits for them, and re-layouts  12.2 us
  transfers between devices with their start and end apart: 1, of which 0 were waited for; matrix products, arithmetic and copies ran while one was open for 2% of the time, Pallas kernels for 0%

profile of v6, /device:TPU:0, one launch (start us, length us, event | category | flops | bytes accessed | tf_op | source)
XLA Modules:
  0.0 506.0 jit_solution(11138827992950242962)
XLA Ops:
  0.7 0.5 collective-permute-start
  1.2 0.1 mul.54
  1.3 0.0 copy-start.12
  1.3 1.3 gather_fusion
  2.7 1.0 fusion.11
  3.6 1.1 copy.29
  4.8 1.0 copy.32.refs_10_.refs_8_
  5.8 0.3 copy.30
  6.1 0.0 copy-start.8
  6.1 0.1 pad_add_fusion.3.where
  6.2 0.1 fusion.14
  6.3 0.0 copy-start.14
  6.4 1.0 fusion.9
  7.4 1.0 concatenate.13.refs_1_
  8.4 1.0 concatenate.14.refs_5_
  9.4 0.6 pad_add_fusion.refs_11_.refs_9_
  10.0 2.5 multiply_sine_fusion
  12.5 215.9 %forward.1 = (f32[8,2048]{1,0:T(8,128)}, f32[3,8,256]{2,1,0:T(8,128)}, f32[384,2048]{1,0:T(8,128)}, bf16[1536,768]{1,0:T(8,128)(2,1)}, bf16[1536,1536]{1,0:T(8,1...) custom-call(bf16[16,128]{1,0:T(8,128)(2,1)} %copy-done.13, ...), custom_call_target="tpu_custom_call" | custom-call | tf_op jit(solution)/shard_map/forward/pallas_call | solution.py:607
  228.5 120.5 %ffn_backward.1 = (bf16[384,2048]{1,0:T(8,128)(2,1)}, bf16[384,2048]{1,0:T(8,128)(2,1)}, f32[256,2176]{1,0:T(8,128)}, bf16[256,2176]{1,0:T(8,128)(2,1)}) custom-call(bf16[384,2048]{1,0:T(8,128)(2,1)} %bitcast.27, bf16[1152,2048]{1,0:T(8,128)(2,1)} %get-tuple-element.73.refs_1_, bf16[1536,768]{1,0:T(8,128)(2,1)} %get-tuple-element.74.refs_2_.refs_16_, ...), custom_call_target="tpu_custom_call" | custom-call | tf_op jit(solution)/shard_map/ffn_backward/pallas_call | solution.py:874
  348.9 133.1 %finale.1 = (f32[384,2048]{1,0:T(8,128)}, bf16[384,2048]{1,0:T(8,128)(2,1)}, bf16[384,2048]{1,0:T(8,128)(2,1)}, bf16[384,2048]{1,0:T(8,128)(2,1)}, bf16[384,2048...) custom-call(f32[8,2048]{1,0:T(8,128)} %get-tuple-element.72.refs_0_,, ...), custom_call_target="tpu_custom_call" | custom-call | tf_op jit(solution)/shard_map/finale/pallas_call | solution.py:1228
  482.1 0.7 constant_dynamic-slice_fusion
  482.8 0.5 slice_bitcast_fusion
  483.3 1.2 copy-done.3
  484.5 1.2 copy-done.4
  485.8 1.1 copy-done.5
  486.8 1.1 copy-done.6
  487.9 1.1 copy-done.7
  489.0 3.9 place_grads.1
  492.9 1.1 copy-done.2
  494.0 1.0 copy.34
  495.0 3.0 copy.35
  498.0 7.9 %restore.1 = (bf16[384,2048]{1,0:T(8,128)(2,1)}, f32[384,2048]{1,0:T(8,128)}) custom-call(s32[8]{0:T(128)S(1)} %fusion.6.places, f32[384,2048]{1,0:T(8,128)} %get-tuple-element.71.refs_1_.middle, bf16[384,2048]{1,0:T(8,128)(2,1)S(1)} %copy-done, bf16[384,2048]{1,0:T(8,128)(2,1)S(1)} %copy-done.1, f32[384,2048]{1,0:T(8,128)} %get-tuple-element.91.grad), custom_call_target="tpu_custom_call" | custom-call | tf_op jit(solution)/shard_map/restore/pallas_call | solution.py:1348
  (43 shorter events, 0.2 us)
Async XLA Ops:
  0.6 5.2 %copy-start.9 = (bf16[2816,128]{1,0:T(8,128)(2,1)S(1)}, bf16[2816,128]{1,0:T(8,128)(2,1)}, u32[]{:S(2)}) copy-start(bf16[2816,128]{1,0:T(8,128)(2,1)} %param.27) | copy-start | bytes 2162692
  0.7 8.7 %collective-permute-start = (s32[3,128]{1,0:T(4,128)}, s32[3,128]{1,0:T(4,128)S(1)}, u32[]{:S(2)}, u32[]{:S(2)}) collective-permute-start(s32[3,128]{1,0:T(4,128)} %param.18), channel_id=1, source_target_pairs={{0,2},{2,0},{4,6},{6,4},{8,10},{10,8},{12,14},{14,12},{16,18},{18,... | collective-permute-start | bytes 4616 | tf_op jit(solution)/shard_map/ppermute | solution.py:24
  1.3 4.9 copy-start.11
  1.3 4.9 copy-start.12
  2.6 3.6 copy-start.10
  5.8 1.5 copy-start.15
  5.8 1.6 copy-start.16
  6.1 2.3 copy-start.8
  6.3 3.0 copy-start.14
  7.4 5.1 %copy-start.13 = (bf16[16,128]{1,0:T(8,128)(2,1)}, bf16[16,128]{1,0:T(8,128)(2,1)S(1)}, u32[]{:S(2)}) copy-start(bf16[16,128]{1,0:T(8,128)(2,1)S(1)} %scatter.9.refs_0_) | copy-start | bytes 12292
  483.3 1.2 copy-start.3
  484.5 1.2 copy-start.4
  485.8 1.1 copy-start.5
  486.8 1.1 copy-start.6
  487.9 1.1 copy-start.7
  492.9 1.1 copy-start.2
  494.0 4.0 copy-start.1
  495.0 3.0 copy-start

commit v7 on v6

--- a/solution.py
+++ b/solution.py
@@ -187,25 +187,30 @@
         size = 4 * self.height
         return self.dst.at[pl.ds(index * size, size), pl.ds(self.start, self.cols)]
 
-    def pass_on(self, index, first):
-        for level in range(first, len(self.far)):
+    def pass_on(self, index, levels):
+        for level in levels:
             reached = index + 2**level
             self.arrivals[reached] = self.links.push(
                 self.unit(index), self.unit(reached), peer(self.far[level])
             )
 
-    def launch(self):
+    def launch(self, nearest=True):
         for copy in self.stage:
             copy.wait_recv()
         for copy in self.local:
             copy.wait()
         self.arrivals = {}
-        self.pass_on(0, 0)
+        self.pass_on(0, range(len(self.far) - 1))
+        if nearest:
+            self.launch_nearest()
+
+    def launch_nearest(self):
+        self.pass_on(0, [len(self.far) - 1])
 
     def forward(self):
         for index in range(1, 2 ** (len(self.far) - 1)):
             self.arrivals.pop(index).wait_recv()
-            self.pass_on(index, index.bit_length())
+            self.pass_on(index, range(index.bit_length(), len(self.far)))
 
     def finish(self):
         for copy in self.arrivals.values():
@@ -511,9 +516,8 @@
                 spread.launch()
         if m == 1:
             gu[0].forward()
-    for spread in down:
-        spread.launch()
     gu[1].forward()
+    down[0].launch(nearest=False)
     tokens.third()
 
     def finish(start):
@@ -523,23 +527,35 @@
         ratio = lax.rsqrt(jnp.mean(value * value, axis=-1, keepdims=True) + epsilon)
         n2[span] = (value * ratio * gain_rows[1:2]).astype(BF)
 
-    low = []
+    tensor = lax.axis_index("tensor")
+
+    def halved(slot, m, which):
+        return n2.at[
+            pl.ds(pl.multiple_of(slot * count + m * rows + which * (rows // 2), 16), rows // 2)
+        ]
+
+    low, passed, sides = [], [], []
     for m in range(micro):
         half[m].wait_recv()
         by_rows(m * rows, rows, 32, finish)
-        low.append(
-            links.push(
-                n2.at[pl.ds(m * rows, rows)], n2.at[pl.ds(2 * count + m * rows, rows)], peer(LOW)
-            )
-        )
+        low.append(links.push(halved(0, m, tensor), halved(2, m, tensor), peer(LOW)))
+        if m == 1:
+            gu[2].forward()
     own_n2 = links.push(n2.at[pl.ds(0, count)], n2.at[pl.ds(count, count)], peer(core=True))
-    gu[2].forward()
-    gu[3].forward()
+    down[1].launch(nearest=False)
+    for m in range(micro):
+        low[m].wait_recv()
+        passed.append(links.push(halved(2, m, tensor), halved(2, m, tensor), peer(tensor=True)))
+        sides.append(links.push(halved(2, m, tensor), halved(3, m, tensor), peer(core=True)))
+        if m == 1:
+            gu[3].forward()
+            for spread in down:
+                spread.launch_nearest()
     for spread in spreads[attn_spreads:gu_spreads]:
         spread.finish()
 
-    def gates(start):
-        span = pl.ds(start, 256)
+    def gates(start, size=256):
+        span = pl.ds(start, size)
         raw = dot_plain(n2[span], gu_w[...])
         parts = silu_parts(raw[:, :main], raw[:, main : 2 * main])
         last = raw[:, 2 * main :]
@@ -555,16 +571,18 @@
 
     own_n2.wait_recv()
     by_rows(0, 2 * count, 256, gates)
-    for copy in low:
+    for m in range(micro):
+        passed[m].wait_recv()
+        sides.append(
+            links.push(halved(2, m, 1 - tensor), halved(3, m, 1 - tensor), peer(core=True))
+        )
+    outs.append(links.copy(gu_w, gu_out))
+    for copy in sides:
         copy.wait_recv()
-    both = links.push(
-        n2.at[pl.ds(2 * count, count)], n2.at[pl.ds(3 * count, count)], peer(core=True)
-    )
+    outs.append(links.copy(n2, n2_out))
+    by_rows(2 * count, count, 128, functools.partial(gates, size=128))
     down[0].forward()
-    outs.append(links.copy(gu_w, gu_out))
-    both.wait_recv()
-    outs.append(links.copy(n2, n2_out))
-    by_rows(2 * count, 2 * count, 256, gates)
+    by_rows(3 * count, count, 128, functools.partial(gates, size=128))
     down[1].forward()
     for spread in spreads[gu_spreads:]:
         spread.finish()

time: 510 us -> 503 us (0.986)
  Pallas kernels: 481 us -> 474 us
    pallas_call x1, Pallas kernels: 216 us -> 209 us  [forward(): pl.pallas_call(functools.partial(forward_kernel, far, main, micro), in_sp...]
where the time goes in v7:
time: 503 us; the launch traced here: 499 us
  Pallas kernels  474 us (94%)
  local copies, waits for them, and re-layouts  19.9 us (4%)
    pallas_call x1, Pallas kernels, forward(): pl.pallas_call(functools.partial(forward_kernel, far, main, micro), in_sp...  209 us
    pallas_call x1, Pallas kernels, finale(): pl.pallas_call(functools.partial(finale_kernel, far, micro), in_specs=any...  132 us
    pallas_call x1, Pallas kernels, ffn_backward(): pl.pallas_call(functools.partial(ffn_backward_kernel, far, main), in_spec...  121 us
    unnamed x38, local copies, waits for them, and re-layouts  12.2 us
  transfers between devices with their start and end apart: 1, of which 0 were waited for; matrix products, arithmetic and copies ran while one was open for 2% of the time, Pallas kernels for 0%

profile of v7, /device:TPU:0, one launch (start us, length us, event | category | flops | bytes accessed | tf_op | source)
XLA Modules:
  0.0 498.8 jit_solution(14425006082276750636)
XLA Ops:
  0.7 0.5 collective-permute-start
  1.2 0.1 mul.54
  1.3 0.0 copy-start.12
  1.3 1.3 gather_fusion
  2.7 1.0 fusion.11
  3.6 1.1 copy.29
  4.8 1.0 copy.32.refs_10_.refs_8_
  5.8 0.3 copy.30
  6.1 0.0 copy-start.8
  6.1 0.1 pad_add_fusion.3.where
  6.2 0.1 fusion.14
  6.3 0.0 copy-start.14
  6.4 1.0 fusion.9
  7.4 1.0 concatenate.13.refs_1_
  8.4 1.0 concatenate.14.refs_5_
  9.4 0.6 pad_add_fusion.refs_11_.refs_9_
  10.0 2.5 multiply_sine_fusion
  12.5 208.8 %forward.1 = (f32[8,2048]{1,0:T(8,128)}, f32[3,8,256]{2,1,0:T(8,128)}, f32[384,2048]{1,0:T(8,128)}, bf16[1536,768]{1,0:T(8,128)(2,1)}, bf16[1536,1536]{1,0:T(8,1...) custom-call(bf16[16,128]{1,0:T(8,128)(2,1)} %copy-done.13, ...), custom_call_target="tpu_custom_call" | custom-call | tf_op jit(solution)/shard_map/forward/pallas_call | solution.py:625
  221.3 121.2 %ffn_backward.1 = (bf16[384,2048]{1,0:T(8,128)(2,1)}, bf16[384,2048]{1,0:T(8,128)(2,1)}, f32[256,2176]{1,0:T(8,128)}, bf16[256,2176]{1,0:T(8,128)(2,1)}) custom-call(bf16[384,2048]{1,0:T(8,128)(2,1)} %bitcast.27, bf16[1152,2048]{1,0:T(8,128)(2,1)} %get-tuple-element.73.refs_1_, bf16[1536,768]{1,0:T(8,128)(2,1)} %get-tuple-element.74.refs_2_.refs_16_, ...), custom_call_target="tpu_custom_call" | custom-call | tf_op jit(solution)/shard_map/ffn_backward/pallas_call | solution.py:892
  342.5 132.3 %finale.1 = (f32[384,2048]{1,0:T(8,128)}, bf16[384,2048]{1,0:T(8,128)(2,1)}, bf16[384,2048]{1,0:T(8,128)(2,1)}, bf16[384,2048]{1,0:T(8,128)(2,1)}, bf16[384,2048...) custom-call(f32[8,2048]{1,0:T(8,128)} %get-tuple-element.72.refs_0_,, ...), custom_call_target="tpu_custom_call" | custom-call | tf_op jit(solution)/shard_map/finale/pallas_call | solution.py:1246
  474.8 0.7 constant_dynamic-slice_fusion
  475.5 0.5 slice_bitcast_fusion
  476.0 1.2 copy-done.3
  477.2 1.2 copy-done.4
  478.5 1.1 copy-done.5
  479.6 1.1 copy-done.6
  480.6 1.1 copy-done.7
  481.7 3.9 place_grads.1
  485.6 1.1 copy-done.2
  486.7 1.0 copy.34
  487.7 3.0 copy.35
  490.7 7.9 %restore.1 = (bf16[384,2048]{1,0:T(8,128)(2,1)}, f32[384,2048]{1,0:T(8,128)}) custom-call(s32[8]{0:T(128)S(1)} %fusion.6.places, f32[384,2048]{1,0:T(8,128)} %get-tuple-element.71.refs_1_.middle, bf16[384,2048]{1,0:T(8,128)(2,1)S(1)} %copy-done, bf16[384,2048]{1,0:T(8,128)(2,1)S(1)} %copy-done.1, f32[384,2048]{1,0:T(8,128)} %get-tuple-element.91.grad), custom_call_target="tpu_custom_call" | custom-call | tf_op jit(solution)/shard_map/restore/pallas_call | solution.py:1366
  (43 shorter events, 0.2 us)
Async XLA Ops:
  0.6 5.2 %copy-start.9 = (bf16[2816,128]{1,0:T(8,128)(2,1)S(1)}, bf16[2816,128]{1,0:T(8,128)(2,1)}, u32[]{:S(2)}) copy-start(bf16[2816,128]{1,0:T(8,128)(2,1)} %param.27) | copy-start | bytes 2162692
  0.7 8.7 %collective-permute-start = (s32[3,128]{1,0:T(4,128)}, s32[3,128]{1,0:T(4,128)S(1)}, u32[]{:S(2)}, u32[]{:S(2)}) collective-permute-start(s32[3,128]{1,0:T(4,128)} %param.18), channel_id=1, source_target_pairs={{0,2},{2,0},{4,6},{6,4},{8,10},{10,8},{12,14},{14,12},{16,18},{18,... | collective-permute-start | bytes 4616 | tf_op jit(solution)/shard_map/ppermute | solution.py:24
  1.3 4.9 copy-start.11
  1.3 4.9 copy-start.12
  2.6 3.6 copy-start.10
  5.8 1.5 copy-start.15
  5.8 1.6 copy-start.16
  6.1 2.3 copy-start.8
  6.3 3.0 copy-start.14
  7.4 5.1 %copy-start.13 = (bf16[16,128]{1,0:T(8,128)(2,1)}, bf16[16,128]{1,0:T(8,128)(2,1)S(1)}, u32[]{:S(2)}) copy-start(bf16[16,128]{1,0:T(8,128)(2,1)S(1)} %scatter.9.refs_0_) | copy-start | bytes 12292
  476.0 1.2 copy-start.3
  477.2 1.2 copy-start.4
  478.5 1.1 copy-start.5
  479.5 1.1 copy-start.6
  480.6 1.1 copy-start.7
  485.6 1.1 copy-start.2
  486.7 4.0 copy-start.1
  487.7 3.0 copy-start
